TPU v7x, 256 devices: a whole 4x4x8 slice. The times are simulated.
256 devices in a mesh: dp: 32 (over y_lo, z, core), rows: 8 (over y_hi, x).
Axes of the slice: x: 4, y: 4 (y_hi: 2, y_lo: 2; y = y_hi * 2 + y_lo), z: 8, core: 2. Of those that a mesh axis runs over, the one named last changes fastest.
Arguments:
- block_input: bfloat16 [64, 48, 48, 768], P('dp', 'rows'), may hold values from -40 to 40
- cotangent: bfloat16 [64, 48, 48, 768], P('dp', 'rows'), may hold values from -6 to 6
- dw_kernel: float32 [49, 768], replicated, may hold values from -0.875 to 0.875
- dw_bias: float32 [768], replicated, may hold values from -3 to 3
- ln_gain: float32 [768], replicated, may hold values from 0.5 to 1.5
- ln_bias: float32 [768], replicated, may hold values from -3 to 3
- w1: bfloat16 [768, 3072], P(None, 'dp'), may hold values from -0.21875 to 0.21875
- b1: bfloat16 [3072], P('dp'), may hold values from -3 to 3
- w2: bfloat16 [3072, 768], P('dp'), may hold values from -0.109375 to 0.109375
- b2: float32 [768], replicated, may hold values from -3 to 3
- gamma: float32 [768], replicated, may hold values from 0.3 to 1.5
Outputs:
- d_input: bfloat16 [64, 48, 48, 768], P('dp', 'rows')
- d_w1: float32 [768, 3072], P(None, 'dp')
- d_b1: float32 [3072], P('dp')
- d_w2: float32 [3072, 768], P('dp')
- param_grads: float32 [54, 768], replicated
All inputs are finite; a program needn't handle non-finite values.
Results may differ from a plain program's by a relative error of at most 0.007.
Values may be sent and summed in bfloat16 or wider, within the bound.
No kernel may reach another device: no remote copies, remote signals or barrier semaphores. Data moves between devices by JAX's collectives and lax.ppermute only.
A program may use at most 128 MiB of HBM per device.

v0:
```python
import math

import jax
import jax.numpy as jnp
import numpy as np
from jax import lax
from jax.experimental import pallas as pl
from jax.experimental.pallas import tpu as pltpu
from jax.sharding import Mesh, PartitionSpec as P

KERNEL = 7
MARGIN = 3
EPSILON = 1e-06
INV_ROOT_TWO = 0.7071067811865476
INV_ROOT_TWO_PI = 0.3989422804014327

AXES = ("y_lo", "z", "core", "y_hi", "x")
SIZES = (2, 8, 2, 2, 4)
DP = ("y_lo", "z", "core")
ROWS = ("y_hi", "x")
PAIRS = ("y_lo", "z")
Y = ("y_lo", "y_hi")


def halo(cells):
    down = [(i, i + 1) for i in range(7)]
    up = [(i + 1, i) for i in range(7)]
    above = lax.ppermute(cells[:, -MARGIN:], ROWS, down)
    below = lax.ppermute(cells[:, :MARGIN], ROWS, up)
    return jnp.concatenate([above, cells, below], axis=1)


def swap(cells):
    return lax.ppermute(cells, "core", [(0, 1), (1, 0)])


def spread_sum(part, axes):
    count = lax.axis_size(axes)
    pieces = part.reshape((count, part.shape[0] // count) + part.shape[1:])
    pieces = lax.all_to_all(pieces, axes, 0, 0)
    return jnp.sum(pieces.astype(jnp.float32), axis=0)


def gather(part, axes):
    count = lax.axis_size(axes)
    return lax.all_to_all(jnp.broadcast_to(part[None], (count,) + part.shape), axes, 0, 0)


def total(small):
    size = small.size
    flat = jnp.pad(small.reshape(-1), (0, -size % (16 * 1024))).reshape(16, -1, 128)
    part = spread_sum(flat, ("core",) + ROWS)
    part = jnp.sum(gather(part, PAIRS), axis=0)
    return gather(part, ("core",) + ROWS).reshape(-1)[:size].reshape(small.shape)


def gather_weights(w1_t, w2, b1):
    w2_h = lax.all_gather(w2, PAIRS, axis=0, tiled=True)
    mine = lax.dynamic_slice(w1_t, (lax.axis_index("x") * 24, 0), (24, w1_t.shape[1]))
    bias = jnp.pad(b1[None], ((0, 7), (0, w1_t.shape[1] - b1.shape[0])))
    pieces = gather(gather(jnp.concatenate([mine, bias], axis=0), "z"), "y_lo")
    b1_h = pieces[:, :, 24, : b1.shape[0]].reshape(-1).astype(jnp.float32)
    w1_h = gather(pieces[:, :, :24], "x").transpose(1, 2, 0, 3, 4).reshape(w2_h.shape)
    return w1_h, w2_h, b1_h


def scatter_terms(terms):
    share = lax.psum_scatter(terms, PAIRS, scatter_dimension=0, tiled=True)
    part = spread_sum(share.reshape(-1, LANES), ROWS).astype(jnp.bfloat16)
    return gather(part, ROWS).reshape(share.shape).astype(jnp.float32)


BLOCK = 256
LANES = 128
NT = (((1,), (1,)), ((), ()))
NN = (((1,), (0,)), ((), ()))
TN = (((0,), (0,)), ((), ()))
VMEM = 50 * 2**20


def mlp_kernel(normed, scaled, w1, w2, b1, terms, grad_normed, d_b1, row):
    @pl.when(pl.program_id(0) == 0)
    def _():
        grad_normed[...] = jnp.zeros_like(grad_normed)
        row[...] = jnp.zeros_like(row)

    n, s = normed[...], scaled[...]
    preact = lax.dot_general(w1[...], n, NT, preferred_element_type=jnp.float32) + b1[:, :1]
    cdf = 0.5 * (1.0 + lax.erf(preact * INV_ROOT_TWO))
    hidden = (preact * cdf).astype(jnp.bfloat16)
    slope = cdf + preact * jnp.exp(-0.5 * preact * preact) * INV_ROOT_TWO_PI
    grad_hidden = lax.dot_general(w2[...], s, NT, preferred_element_type=jnp.float32)
    grad_preact = (grad_hidden * slope).astype(jnp.bfloat16)
    total = lax.dot_general(hidden, s, NN, preferred_element_type=jnp.float32)
    terms[:, n.shape[1] :] = total.astype(jnp.bfloat16)
    row[...] += jnp.sum(total * w2[...].astype(jnp.float32), axis=0, keepdims=True)
    terms[:, : n.shape[1]] = lax.dot_general(
        grad_preact, n, NN, preferred_element_type=jnp.float32
    ).astype(jnp.bfloat16)
    d_b1[...] = jnp.broadcast_to(
        jnp.sum(grad_preact.astype(jnp.float32), axis=1, keepdims=True), d_b1.shape
    )
    grad_normed[...] += lax.dot_general(
        grad_preact, w1[...], TN, preferred_element_type=jnp.float32
    )


def mlp(normed, scaled, w1, w2, b1):
    pixels, chans = normed.shape
    hid = w1.shape[0]
    whole = pl.BlockSpec((pixels, chans), lambda i: (0, 0))
    block = pl.BlockSpec((BLOCK, chans), lambda i: (i, 0))
    both = pl.BlockSpec((BLOCK, 2 * chans), lambda i: (i, 0))
    lane = pl.BlockSpec((BLOCK, LANES), lambda i: (i, 0))
    return pl.pallas_call(
        mlp_kernel,
        grid=(hid // BLOCK,),
        in_specs=[whole, whole, block, block, lane],
        out_specs=[both, whole, lane, pl.BlockSpec((1, chans), lambda i: (0, 0))],
        out_shape=[
            jax.ShapeDtypeStruct((hid, 2 * chans), jnp.bfloat16),
            jax.ShapeDtypeStruct((pixels, chans), jnp.float32),
            jax.ShapeDtypeStruct((hid, LANES), jnp.float32),
            jax.ShapeDtypeStruct((1, chans), jnp.float32),
        ],
        compiler_params=pltpu.CompilerParams(vmem_limit_bytes=VMEM),
        cost_estimate=pl.CostEstimate(
            flops=10 * pixels * hid * chans, bytes_accessed=2**24, transcendentals=2 * pixels * hid
        ),
    )(normed, scaled, w1, w2, jnp.broadcast_to(b1[:, None], (hid, LANES)))


def transposed_kernel(padded, cotangent, kernel, d_input, wide):
    rows, cols = d_input.shape[1:3]
    wide[...] = padded[0].astype(jnp.float32)
    for at in range(0, cols, 24):
        sums = [cotangent[0, r, at : at + 24].astype(jnp.float32) for r in range(rows)]
        for b in range(KERNEL):
            column = [(KERNEL - 1 - a) * KERNEL + KERNEL - 1 - b for a in range(KERNEL)]
            taps = [kernel[t : t + 1] for t in column]
            for r in range(rows + KERNEL - 1):
                cells = wide[r, at + b : at + b + 24]
                for a in range(max(0, r - rows + 1), min(KERNEL, r + 1)):
                    sums[r - a] = sums[r - a] + cells * taps[a]
        for r in range(rows):
            d_input[0, r, at : at + 24] = sums[r].astype(jnp.bfloat16)


def transposed(padded, cotangent, kernel):
    images, high, wide, chans = padded.shape
    rows, cols = cotangent.shape[1:3]
    maps = pl.BlockSpec((1, rows, cols, LANES), lambda c, i: (i, 0, 0, c))
    return pl.pallas_call(
        transposed_kernel,
        grid=(chans // LANES, images),
        in_specs=[
            pl.BlockSpec((1, high, wide, LANES), lambda c, i: (i, 0, 0, c)),
            maps,
            pl.BlockSpec((KERNEL * KERNEL, LANES), lambda c, i: (0, c)),
        ],
        out_specs=maps,
        out_shape=jax.ShapeDtypeStruct(cotangent.shape, jnp.bfloat16),
        scratch_shapes=[pltpu.VMEM((high, wide, LANES), jnp.float32)],
        compiler_params=pltpu.CompilerParams(vmem_limit_bytes=VMEM),
        cost_estimate=pl.CostEstimate(
            flops=10**10, bytes_accessed=2**22, transcendentals=0
        ),
    )(padded, cotangent, kernel)


def taps_kernel(padded, grad, sums, wide, grad_wide):
    rows, cols = grad.shape[1:3]
    wide[...] = padded[0].astype(jnp.float32)
    grad_wide[...] = grad[0].astype(jnp.float32)

    @pl.when(pl.program_id(1) == 0)
    def _():
        sums[...] = jnp.zeros_like(sums)

    for b in range(KERNEL):
        totals = [jnp.zeros((8, LANES), jnp.float32) for _ in range(KERNEL)]
        for at in range(0, cols, 16):
            own = [grad_wide[r, at : at + 16] for r in range(rows)]
            for r in range(rows + KERNEL - 1):
                cells = wide[r, at + b : at + b + 16]
                for a in range(max(0, r - rows + 1), min(KERNEL, r + 1)):
                    product = cells * own[r - a]
                    totals[a] = totals[a] + (product[:8] + product[8:])
        for a in range(KERNEL):
            t = a * KERNEL + b
            sums[t : t + 1] += jnp.sum(totals[a], axis=0, keepdims=True)


def tap_sums(padded, grad):
    images, high, wide, chans = padded.shape
    rows, cols = grad.shape[1:3]
    return pl.pallas_call(
        taps_kernel,
        grid=(chans // LANES, images),
        in_specs=[
            pl.BlockSpec((1, high, wide, LANES), lambda c, i: (i, 0, 0, c)),
            pl.BlockSpec((1, rows, cols, LANES), lambda c, i: (i, 0, 0, c)),
        ],
        out_specs=pl.BlockSpec((KERNEL * KERNEL, LANES), lambda c, i: (0, c)),
        out_shape=jax.ShapeDtypeStruct((KERNEL * KERNEL, chans), jnp.float32),
        scratch_shapes=[
            pltpu.VMEM((high, wide, LANES), jnp.float32),
            pltpu.VMEM((rows, cols, LANES), jnp.float32),
        ],
        compiler_params=pltpu.CompilerParams(vmem_limit_bytes=VMEM),
        cost_estimate=pl.CostEstimate(
            flops=10**10, bytes_accessed=2**22, transcendentals=0
        ),
    )(padded, grad)


def pad_columns(cells):
    return jnp.pad(cells, ((0, 0), (0, 0), (MARGIN, 8 - MARGIN), (0, 0)))


def depthwise(padded, kernel, height, width):
    total = jnp.zeros(padded.shape[:-3] + (height, width, padded.shape[-1]), jnp.float32)
    for row_tap in range(KERNEL):
        for col_tap in range(KERNEL):
            window = padded[:, row_tap : row_tap + height, col_tap : col_tap + width]
            total = total + window.astype(jnp.float32) * kernel[row_tap * KERNEL + col_tap]
    return total


def shards(block_input, cotangent, dw_kernel, dw_bias, ln_gain, ln_bias, w1, b1, w2, b2, gamma):
    images, rows_here, cols, chans = block_input.shape
    shard = w1.shape[1]
    pixels = images * rows_here * cols
    flat_cot = cotangent.reshape(pixels, chans).astype(jnp.float32)
    scaled = (flat_cot * gamma).astype(jnp.bfloat16)
    w1_t, w2_h, b1_h = gather_weights(w1.T, w2, b1)

    padded = pad_columns(halo(block_input))
    scaled2 = jnp.concatenate([scaled, swap(scaled)], axis=0)
    conv = depthwise(padded, dw_kernel, rows_here, cols) + dw_bias
    center = conv - jnp.mean(conv, axis=-1, keepdims=True)
    spread = jnp.mean(center * center, axis=-1, keepdims=True)
    rstd = lax.rsqrt(spread + EPSILON).reshape(pixels, 1)
    norm = center.reshape(pixels, chans) * rstd
    normed = (norm * ln_gain + ln_bias).astype(jnp.bfloat16)
    normed2 = jnp.concatenate([normed, swap(normed)], axis=0)

    terms, grad_normed2, sums_b1, moment_row = mlp(normed2, scaled2, w1_t, w2_h, b1_h)
    grad_normed = grad_normed2[:pixels] + swap(grad_normed2[pixels:].astype(jnp.bfloat16)).astype(
        jnp.float32
    )
    share = scatter_terms(terms)

    weighted = grad_normed * ln_gain
    grad_conv = (
        rstd
        * (
            weighted
            - jnp.mean(weighted, axis=-1, keepdims=True)
            - norm * jnp.mean(weighted * norm, axis=-1, keepdims=True)
        )
    ).astype(jnp.bfloat16)
    grad_maps = grad_conv.reshape(block_input.shape)
    grad_padded = pad_columns(halo(grad_maps))
    d_input = transposed(grad_padded, cotangent, dw_kernel)

    grad_wide = grad_maps.astype(jnp.float32)
    cot_sums = jnp.sum(flat_cot, axis=0)
    core = lax.axis_index("core")
    sums_b1 = sums_b1[:, 0][None]
    pair_b1 = jnp.where(core == jnp.arange(2)[:, None], sums_b1, 0.0)
    local_small = jnp.concatenate(
        [
            tap_sums(padded, grad_maps),
            jnp.sum(grad_wide, axis=(0, 1, 2))[None],
            jnp.sum(grad_normed * norm, axis=0)[None],
            jnp.sum(grad_normed, axis=0)[None],
            (gamma * cot_sums)[None],
            moment_row / gamma + b2 * cot_sums,
            pair_b1.reshape(-1, chans),
        ],
        axis=0,
    )
    total_small = total(local_small)
    factor = 1.0 / math.sqrt(pixels * 256)
    param_grads = total_small[:54] * factor
    at = (lax.axis_index("y_lo") * 8 + lax.axis_index("z")) * shard
    sums = total_small[54:].reshape(2, -1)
    d_b1 = lax.dynamic_slice(sums, (core, at), (1, shard)).reshape(shard) * factor
    share = share * factor
    d_w1, d_w2 = share[:, :chans].T, share[:, chans:]
    return (d_input.reshape(block_input.shape), d_w1, d_b1, d_w2, param_grads)


def solution(mesh):
    fine = Mesh(mesh.devices.reshape(SIZES), AXES)
    placed = (
        P(DP, ROWS, None, None),
        P(DP, ROWS, None, None),
        P(),
        P(),
        P(),
        P(),
        P(None, DP),
        P(DP),
        P(DP, None),
        P(),
        P(),
    )
    return jax.shard_map(
        shards,
        mesh=fine,
        in_specs=placed,
        out_specs=(P(DP, ROWS, None, None), P(None, DP), P(DP), P(DP, None), P()),
        check_vma=False,
    )
```

profile of v0, /device:TPU:2, one launch (start us, length us, event | category | flops | bytes accessed | tf_op | source)
XLA Modules:
  0.0 259.2 jit_solution(5516697989420093287)
XLA Ops:
  9.3 4.3 %collective-permute-start.1 = (bf16[2,3,48,768]{3,2,1,0:T(8,128)(2,1)S(1)}, bf16[2,3,48,768]{3,2,1,0:T(8,128)(2,1)S(1)}, u32[]{:S(2)}, u32[]{:S(2)}) collective-permute-start(bf16[2,3,48,768]{3,2,1,0:T(8,128)(2,1)S(1)} %get-tuple-element.79), channel_id=1, source_target_pairs={{1,0},{2,1},{3,2},{4,3},{5,4},{6,5},{7,6},{9,8},{10,9},{11,10},{12... | collective-permute-start | bytes 1327112 | tf_op jit(solution)/shard_map/ppermute | solution.py:29
  17.4 8.2 %all-to-all-start = ((bf16[8,32,768]{2,1,0:T(8,128)(2,1)}), bf16[8,32,768]{2,1,0:T(8,128)(2,1)}, u32[]{:S(2)}, u32[]{:S(2)}) async-start(bf16[8,32,768]{2,1,0:T(8,128)(2,1)} %broadcast_in_dim.57), calls=%async_computation | async-start | bytes 786432 | tf_op jit(solution)/shard_map/all_to_all | solution.py:46
  32.8 8.3 %all-to-all-done = bf16[8,32,768]{2,1,0:T(8,128)(2,1)} async-done(((bf16[8,32,768]{2,1,0:T(8,128)(2,1)}), bf16[8,32,768]{2,1,0:T(8,128)(2,1)}, u32[]{:S(2)}, u32[]{:S(2)}) %all-to-all-start) | async-done | bytes 393248 | tf_op jit(solution)/shard_map/all_to_all | solution.py:46
  43.1 4.3 %all-to-all-start.1 = ((bf16[2,8,32,768]{3,2,1,0:T(8,128)(2,1)}), bf16[2,8,32,768]{3,2,1,0:T(8,128)(2,1)}, u32[]{:S(2)}, u32[]{:S(2)}) async-start(bf16[2,8,32,768]{3,2,1,0:T(8,128)(2,1)} %broadcast_in_dim.58), calls=%async_computation.1 | async-start | bytes 1572864 | tf_op jit(solution)/shard_map/all_to_all | solution.py:46
  47.5 15.5 %fusion.11 = (f32[2,6,48]{2,1,0:T(8,128)S(1)}, f32[2,6,48,768]{3,2,1,0:T(8,128)}) fusion(f32[768]{0:T(1024)S(1)} %copy-done.32, f32[768]{0:T(1024)S(1)} %get-tuple-element.65, bf16[2,12,56,768]{3,2,1,0:T(8,128)(2,1)S(1)} %fusion.5.padded, f32[768]{0:T(1024)S(1)} %get-tuple-element.18, f32[768]{0:T(1024)S(1)} %get-tuple-element.19, f32[768]{0:T(1024)S(1)} %copy-done.16, ...), kind=kLoop, calls=%fused_computation.99 | loop fusion | flops 65469888 | bytes 45277440 | tf_op jit(solution)/shard_map/reduce_sum | solution.py:241
  63.0 3.4 %all-to-all-done.1 = bf16[2,8,32,768]{3,2,1,0:T(8,128)(2,1)} async-done(((bf16[2,8,32,768]{3,2,1,0:T(8,128)(2,1)}), bf16[2,8,32,768]{3,2,1,0:T(8,128)(2,1)}, u32[]{:S(2)}, u32[]{:S(2)}) %all-to-all-start.1) | async-done | bytes 786464 | tf_op jit(solution)/shard_map/all_to_all | solution.py:46
  69.2 7.9 %all-to-all-start.2 = ((bf16[4,2,8,24,768]{4,3,2,1,0:T(8,128)(2,1)}), bf16[4,2,8,24,768]{4,3,2,1,0:T(8,128)(2,1)}, u32[]{:S(2)}, u32[]{:S(2)}) async-start(bf16[4,2,8,24,768]{4,3,2,1,0:T(8,128)(2,1)} %broadcast_in_dim.104), calls=%async_computation.2 | async-start | bytes 4718592 | tf_op jit(solution)/shard_map/all_to_all | solution.py:46
  80.1 3.3 %add_convert_fusion = (bf16[576,768]{1,0:T(8,128)(2,1)}, f32[576,768]{1,0:T(8,128)}) fusion(f32[768]{0:T(1024)S(1)} %copy-done.33, f32[768]{0:T(1024)S(1)} %copy-done.14, f32[576]{0:T(1024)S(1)} %rsqrt.13, f32[2,6,48,768]{3,2,1,0:T(8,128)} %get-tuple-element.71), kind=kLoop, calls=%fused_computation.21 | loop fusion | flops 1769472 | bytes 4432128 | tf_op jit(solution)/shard_map/convert_element_type | solution.py:245
  89.9 14.0 %all-to-all-done.2 = bf16[4,2,8,24,768]{4,3,2,1,0:T(8,128)(2,1)} async-done(((bf16[4,2,8,24,768]{4,3,2,1,0:T(8,128)(2,1)}), bf16[4,2,8,24,768]{4,3,2,1,0:T(8,128)(2,1)}, u32[]{:S(2)}, u32[]{:S(2)}) %all-to-all-start.2) | async-done | bytes 2359328 | tf_op jit(solution)/shard_map/all_to_all | solution.py:46
  103.9 3.3 %copy.17 = bf16[2,8,4,24,768]{4,3,2,1,0:T(8,128)(2,1)} copy(bf16[2,8,4,24,768]{4,3,1,0,2:T(8,128)(2,1)} %bitcast.4) | data formatting | bytes 4718592 | tf_op jit(solution)/shard_map/transpose | solution.py:63
  108.9 20.8 %shard_map.146 = (bf16[1536,1536]{1,0:T(8,128)(2,1)}, f32[1152,768]{1,0:T(8,128)}, f32[1536,128]{1,0:T(8,128)S(1)}, f32[1,768]{1,0:T(1,128)S(1)}) custom-call(bf16[1152,768]{1,0:T(8,128)(2,1)S(1)} %copy-done.4, bf16[1152,768]{1,0:T(8,128)(2,1)} %pad_maximum_fusion.1.scaled, bf16[1536,768]{1,0:T(8,128)(2,1)} %bitcast.25, ...), custom_call_target="tpu_custom_call" | custom-call | flops 13589544960 | bytes 16777216 | tf_op jit(solution)/shard_map/pallas_call | solution.py:115
  136.2 3.1 %multiply_reduce_fusion = (f32[768]{0:T(1024)S(1)}, f32[576]{0:T(1024)S(1)}, f32[576]{0:T(1024)S(1)}, f32[768]{0:T(1024)S(1)}) fusion(f32[576,768]{1,0:T(8,128)} %get-tuple-element.69, bf16[576,768]{1,0:T(8,128)(2,1)} %collective-permute-done.4, f32[1152,768]{1,0:T(8,128)} %get-tuple-element.9, f32[768]{0:T(1024)S(1)} %copy-done.14), kind=kLoop, calls=%fused_computation.16 | loop fusion | flops 3978624 | bytes 4437504 | tf_op jit(solution)/shard_map/reduce_sum | solution.py:276
  141.6 7.5 %shard_map.148 = f32[49,768]{1,0:T(8,128)S(1)} custom-call(bf16[2,12,56,768]{3,2,1,0:T(8,128)(2,1)S(1)} %fusion.5.padded, bf16[2,6,48,768]{3,2,1,0:T(8,128)(2,1)S(1)} %bitcast.22), custom_call_target="tpu_custom_call" | custom-call | flops 10000000000 | bytes 4194304 | tf_op jit(solution)/shard_map/pallas_call | solution.py:197
  150.0 5.1 %all-to-all-start.5 = ((f32[16,1,24,128]{3,2,1,0:T(8,128)}), f32[16,1,24,128]{3,2,1,0:T(8,128)S(1)}, u32[]{:S(2)}, u32[]{:S(2)}) async-start(f32[16,1,24,128]{3,2,1,0:T(8,128)} %bitcast.8), calls=%async_computation.6 | async-start | bytes 393216 | tf_op jit(solution)/shard_map/all_to_all | solution.py:40
  157.2 3.8 %collective-permute-start.5 = (bf16[2,3,48,768]{3,2,1,0:T(8,128)(2,1)S(1)}, bf16[2,3,48,768]{3,2,1,0:T(8,128)(2,1)}, u32[]{:S(2)}, u32[]{:S(2)}) collective-permute-start(bf16[2,3,48,768]{3,2,1,0:T(8,128)(2,1)S(1)} %get-tuple-element.74), channel_id=1, source_target_pairs={{0,1},{1,2},{2,3},{3,4},{4,5},{5,6},{6,7},{8,9},{9,10},{10,11},{11... | collective-permute-start | bytes 1327112 | tf_op jit(solution)/shard_map/ppermute | solution.py:28
  161.1 5.0 %all-to-all-done.5 = f32[16,1,24,128]{3,2,1,0:T(8,128)S(1)} async-done(((f32[16,1,24,128]{3,2,1,0:T(8,128)}), f32[16,1,24,128]{3,2,1,0:T(8,128)S(1)}, u32[]{:S(2)}, u32[]{:S(2)}) %all-to-all-start.5) | async-done | bytes 196640 | tf_op jit(solution)/shard_map/all_to_all | solution.py:40
  166.8 3.7 %all-to-all-start.6 = ((f32[16,1,24,128]{3,2,1,0:T(8,128)}), f32[16,1,24,128]{3,2,1,0:T(8,128)S(1)}, u32[]{:S(2)}, u32[]{:S(2)}) async-start(f32[16,1,24,128]{3,2,1,0:T(8,128)} %broadcast_in_dim.120), calls=%async_computation.7 | async-start | bytes 393216 | tf_op jit(solution)/shard_map/all_to_all | solution.py:46
  170.4 12.0 %all-to-all-done.6 = f32[16,1,24,128]{3,2,1,0:T(8,128)S(1)} async-done(((f32[16,1,24,128]{3,2,1,0:T(8,128)}), f32[16,1,24,128]{3,2,1,0:T(8,128)S(1)}, u32[]{:S(2)}, u32[]{:S(2)}) %all-to-all-start.6) | async-done | bytes 196640 | tf_op jit(solution)/shard_map/all_to_all | solution.py:46
  183.1 23.3 %all-to-all-start.7 = ((f32[16,1,24,128]{3,2,1,0:T(8,128)}), f32[16,1,24,128]{3,2,1,0:T(8,128)S(1)}, u32[]{:S(2)}, u32[]{:S(2)}) async-start(f32[16,1,24,128]{3,2,1,0:T(8,128)} %broadcast_in_dim.121), calls=%async_computation.8 | async-start | bytes 393216 | tf_op jit(solution)/shard_map/all_to_all | solution.py:46
  206.5 3.5 %select_maximum_fusion.padded = bf16[2,12,56,768]{3,2,1,0:T(8,128)(2,1)} fusion(bf16[2,3,48,768]{3,2,1,0:T(8,128)(2,1)} %collective-permute-done.6, bf16[2,6,48,768]{3,2,1,0:T(8,128)(2,1)S(1)} %bitcast.24, bf16[2,3,48,768]{3,2,1,0:T(8,128)(2,1)} %collective-permute-done.5), kind=kLoop, calls=%fused_computation.3 | loop fusion | flops 12386304 | bytes 3833856 | tf_op jit(solution)/shard_map/concatenate | solution.py:30
  213.8 12.4 %all-to-all-start.3 = ((bf16[8,144,128]{2,1,0:T(8,128)(2,1)}), bf16[8,144,128]{2,1,0:T(8,128)(2,1)S(1)}, u32[]{:S(2)}, u32[]{:S(2)}) async-start(bf16[8,144,128]{2,1,0:T(8,128)(2,1)} %reshape_reshape.6), calls=%async_computation.4 | async-start | bytes 589824 | tf_op jit(solution)/shard_map/all_to_all | solution.py:40
  227.8 7.7 %shard_map.147 = bf16[2,6,48,768]{3,2,1,0:T(8,128)(2,1)} custom-call(bf16[2,12,56,768]{3,2,1,0:T(8,128)(2,1)S(1)} %copy-done.3, bf16[2,6,48,768]{3,2,1,0:T(8,128)(2,1)S(1)} %copy-done.2, f32[49,768]{1,0:T(8,128)S(1)} %copy-done.7), custom_call_target="tpu_custom_call" | custom-call | flops 10000000000 | bytes 4194304 | tf_op jit(solution)/shard_map/pallas_call | solution.py:153
  236.3 7.2 %all-to-all-start.4 = ((bf16[8,144,128]{2,1,0:T(8,128)(2,1)}), bf16[8,144,128]{2,1,0:T(8,128)(2,1)S(1)}, u32[]{:S(2)}, u32[]{:S(2)}) async-start(bf16[8,144,128]{2,1,0:T(8,128)(2,1)} %broadcast_in_dim.106), calls=%async_computation.5 | async-start | bytes 589824 | tf_op jit(solution)/shard_map/all_to_all | solution.py:46
  244.8 6.5 %all-to-all-done.4 = bf16[8,144,128]{2,1,0:T(8,128)(2,1)S(1)} async-done(((bf16[8,144,128]{2,1,0:T(8,128)(2,1)}), bf16[8,144,128]{2,1,0:T(8,128)(2,1)S(1)}, u32[]{:S(2)}, u32[]{:S(2)}) %all-to-all-start.4) | async-done | bytes 294944 | tf_op jit(solution)/shard_map/all_to_all | solution.py:46
  (153 shorter events, 50.4 us)
Async XLA Ops:
  9.3 17.1 %copy-start.7 = (f32[49,768]{1,0:T(8,128)S(1)}, f32[49,768]{1,0:T(8,128)}, u32[]{:S(2)}) copy-start(f32[49,768]{1,0:T(8,128)} %kernel.1) | copy-start | bytes 451588
  9.3 19.3 %collective-permute-start.1 = (bf16[2,3,48,768]{3,2,1,0:T(8,128)(2,1)S(1)}, bf16[2,3,48,768]{3,2,1,0:T(8,128)(2,1)S(1)}, u32[]{:S(2)}, u32[]{:S(2)}) collective-permute-start(bf16[2,3,48,768]{3,2,1,0:T(8,128)(2,1)S(1)} %get-tuple-element.79), channel_id=1, source_target_pairs={{1,0},{2,1},{3,2},{4,3},{5,4},{6,5},{7,6},{9,8},{10,9},{11,10},{12... | collective-permute-start | bytes 1327112 | tf_op jit(solution)/shard_map/ppermute | solution.py:29
  13.6 13.8 %collective-permute-start = (bf16[2,3,48,768]{3,2,1,0:T(8,128)(2,1)}, bf16[2,3,48,768]{3,2,1,0:T(8,128)(2,1)S(1)}, u32[]{:S(2)}, u32[]{:S(2)}) collective-permute-start(bf16[2,3,48,768]{3,2,1,0:T(8,128)(2,1)} %get-tuple-element.78), channel_id=1, source_target_pairs={{0,1},{1,2},{2,3},{3,4},{4,5},{5,6},{6,7},{8,9},{9,10},{10,11},{11... | collective-permute-start | bytes 1327112 | tf_op jit(solution)/shard_map/ppermute | solution.py:28
  16.6 66.8 %collective-permute-start.3 = (bf16[576,768]{1,0:T(8,128)(2,1)}, bf16[576,768]{1,0:T(8,128)(2,1)}, u32[]{:S(2)}, u32[]{:S(2)}) collective-permute-start(bf16[576,768]{1,0:T(8,128)(2,1)} %fusion.6), channel_id=1, source_target_pairs={{0,8},{8,0},{1,9},{9,1},{2,10},{10,2},{3,11},{11,3},{4,12},{12,4},... | collective-permute-start | bytes 2654216 | tf_op jit(solution)/shard_map/ppermute | solution.py:34
  17.4 23.7 %all-to-all-start = ((bf16[8,32,768]{2,1,0:T(8,128)(2,1)}), bf16[8,32,768]{2,1,0:T(8,128)(2,1)}, u32[]{:S(2)}, u32[]{:S(2)}) async-start(bf16[8,32,768]{2,1,0:T(8,128)(2,1)} %broadcast_in_dim.57), calls=%async_computation | async-start | bytes 786432 | tf_op jit(solution)/shard_map/all_to_all | solution.py:46
  25.6 81.5 %all-gather.2.cloned.1.call-start = ((), (), s32[]{:S(2)}) async-start(), calls=%async_computation.9 | async-start | bytes 2506752 | tf_op jit(solution)/shard_map/all_gather | solution.py:58
  32.6 14.8 %copy-start.16 = (f32[768]{0:T(1024)S(1)}, f32[768]{0:T(1024)}, u32[]{:S(2)}) copy-start(f32[768]{0:T(1024)} %get-tuple-element.20) | copy-start | bytes 9220
  32.6 14.8 %copy-start.17 = (f32[768]{0:T(1024)S(1)}, f32[768]{0:T(1024)}, u32[]{:S(2)}) copy-start(f32[768]{0:T(1024)} %get-tuple-element.21) | copy-start | bytes 9220
  32.6 14.8 %copy-start.18 = (f32[768]{0:T(1024)S(1)}, f32[768]{0:T(1024)}, u32[]{:S(2)}) copy-start(f32[768]{0:T(1024)} %get-tuple-element.22) | copy-start | bytes 9220
  32.6 14.8 %copy-start.19 = (f32[768]{0:T(1024)S(1)}, f32[768]{0:T(1024)}, u32[]{:S(2)}) copy-start(f32[768]{0:T(1024)} %get-tuple-element.23) | copy-start | bytes 9220
  32.6 14.8 %copy-start.20 = (f32[768]{0:T(1024)S(1)}, f32[768]{0:T(1024)}, u32[]{:S(2)}) copy-start(f32[768]{0:T(1024)} %get-tuple-element.24) | copy-start | bytes 9220
  43.1 23.4 %all-to-all-start.1 = ((bf16[2,8,32,768]{3,2,1,0:T(8,128)(2,1)}), bf16[2,8,32,768]{3,2,1,0:T(8,128)(2,1)}, u32[]{:S(2)}, u32[]{:S(2)}) async-start(bf16[2,8,32,768]{3,2,1,0:T(8,128)(2,1)} %broadcast_in_dim.58), calls=%async_computation.1 | async-start | bytes 1572864 | tf_op jit(solution)/shard_map/all_to_all | solution.py:46
  69.2 34.7 %all-to-all-start.2 = ((bf16[4,2,8,24,768]{4,3,2,1,0:T(8,128)(2,1)}), bf16[4,2,8,24,768]{4,3,2,1,0:T(8,128)(2,1)}, u32[]{:S(2)}, u32[]{:S(2)}) async-start(bf16[4,2,8,24,768]{4,3,2,1,0:T(8,128)(2,1)} %broadcast_in_dim.104), calls=%async_computation.2 | async-start | bytes 4718592 | tf_op jit(solution)/shard_map/all_to_all | solution.py:46
  77.0 134.7 %reduce-scatter.2.cloned.1.call-start = ((), (), s32[]{:S(2)}) async-start(), calls=%async_computation.10 | async-start | bytes 5013504 | tf_op jit(solution)/shard_map/reduce_scatter | solution.py:68
  83.4 3.7 %collective-permute-start.2 = (bf16[576,768]{1,0:T(8,128)(2,1)}, bf16[576,768]{1,0:T(8,128)(2,1)}, u32[]{:S(2)}, u32[]{:S(2)}) collective-permute-start(bf16[576,768]{1,0:T(8,128)(2,1)} %get-tuple-element.68), channel_id=1, source_target_pairs={{0,8},{8,0},{1,9},{9,1},{2,10},{10,2},{3,11},{11,3},{4,12},{12,4},... | collective-permute-start | bytes 2654216 | tf_op jit(solution)/shard_map/ppermute | solution.py:34
  133.4 2.8 %collective-permute-start.4 = (bf16[576,768]{1,0:T(8,128)(2,1)}, bf16[576,768]{1,0:T(8,128)(2,1)}, u32[]{:S(2)}, u32[]{:S(2)}) collective-permute-start(bf16[576,768]{1,0:T(8,128)(2,1)} %slice.642), channel_id=1, source_target_pairs={{0,8},{8,0},{1,9},{9,1},{2,10},{10,2},{3,11},{11,3},{4,12},{12,4},... | collective-permute-start | bytes 2654216 | tf_op jit(solution)/shard_map/ppermute | solution.py:34
  150.0 16.0 %all-to-all-start.5 = ((f32[16,1,24,128]{3,2,1,0:T(8,128)}), f32[16,1,24,128]{3,2,1,0:T(8,128)S(1)}, u32[]{:S(2)}, u32[]{:S(2)}) async-start(f32[16,1,24,128]{3,2,1,0:T(8,128)} %bitcast.8), calls=%async_computation.6 | async-start | bytes 393216 | tf_op jit(solution)/shard_map/all_to_all | solution.py:40
  155.2 51.2 %collective-permute-start.6 = (bf16[2,3,48,768]{3,2,1,0:T(8,128)(2,1)S(1)}, bf16[2,3,48,768]{3,2,1,0:T(8,128)(2,1)}, u32[]{:S(2)}, u32[]{:S(2)}) collective-permute-start(bf16[2,3,48,768]{3,2,1,0:T(8,128)(2,1)S(1)} %get-tuple-element.75), channel_id=1, source_target_pairs={{1,0},{2,1},{3,2},{4,3},{5,4},{6,5},{7,6},{9,8},{10,9},{11,10},{12... | collective-permute-start | bytes 1327112 | tf_op jit(solution)/shard_map/ppermute | solution.py:29
  157.2 49.2 %collective-permute-start.5 = (bf16[2,3,48,768]{3,2,1,0:T(8,128)(2,1)S(1)}, bf16[2,3,48,768]{3,2,1,0:T(8,128)(2,1)}, u32[]{:S(2)}, u32[]{:S(2)}) collective-permute-start(bf16[2,3,48,768]{3,2,1,0:T(8,128)(2,1)S(1)} %get-tuple-element.74), channel_id=1, source_target_pairs={{0,1},{1,2},{2,3},{3,4},{4,5},{5,6},{6,7},{8,9},{9,10},{10,11},{11... | collective-permute-start | bytes 1327112 | tf_op jit(solution)/shard_map/ppermute | solution.py:28
  166.8 15.6 %all-to-all-start.6 = ((f32[16,1,24,128]{3,2,1,0:T(8,128)}), f32[16,1,24,128]{3,2,1,0:T(8,128)S(1)}, u32[]{:S(2)}, u32[]{:S(2)}) async-start(f32[16,1,24,128]{3,2,1,0:T(8,128)} %broadcast_in_dim.120), calls=%async_computation.7 | async-start | bytes 393216 | tf_op jit(solution)/shard_map/all_to_all | solution.py:46
  183.1 30.7 %all-to-all-start.7 = ((f32[16,1,24,128]{3,2,1,0:T(8,128)}), f32[16,1,24,128]{3,2,1,0:T(8,128)S(1)}, u32[]{:S(2)}, u32[]{:S(2)}) async-start(f32[16,1,24,128]{3,2,1,0:T(8,128)} %broadcast_in_dim.121), calls=%async_computation.8 | async-start | bytes 393216 | tf_op jit(solution)/shard_map/all_to_all | solution.py:46
  206.5 19.7 %copy-start.2 = (bf16[2,6,48,768]{3,2,1,0:T(8,128)(2,1)S(1)}, bf16[2,6,48,768]{3,2,1,0:T(8,128)(2,1)}, u32[]{:S(2)}) copy-start(bf16[2,6,48,768]{3,2,1,0:T(8,128)(2,1)} %cotangent.1) | copy-start | bytes 2654212
  213.8 21.7 %all-to-all-start.3 = ((bf16[8,144,128]{2,1,0:T(8,128)(2,1)}), bf16[8,144,128]{2,1,0:T(8,128)(2,1)S(1)}, u32[]{:S(2)}, u32[]{:S(2)}) async-start(bf16[8,144,128]{2,1,0:T(8,128)(2,1)} %reshape_reshape.6), calls=%async_computation.4 | async-start | bytes 589824 | tf_op jit(solution)/shard_map/all_to_all | solution.py:40
  236.3 15.0 %all-to-all-start.4 = ((bf16[8,144,128]{2,1,0:T(8,128)(2,1)}), bf16[8,144,128]{2,1,0:T(8,128)(2,1)S(1)}, u32[]{:S(2)}, u32[]{:S(2)}) async-start(bf16[8,144,128]{2,1,0:T(8,128)(2,1)} %broadcast_in_dim.106), calls=%async_computation.5 | async-start | bytes 589824 | tf_op jit(solution)/shard_map/all_to_all | solution.py:46
  (29 other events, 248.8 us)
Sparse Core Ops, SparseCore 0:
  28.3 76.1 all-gather.1
  130.8 80.9 reduce-scatter.1
where the time goes:
time: 261 us; the launch traced here: 259 us
  starting transfers between devices  84.3 us (32%)
  waiting for transfers between devices  53.8 us (21%)
  other arithmetic  41.8 us (16%)
  Pallas kernels  36 us (14%)
  local copies, waits for them, and re-layouts  28.6 us (11%)
  between operations  14.7 us (6%)
    all_to_all x6, starting transfers between devices, gather(): lax.all_to_all(jnp.broadcast_to(part[None], (count,) + part.shape), axes,...  54.6 us
    all_to_all x6, waiting for transfers between devices, gather(): lax.all_to_all(jnp.broadcast_to(part[None], (count,) + part.shape), axes,...  44.2 us
    pallas_call x1, Pallas kernels, mlp(): pl.pallas_call(mlp_kernel, grid=(hid // BLOCK,), in_specs=[whole, whole,...  20.8 us
    all_to_all x2, starting transfers between devices, spread_sum(): pieces = lax.all_to_all(pieces, axes, 0, 0)  17.5 us
    reduce_sum x1, other arithmetic, shards(): center = conv - jnp.mean(conv, axis=-1, keepdims=True)  15.5 us
    pallas_call x1, Pallas kernels, transposed(): pl.pallas_call(transposed_kernel, grid=(chans // LANES, images), in_specs...  7.67 us
    pallas_call x1, Pallas kernels, tap_sums(): pl.pallas_call(taps_kernel, grid=(chans // LANES, images), in_specs=[pl.B...  7.5 us
    broadcast_in_dim x6, local copies, waits for them, and re-layouts, gather(): jnp.broadcast_to(part[None], (count,) + part.shape)  6.49 us
  transfers between devices with their start and end apart: 17, of which 8 were waited for; matrix products, arithmetic and copies ran while one was open for 24% of the time, Pallas kernels for 6%

commit v1 on v0

--- a/solution.py
+++ b/solution.py
@@ -46,88 +46,169 @@
     return lax.all_to_all(jnp.broadcast_to(part[None], (count,) + part.shape), axes, 0, 0)
 
 
-def total(small):
-    size = small.size
-    flat = jnp.pad(small.reshape(-1), (0, -size % (16 * 1024))).reshape(16, -1, 128)
-    part = spread_sum(flat, ("core",) + ROWS)
-    part = jnp.sum(gather(part, PAIRS), axis=0)
-    return gather(part, ("core",) + ROWS).reshape(-1)[:size].reshape(small.shape)
-
-
-def gather_weights(w1_t, w2, b1):
-    w2_h = lax.all_gather(w2, PAIRS, axis=0, tiled=True)
-    mine = lax.dynamic_slice(w1_t, (lax.axis_index("x") * 24, 0), (24, w1_t.shape[1]))
-    bias = jnp.pad(b1[None], ((0, 7), (0, w1_t.shape[1] - b1.shape[0])))
-    pieces = gather(gather(jnp.concatenate([mine, bias], axis=0), "z"), "y_lo")
-    b1_h = pieces[:, :, 24, : b1.shape[0]].reshape(-1).astype(jnp.float32)
-    w1_h = gather(pieces[:, :, :24], "x").transpose(1, 2, 0, 3, 4).reshape(w2_h.shape)
-    return w1_h, w2_h, b1_h
-
-
-def scatter_terms(terms):
-    share = lax.psum_scatter(terms, PAIRS, scatter_dimension=0, tiled=True)
-    part = spread_sum(share.reshape(-1, LANES), ROWS).astype(jnp.bfloat16)
-    return gather(part, ROWS).reshape(share.shape).astype(jnp.float32)
-
-
-BLOCK = 256
+def across(cells, m):
+    flip = (m % 2) * 2 + m // 2
+    return lax.ppermute(cells, Y, [(i, i ^ flip) for i in range(4)])
+
+
+def relative(cells):
+    half = cells.shape[-1] // 2
+    turned = jnp.concatenate([cells[..., half:], cells[..., :half]], axis=-1)
+    return jnp.where(lax.axis_index("y_hi") == 1, turned, cells)
+
+
+def gather_z(w1_t, w2, b1):
+    x, y_hi = lax.axis_index("x"), lax.axis_index("y_hi")
+    mine = [lax.dynamic_slice(w, (x * 24, y_hi * 384), (24, 384)) for w in (w1_t, w2)]
+    bias = jnp.pad(b1[None], ((0, 7), (0, 384 - b1.shape[0])))
+    return gather(jnp.concatenate(mine + [bias], axis=0), "z")
+
+
+def gather_w1(along_z):
+    part = along_z[:, :24].reshape(192, 384)
+    near, far, last = [across(part, m) for m in (1, 2, 3)]
+    whole = jnp.concatenate(
+        [jnp.concatenate([part, far], axis=1), jnp.concatenate([near, last], axis=1)], axis=0
+    )
+    return gather(whole, "x").reshape(-1, 768)
+
+
+def gather_w2(part):
+    half = part.shape[0] // 2
+    near, last = across(part, 1), across(part, 3)
+    far = jnp.concatenate([across(last[:half], 1), across(near[half:], 3)], axis=0)
+    return part, near, far, last
+
+
+def gather_b1(along_z):
+    bias = along_z[:, 48, :96]
+    bias = jnp.stack([bias, across(bias, 1)]).reshape(2, 8, 4, 24).astype(jnp.float32)
+    return bias.transpose(2, 0, 1, 3).reshape(-1)
+
+
+def scatter_terms(d_w1, parts):
+    own, near, far, last = parts
+    half = far.shape[0] // 2
+    up = across(far[:half], 1).astype(jnp.float32)
+    down = across(far[half:], 3).astype(jnp.float32)
+    last = jnp.concatenate(
+        [(last[:half].astype(jnp.float32) + up).astype(jnp.bfloat16), last[half:]], axis=0
+    )
+    near = jnp.concatenate(
+        [near[:half], (near[half:].astype(jnp.float32) + down).astype(jnp.bfloat16)], axis=0
+    )
+    second = own.astype(jnp.float32)
+    second = second + across(near, 1).astype(jnp.float32) + across(last, 3).astype(jnp.float32)
+    first = spread_sum(d_w1, "x").astype(jnp.bfloat16)
+    first, second = lax.optimization_barrier((first, second.astype(jnp.bfloat16)))
+    second = spread_sum(second, "x")
+    sent = (first[192:, :384], first[:192, 384:], first[192:, 384:])
+    first = first[:192, :384].astype(jnp.float32)
+    for m in (1, 2, 3):
+        first = first + across(sent[m - 1], m).astype(jnp.float32)
+    return first, second
+
+
+def two(cells):
+    high = lax.reduce_precision(cells, 8, 7)
+    return jnp.concatenate([high, cells - high], axis=0).astype(jnp.bfloat16)
+
+
+def finish(first, second, small):
+    small = small + swap(small)
+    small = small + lax.ppermute(small, "y_lo", [(0, 1), (1, 0)])
+    first, second, small = lax.optimization_barrier((first, second, small))
+    small = two(spread_sum(small, ROWS))
+    terms = jnp.concatenate([first, second], axis=1).astype(jnp.bfloat16).reshape(8, 24, 768)
+    small = jnp.broadcast_to(small[None], (8,) + small.shape)
+    pieces = lax.all_to_all(jnp.concatenate([terms, small], axis=1), "z", 0, 0)
+    total = jnp.sum(pieces.astype(jnp.float32), axis=0)
+    small = total[24:32] + total[32:]
+    total = gather(jnp.concatenate([total[:24].astype(jnp.bfloat16), two(small)], axis=0), ROWS)
+    total = total.astype(jnp.float32)
+    blocks = total[:, :24].reshape(2, 4, 24, 2, 384).transpose(3, 1, 2, 0, 4).reshape(2, 96, 768)
+    return blocks[0], blocks[1], (total[:, 24:32] + total[:, 32:]).reshape(-1, 768)
+
+
+BLOCK = 384
 LANES = 128
 NT = (((1,), (1,)), ((), ()))
 NN = (((1,), (0,)), ((), ()))
 TN = (((0,), (0,)), ((), ()))
-VMEM = 50 * 2**20
-
-
-def mlp_kernel(normed, scaled, w1, w2, b1, terms, grad_normed, d_b1, row):
+VMEM = 56 * 2**20
+
+
+def mlp_kernel(
+    normed, scaled, w1, q0, q1, q2, q3, b1, d_w1, m0, m1, m2, m3, own, peer, d_b1, row, sums
+):
     @pl.when(pl.program_id(0) == 0)
     def _():
-        grad_normed[...] = jnp.zeros_like(grad_normed)
+        sums[...] = jnp.zeros_like(sums)
         row[...] = jnp.zeros_like(row)
 
     n, s = normed[...], scaled[...]
+    high, wide = q0.shape
+    w2 = jnp.concatenate(
+        [
+            jnp.concatenate([q0[...], q2[...]], axis=1),
+            jnp.concatenate([q1[...], q3[...]], axis=1),
+        ],
+        axis=0,
+    )
     preact = lax.dot_general(w1[...], n, NT, preferred_element_type=jnp.float32) + b1[:, :1]
     cdf = 0.5 * (1.0 + lax.erf(preact * INV_ROOT_TWO))
     hidden = (preact * cdf).astype(jnp.bfloat16)
     slope = cdf + preact * jnp.exp(-0.5 * preact * preact) * INV_ROOT_TWO_PI
-    grad_hidden = lax.dot_general(w2[...], s, NT, preferred_element_type=jnp.float32)
+    grad_hidden = lax.dot_general(w2, s, NT, preferred_element_type=jnp.float32)
     grad_preact = (grad_hidden * slope).astype(jnp.bfloat16)
-    total = lax.dot_general(hidden, s, NN, preferred_element_type=jnp.float32)
-    terms[:, n.shape[1] :] = total.astype(jnp.bfloat16)
-    row[...] += jnp.sum(total * w2[...].astype(jnp.float32), axis=0, keepdims=True)
-    terms[:, : n.shape[1]] = lax.dot_general(
-        grad_preact, n, NN, preferred_element_type=jnp.float32
-    ).astype(jnp.bfloat16)
+    d_w1[...] = lax.dot_general(grad_preact, n, NN, preferred_element_type=jnp.float32).astype(
+        jnp.bfloat16
+    )
+    moment = lax.dot_general(hidden, s, NN, preferred_element_type=jnp.float32)
+    m0[...] = moment[:high, :wide].astype(jnp.bfloat16)
+    m1[...] = moment[high:, :wide].astype(jnp.bfloat16)
+    m2[...] = moment[:high, wide:].astype(jnp.bfloat16)
+    m3[...] = moment[high:, wide:].astype(jnp.bfloat16)
+    row[...] += jnp.sum(moment * w2.astype(jnp.float32), axis=0, keepdims=True)
     d_b1[...] = jnp.broadcast_to(
         jnp.sum(grad_preact.astype(jnp.float32), axis=1, keepdims=True), d_b1.shape
     )
-    grad_normed[...] += lax.dot_general(
-        grad_preact, w1[...], TN, preferred_element_type=jnp.float32
-    )
-
-
-def mlp(normed, scaled, w1, w2, b1):
+    sums[...] += lax.dot_general(grad_preact, w1[...], TN, preferred_element_type=jnp.float32)
+
+    @pl.when(pl.program_id(0) == pl.num_programs(0) - 1)
+    def _():
+        half = own.shape[0]
+        own[...] = sums[:half]
+        peer[...] = sums[half:].astype(jnp.bfloat16)
+
+
+def mlp(normed, scaled, w1, parts, b1):
     pixels, chans = normed.shape
     hid = w1.shape[0]
     whole = pl.BlockSpec((pixels, chans), lambda i: (0, 0))
+    half = pl.BlockSpec((pixels // 2, chans), lambda i: (0, 0))
     block = pl.BlockSpec((BLOCK, chans), lambda i: (i, 0))
-    both = pl.BlockSpec((BLOCK, 2 * chans), lambda i: (i, 0))
+    part = pl.BlockSpec((BLOCK // 2, chans // 2), lambda i: (i, 0))
     lane = pl.BlockSpec((BLOCK, LANES), lambda i: (i, 0))
     return pl.pallas_call(
         mlp_kernel,
         grid=(hid // BLOCK,),
-        in_specs=[whole, whole, block, block, lane],
-        out_specs=[both, whole, lane, pl.BlockSpec((1, chans), lambda i: (0, 0))],
-        out_shape=[
-            jax.ShapeDtypeStruct((hid, 2 * chans), jnp.bfloat16),
-            jax.ShapeDtypeStruct((pixels, chans), jnp.float32),
+        in_specs=[whole, whole, block] + [part] * 4 + [lane],
+        out_specs=[block] + [part] * 4 + [half, half, lane, pl.BlockSpec((1, chans), lambda i: (0, 0))],
+        out_shape=[jax.ShapeDtypeStruct((hid, chans), jnp.bfloat16)]
+        + [jax.ShapeDtypeStruct((hid // 2, chans // 2), jnp.bfloat16)] * 4
+        + [
+            jax.ShapeDtypeStruct((pixels // 2, chans), jnp.float32),
+            jax.ShapeDtypeStruct((pixels // 2, chans), jnp.bfloat16),
             jax.ShapeDtypeStruct((hid, LANES), jnp.float32),
             jax.ShapeDtypeStruct((1, chans), jnp.float32),
         ],
+        scratch_shapes=[pltpu.VMEM((pixels, chans), jnp.float32)],
         compiler_params=pltpu.CompilerParams(vmem_limit_bytes=VMEM),
         cost_estimate=pl.CostEstimate(
             flops=10 * pixels * hid * chans, bytes_accessed=2**24, transcendentals=2 * pixels * hid
         ),
-    )(normed, scaled, w1, w2, jnp.broadcast_to(b1[:, None], (hid, LANES)))
+    )(normed, scaled, w1, *parts, jnp.broadcast_to(b1[:, None], (hid, LANES)))
 
 
 def transposed_kernel(padded, cotangent, kernel, d_input, wide):
@@ -233,9 +314,15 @@
     pixels = images * rows_here * cols
     flat_cot = cotangent.reshape(pixels, chans).astype(jnp.float32)
     scaled = (flat_cot * gamma).astype(jnp.bfloat16)
-    w1_t, w2_h, b1_h = gather_weights(w1.T, w2, b1)
-
-    padded = pad_columns(halo(block_input))
+    along_z = gather_z(w1.T, w2, b1)
+    maps, along_z = lax.optimization_barrier((block_input, along_z))
+    w2_part = gather(along_z[:, 24:48].reshape(192, 384), "x").reshape(768, 384)
+    w1_h = gather_w1(along_z)
+    b1_h = gather_b1(along_z)
+    padded, w2_part = lax.optimization_barrier((halo(maps), w2_part))
+    padded = pad_columns(padded)
+    w2_parts = gather_w2(w2_part)
+    scaled = relative(scaled)
     scaled2 = jnp.concatenate([scaled, swap(scaled)], axis=0)
     conv = depthwise(padded, dw_kernel, rows_here, cols) + dw_bias
     center = conv - jnp.mean(conv, axis=-1, keepdims=True)
@@ -243,13 +330,13 @@
     rstd = lax.rsqrt(spread + EPSILON).reshape(pixels, 1)
     norm = center.reshape(pixels, chans) * rstd
     normed = (norm * ln_gain + ln_bias).astype(jnp.bfloat16)
+    normed = relative(normed)
     normed2 = jnp.concatenate([normed, swap(normed)], axis=0)
 
-    terms, grad_normed2, sums_b1, moment_row = mlp(normed2, scaled2, w1_t, w2_h, b1_h)
-    grad_normed = grad_normed2[:pixels] + swap(grad_normed2[pixels:].astype(jnp.bfloat16)).astype(
-        jnp.float32
-    )
-    share = scatter_terms(terms)
+    d_w1, *parts, own, peer, sums_b1, moment_row = mlp(normed2, scaled2, w1_h, w2_parts, b1_h)
+    first, second = scatter_terms(d_w1, parts)
+    grad_normed = relative(own + swap(peer).astype(jnp.float32))
+    moment_row = relative(moment_row)
 
     weighted = grad_normed * ln_gain
     grad_conv = (
@@ -267,7 +354,8 @@
     grad_wide = grad_maps.astype(jnp.float32)
     cot_sums = jnp.sum(flat_cot, axis=0)
     core = lax.axis_index("core")
-    sums_b1 = sums_b1[:, 0][None]
+    y_lo = lax.axis_index("y_lo")
+    sums_b1 = jnp.roll(sums_b1[:, 0].reshape(4, 2, 8, 24), y_lo, 1).reshape(1, -1)
     pair_b1 = jnp.where(core == jnp.arange(2)[:, None], sums_b1, 0.0)
     local_small = jnp.concatenate(
         [
@@ -278,17 +366,17 @@
             (gamma * cot_sums)[None],
             moment_row / gamma + b2 * cot_sums,
             pair_b1.reshape(-1, chans),
+            jnp.zeros((6, chans), jnp.float32),
         ],
         axis=0,
     )
-    total_small = total(local_small)
+    d_w1, d_w2, total_small = finish(first, second, local_small)
     factor = 1.0 / math.sqrt(pixels * 256)
     param_grads = total_small[:54] * factor
-    at = (lax.axis_index("y_lo") * 8 + lax.axis_index("z")) * shard
-    sums = total_small[54:].reshape(2, -1)
-    d_b1 = lax.dynamic_slice(sums, (core, at), (1, shard)).reshape(shard) * factor
-    share = share * factor
-    d_w1, d_w2 = share[:, :chans].T, share[:, chans:]
+    sums = total_small[54:58].reshape(2, 4, 2, 8, 24)
+    mine = (core, 0, y_lo, lax.axis_index("z"), 0)
+    d_b1 = lax.dynamic_slice(sums, mine, (1, 4, 1, 1, 24)).reshape(shard) * factor
+    d_w1, d_w2 = (d_w1 * factor).T, d_w2 * factor
     return (d_input.reshape(block_input.shape), d_w1, d_b1, d_w2, param_grads)
 
 

time: 261 us -> 254 us (0.973)
  waiting for transfers between devices: 53.8 us -> 36.4 us
  between operations: 14.7 us -> 1.29 us
  blocking collectives: 0 us -> 12.3 us
  Pallas kernels: 36 us -> 43.7 us
  other arithmetic: 41.8 us -> 45.5 us
  local copies, waits for them, and re-layouts: 28.6 us -> 32.1 us
  starting transfers between devices: 84.3 us -> 81 us
    all_to_all x6 -> x4, waiting for transfers between devices: 44.2 us -> 9.7 us  [gather(): lax.all_to_all(jnp.broadcast_to(part[None], (count,) + part.shape), axes,...]
    ppermute x0 -> x16, starting transfers between devices: none -> 23.8 us  [the longest x15 21.7 us: across(): return lax.ppermute(cells, Y, [(i, i ^ flip) for i in range(4)])]
    all_to_all x6 -> x4, starting transfers between devices: 54.6 us -> 31.8 us  [gather(): lax.all_to_all(jnp.broadcast_to(part[None], (count,) + part.shape), axes,...]
    ppermute x0 -> x16, waiting for transfers between devices: none -> 18.5 us  [the longest x15 18.5 us: across(): return lax.ppermute(cells, Y, [(i, i ^ flip) for i in range(4)])]
    all_to_all x0 -> x1, blocking collectives: none -> 12.3 us  [spread_sum(): pieces = lax.all_to_all(pieces, axes, 0, 0)]
    all_to_all x2, starting transfers between devices: 17.5 us -> 9.8 us  [spread_sum(): pieces = lax.all_to_all(pieces, axes, 0, 0)]
    ppermute x2, waiting for transfers between devices: 0.01 us -> 5.46 us  [halo(): below = lax.ppermute(cells[:, :MARGIN], ROWS, up)]
    all_to_all x2, waiting for transfers between devices: 4.96 us -> 0.01 us  [spread_sum(): pieces = lax.all_to_all(pieces, axes, 0, 0)]
  transfers between devices with their start and end apart: 17 -> 31, of which waited for: 8 -> 10; matrix products, arithmetic and copies ran while one was open for 24% -> 26% of each run, Pallas kernels for 6% -> 8%
where the time goes in v1:
time: 254 us; the launch traced here: 252 us
  starting transfers between devices  81 us (32%)
  other arithmetic  45.5 us (18%)
  Pallas kernels  43.7 us (17%)
  waiting for transfers between devices  36.4 us (14%)
  local copies, waits for them, and re-layouts  32.1 us (13%)
  blocking collectives  12.3 us (5%)
    all_to_all x4, starting transfers between devices, gather(): lax.all_to_all(jnp.broadcast_to(part[None], (count,) + part.shape), axes,...  31.8 us
    pallas_call x1, Pallas kernels, mlp(): pl.pallas_call(mlp_kernel, grid=(hid // BLOCK,), in_specs=[whole, whole,...  22.7 us
    ppermute x15, starting transfers between devices, across(): return lax.ppermute(cells, Y, [(i, i ^ flip) for i in range(4)])  21.7 us
    ppermute x15, waiting for transfers between devices, across(): return lax.ppermute(cells, Y, [(i, i ^ flip) for i in range(4)])  18.5 us
    reduce_sum x1, other arithmetic, shards(): center = conv - jnp.mean(conv, axis=-1, keepdims=True)  13.9 us
    all_to_all x1, blocking collectives, spread_sum(): pieces = lax.all_to_all(pieces, axes, 0, 0)  12.3 us
    pallas_call x1, Pallas kernels, tap_sums(): pl.pallas_call(taps_kernel, grid=(chans // LANES, images), in_specs=[pl.B...  10.7 us
    pallas_call x1, Pallas kernels, transposed(): pl.pallas_call(transposed_kernel, grid=(chans // LANES, images), in_specs...  10.3 us
  transfers between devices with their start and end apart: 31, of which 10 were waited for; matrix products, arithmetic and copies ran while one was open for 26% of the time, Pallas kernels for 8%

profile of v1, /device:TPU:2, one launch (start us, length us, event | category | flops | bytes accessed | tf_op | source)
XLA Modules:
  0.0 252.4 jit_solution(6274665103679255238)
XLA Ops:
  3.3 8.5 %all-to-all-start = ((bf16[8,56,384]{2,1,0:T(8,128)(2,1)}), bf16[8,56,384]{2,1,0:T(8,128)(2,1)S(1)}, u32[]{:S(2)}, u32[]{:S(2)}) async-start(bf16[8,56,384]{2,1,0:T(8,128)(2,1)} %broadcast_in_dim.104), calls=%async_computation | async-start | bytes 688128 | tf_op jit(solution)/shard_map/all_to_all | solution.py:46
  15.7 9.7 %all-to-all-done = bf16[8,56,384]{2,1,0:T(8,128)(2,1)S(1)} async-done(((bf16[8,56,384]{2,1,0:T(8,128)(2,1)}), bf16[8,56,384]{2,1,0:T(8,128)(2,1)S(1)}, u32[]{:S(2)}, u32[]{:S(2)}) %all-to-all-start) | async-done | bytes 344096 | tf_op jit(solution)/shard_map/all_to_all | solution.py:46
  28.7 3.4 %collective-permute-start = (bf16[2,3,48,768]{3,2,1,0:T(8,128)(2,1)S(1)}, bf16[2,3,48,768]{3,2,1,0:T(8,128)(2,1)}, u32[]{:S(2)}, u32[]{:S(2)}) collective-permute-start(bf16[2,3,48,768]{3,2,1,0:T(8,128)(2,1)S(1)} %get-tuple-element.111), channel_id=1, source_target_pairs={{0,1},{1,2},{2,3},{3,4},{4,5},{5,6},{6,7},{8,9},{9,10},{10,11},{11... | collective-permute-start | bytes 1327112 | tf_op jit(solution)/shard_map/ppermute | solution.py:28
  33.1 8.2 %all-to-all-start.1 = ((bf16[4,192,384]{2,1,0:T(8,128)(2,1)}), bf16[4,192,384]{2,1,0:T(8,128)(2,1)}, u32[]{:S(2)}, u32[]{:S(2)}) async-start(bf16[4,192,384]{2,1,0:T(8,128)(2,1)} %broadcast_in_dim.106), calls=%async_computation.1 | async-start | bytes 1179648 | tf_op jit(solution)/shard_map/all_to_all | solution.py:46
  43.1 3.0 %collective-permute-start.4 = (bf16[192,384]{1,0:T(8,128)(2,1)S(1)}, bf16[192,384]{1,0:T(8,128)(2,1)S(1)}, u32[]{:S(2)}, u32[]{:S(2)}) collective-permute-start(bf16[192,384]{1,0:T(8,128)(2,1)S(1)} %bitcast.57), channel_id=1, source_target_pairs={{0,4},{4,0},{128,132},{132,128},{1,5},{5,1},{129,133},{133,129},{2... | collective-permute-start | bytes 442376 | tf_op jit(solution)/shard_map/ppermute | solution.py:51
  53.8 6.2 %all-to-all-start.2 = ((bf16[4,384,768]{2,1,0:T(8,128)(2,1)}), bf16[4,384,768]{2,1,0:T(8,128)(2,1)}, u32[]{:S(2)}, u32[]{:S(2)}) async-start(bf16[4,384,768]{2,1,0:T(8,128)(2,1)} %broadcast_in_dim.107), calls=%async_computation.2 | async-start | bytes 4718592 | tf_op jit(solution)/shard_map/all_to_all | solution.py:46
  61.5 3.1 %collective-permute-start.8 = (bf16[768,384]{1,0:T(8,128)(2,1)}, bf16[768,384]{1,0:T(8,128)(2,1)}, u32[]{:S(2)}, u32[]{:S(2)}) collective-permute-start(bf16[768,384]{1,0:T(8,128)(2,1)} %bitcast.3.q0), channel_id=1, source_target_pairs={{0,132},{4,128},{128,4},{132,0},{1,133},{5,129},{129,5},{133,1},{2... | collective-permute-start | bytes 1769480 | tf_op jit(solution)/shard_map/ppermute | solution.py:51
  64.7 13.9 %fusion.14 = (f32[2,6,48]{2,1,0:T(8,128)S(1)}, f32[2,6,48,768]{3,2,1,0:T(8,128)S(1)}) fusion(f32[768]{0:T(1024)S(1)} %copy-done.16, f32[768]{0:T(1024)S(1)} %get-tuple-element.93, f32[768]{0:T(1024)S(1)} %get-tuple-element.46, f32[768]{0:T(1024)S(1)} %get-tuple-element.47, f32[768]{0:T(1024)S(1)} %get-tuple-element.48, ...), kind=kLoop, calls=%fused_computation.126 | loop fusion | flops 65469888 | bytes 9939200 | tf_op jit(solution)/shard_map/reduce_sum | solution.py:328
  99.3 2.8 %pad_maximum_fusion.2.scaled = bf16[1152,768]{1,0:T(8,128)(2,1)} fusion(bf16[576,768]{1,0:T(8,128)(2,1)} %collective-permute-done.3, bf16[576,768]{1,0:T(8,128)(2,1)} %maximum_select_fusion.2), kind=kLoop, calls=%fused_computation.10 | loop fusion | flops 3538944 | bytes 3538944 | tf_op jit(solution)/shard_map/concatenate | solution.py:326
  104.3 3.4 %collective-permute-done.10 = bf16[384,384]{1,0:T(8,128)(2,1)S(1)} collective-permute-done((bf16[384,384]{1,0:T(8,128)(2,1)S(1)}, bf16[384,384]{1,0:T(8,128)(2,1)S(1)}, u32[]{:S(2)}, u32[]{:S(2)}) %collective-permute-start.10) | collective-permute-done | bytes 294944 | tf_op jit(solution)/shard_map/ppermute | solution.py:51
  109.0 2.8 %pad_maximum_fusion.1.normed = bf16[1152,768]{1,0:T(8,128)(2,1)} fusion(bf16[576,768]{1,0:T(8,128)(2,1)} %collective-permute-done.2, bf16[576,768]{1,0:T(8,128)(2,1)} %maximum_select_fusion.1), kind=kLoop, calls=%fused_computation.9 | loop fusion | flops 3538944 | bytes 3538944 | tf_op jit(solution)/shard_map/concatenate | solution.py:334
  113.0 22.7 %shard_map.146 = (bf16[1536,768]{1,0:T(8,128)(2,1)}, bf16[768,384]{1,0:T(8,128)(2,1)}, bf16[768,384]{1,0:T(8,128)(2,1)}, bf16[768,384]{1,0:T(8,128)(2,1)}, bf16[...) custom-call(bf16[1152,768]{1,0:T(8,128)(2,1)} %pad_maximum_fusion.1., ...), custom_call_target="tpu_custom_call" | custom-call | flops 13589544960 | bytes 16777216 | tf_op jit(solution)/shard_map/pallas_call | solution.py:193
  135.8 4.9 %all-to-all-start.3 = ((bf16[4,384,768]{2,1,0:T(8,128)(2,1)}), bf16[4,384,768]{2,1,0:T(8,128)(2,1)}, u32[]{:S(2)}, u32[]{:S(2)}) async-start(bf16[4,384,768]{2,1,0:T(8,128)(2,1)} %bitcast.50), calls=%async_computation.3 | async-start | bytes 4718592 | tf_op jit(solution)/shard_map/all_to_all | solution.py:40
  148.3 3.8 %collective-permute-done.17 = bf16[384,384]{1,0:T(8,128)(2,1)} collective-permute-done((bf16[384,384]{1,0:T(8,128)(2,1)}, bf16[384,384]{1,0:T(8,128)(2,1)}, u32[]{:S(2)}, u32[]{:S(2)}) %collective-permute-start.17) | collective-permute-done | bytes 294944 | tf_op jit(solution)/shard_map/ppermute | solution.py:51
  160.4 10.7 %shard_map.148 = f32[49,768]{1,0:T(8,128)} custom-call(bf16[2,12,56,768]{3,2,1,0:T(8,128)(2,1)} %pad.12.padded, bf16[2,6,48,768]{3,2,1,0:T(8,128)(2,1)} %bitcast.47), custom_call_target="tpu_custom_call" | custom-call | flops 10000000000 | bytes 4194304 | tf_op jit(solution)/shard_map/pallas_call | solution.py:278
  179.2 4.8 %all-to-all-start.4 = ((bf16[4,192,384]{2,1,0:T(8,128)(2,1)}), bf16[4,192,384]{2,1,0:T(8,128)(2,1)S(1)}, u32[]{:S(2)}, u32[]{:S(2)}) async-start(bf16[4,192,384]{2,1,0:T(8,128)(2,1)} %bitcast.11), calls=%async_computation.4 | async-start | bytes 1179648 | tf_op jit(solution)/shard_map/all_to_all | solution.py:40
  188.3 5.6 %collective-permute-done.21 = bf16[192,384]{1,0:T(8,128)(2,1)S(1)} collective-permute-done((bf16[192,384]{1,0:T(8,128)(2,1)S(1)}, bf16[192,384]{1,0:T(8,128)(2,1)S(1)}, u32[]{:S(2)}, u32[]{:S(2)}) %collective-permute-start.21) | collective-permute-done | bytes 147488 | tf_op jit(solution)/shard_map/ppermute | solution.py:51
  194.8 12.3 %all_to_all.40 = f32[8,8,768]{2,1,0:T(8,128)S(1)} all-to-all(f32[8,8,768]{2,1,0:T(8,128)S(1)} %bitcast.54), channel_id=1, replica_groups=mesh['y_lo'=2,'z'=8,'core'=2,'y_hi'=2,'x'=4] {'y_hi','x'}, dimensions={0} | all-to-all | bytes 393216 | tf_op jit(solution)/shard_map/all_to_all | solution.py:40
  208.0 3.5 %all-to-all-start.6 = ((bf16[8,40,768]{2,1,0:T(8,128)(2,1)}), bf16[8,40,768]{2,1,0:T(8,128)(2,1)S(1)}, u32[]{:S(2)}, u32[]{:S(2)}) async-start(bf16[8,40,768]{2,1,0:T(8,128)(2,1)} %pad_maximum_fusion.6), calls=%async_computation.6 | async-start | bytes 983040 | tf_op jit(solution)/shard_map/all_to_all | solution.py:124
  211.6 3.1 %collective-permute-start.14 = (bf16[2,3,48,768]{3,2,1,0:T(8,128)(2,1)S(1)}, bf16[2,3,48,768]{3,2,1,0:T(8,128)(2,1)S(1)}, u32[]{:S(2)}, u32[]{:S(2)}) collective-permute-start(bf16[2,3,48,768]{3,2,1,0:T(8,128)(2,1)S(1)} %get-tuple-element.106), channel_id=1, source_target_pairs={{1,0},{2,1},{3,2},{4,3},{5,4},{6,5},{7,6},{9,8},{10,9},{11,10},{12... | collective-permute-start | bytes 1327112 | tf_op jit(solution)/shard_map/ppermute | solution.py:29
  217.4 5.5 %collective-permute-done.14 = bf16[2,3,48,768]{3,2,1,0:T(8,128)(2,1)S(1)} collective-permute-done((bf16[2,3,48,768]{3,2,1,0:T(8,128)(2,1)S(1)}, bf16[2,3,48,768]{3,2,1,0:T(8,128)(2,1)S(1)}, u32[]{:S(2)}, u32[]{:S(2)}) %collective-permute-start.14) | collective-permute-done | bytes 442400 | tf_op jit(solution)/shard_map/ppermute | solution.py:29
  222.9 2.8 %collective-permute-done.13 = bf16[2,3,48,768]{3,2,1,0:T(8,128)(2,1)S(1)} collective-permute-done((bf16[2,3,48,768]{3,2,1,0:T(8,128)(2,1)S(1)}, bf16[2,3,48,768]{3,2,1,0:T(8,128)(2,1)S(1)}, u32[]{:S(2)}, u32[]{:S(2)}) %collective-permute-start.13) | collective-permute-done | bytes 442400 | tf_op jit(solution)/shard_map/ppermute | solution.py:28
  228.9 9.0 %all-to-all-start.7 = ((bf16[8,40,768]{2,1,0:T(8,128)(2,1)}), bf16[8,40,768]{2,1,0:T(8,128)(2,1)S(1)}, u32[]{:S(2)}, u32[]{:S(2)}) async-start(bf16[8,40,768]{2,1,0:T(8,128)(2,1)} %broadcast_in_dim.126), calls=%async_computation.7 | async-start | bytes 983040 | tf_op jit(solution)/shard_map/all_to_all | solution.py:46
  237.9 10.3 %shard_map.147 = bf16[2,6,48,768]{3,2,1,0:T(8,128)(2,1)} custom-call(bf16[2,12,56,768]{3,2,1,0:T(8,128)(2,1)} %fusion.5.padded, bf16[2,6,48,768]{3,2,1,0:T(8,128)(2,1)} %cotangent.1, f32[49,768]{1,0:T(8,128)} %kernel.1), custom_call_target="tpu_custom_call" | custom-call | flops 10000000000 | bytes 4194304 | tf_op jit(solution)/shard_map/pallas_call | solution.py:234
  (183 shorter events, 87.0 us)
Async XLA Ops:
  3.3 22.1 %all-to-all-start = ((bf16[8,56,384]{2,1,0:T(8,128)(2,1)}), bf16[8,56,384]{2,1,0:T(8,128)(2,1)S(1)}, u32[]{:S(2)}, u32[]{:S(2)}) async-start(bf16[8,56,384]{2,1,0:T(8,128)(2,1)} %broadcast_in_dim.104), calls=%async_computation | async-start | bytes 688128 | tf_op jit(solution)/shard_map/all_to_all | solution.py:46
  26.3 24.6 %collective-permute-start.1 = (bf16[2,3,48,768]{3,2,1,0:T(8,128)(2,1)}, bf16[2,3,48,768]{3,2,1,0:T(8,128)(2,1)}, u32[]{:S(2)}, u32[]{:S(2)}) collective-permute-start(bf16[2,3,48,768]{3,2,1,0:T(8,128)(2,1)} %get-tuple-element.112), channel_id=1, source_target_pairs={{1,0},{2,1},{3,2},{4,3},{5,4},{6,5},{7,6},{9,8},{10,9},{11,10},{12... | collective-permute-start | bytes 1327112 | tf_op jit(solution)/shard_map/ppermute | solution.py:29
  28.7 22.1 %collective-permute-start = (bf16[2,3,48,768]{3,2,1,0:T(8,128)(2,1)S(1)}, bf16[2,3,48,768]{3,2,1,0:T(8,128)(2,1)}, u32[]{:S(2)}, u32[]{:S(2)}) collective-permute-start(bf16[2,3,48,768]{3,2,1,0:T(8,128)(2,1)S(1)} %get-tuple-element.111), channel_id=1, source_target_pairs={{0,1},{1,2},{2,3},{3,4},{4,5},{5,6},{6,7},{8,9},{9,10},{10,11},{11... | collective-permute-start | bytes 1327112 | tf_op jit(solution)/shard_map/ppermute | solution.py:28
  33.1 19.2 %all-to-all-start.1 = ((bf16[4,192,384]{2,1,0:T(8,128)(2,1)}), bf16[4,192,384]{2,1,0:T(8,128)(2,1)}, u32[]{:S(2)}, u32[]{:S(2)}) async-start(bf16[4,192,384]{2,1,0:T(8,128)(2,1)} %broadcast_in_dim.106), calls=%async_computation.1 | async-start | bytes 1179648 | tf_op jit(solution)/shard_map/all_to_all | solution.py:46
  48.3 51.0 %collective-permute-start.3 = (bf16[576,768]{1,0:T(8,128)(2,1)}, bf16[576,768]{1,0:T(8,128)(2,1)}, u32[]{:S(2)}, u32[]{:S(2)}) collective-permute-start(bf16[576,768]{1,0:T(8,128)(2,1)} %maximum_select_fusion.2), channel_id=1, source_target_pairs={{0,8},{8,0},{1,9},{9,1},{2,10},{10,2},{3,11},{11,3},{4,12},{12,4},... | collective-permute-start | bytes 2654216 | tf_op jit(solution)/shard_map/ppermute | solution.py:34
  53.8 58.0 %all-to-all-start.2 = ((bf16[4,384,768]{2,1,0:T(8,128)(2,1)}), bf16[4,384,768]{2,1,0:T(8,128)(2,1)}, u32[]{:S(2)}, u32[]{:S(2)}) async-start(bf16[4,384,768]{2,1,0:T(8,128)(2,1)} %broadcast_in_dim.107), calls=%async_computation.2 | async-start | bytes 4718592 | tf_op jit(solution)/shard_map/all_to_all | solution.py:46
  60.0 36.3 %collective-permute-start.7 = (bf16[768,384]{1,0:T(8,128)(2,1)}, bf16[768,384]{1,0:T(8,128)(2,1)}, u32[]{:S(2)}, u32[]{:S(2)}) collective-permute-start(bf16[768,384]{1,0:T(8,128)(2,1)} %bitcast.3.q0), channel_id=1, source_target_pairs={{0,128},{4,132},{128,0},{132,4},{1,129},{5,133},{129,1},{133,5},{2... | collective-permute-start | bytes 1769480 | tf_op jit(solution)/shard_map/ppermute | solution.py:51
  61.5 36.4 %collective-permute-start.8 = (bf16[768,384]{1,0:T(8,128)(2,1)}, bf16[768,384]{1,0:T(8,128)(2,1)}, u32[]{:S(2)}, u32[]{:S(2)}) collective-permute-start(bf16[768,384]{1,0:T(8,128)(2,1)} %bitcast.3.q0), channel_id=1, source_target_pairs={{0,132},{4,128},{128,4},{132,0},{1,133},{5,129},{129,5},{133,1},{2... | collective-permute-start | bytes 1769480 | tf_op jit(solution)/shard_map/ppermute | solution.py:51
  83.2 25.8 %collective-permute-start.2 = (bf16[576,768]{1,0:T(8,128)(2,1)}, bf16[576,768]{1,0:T(8,128)(2,1)}, u32[]{:S(2)}, u32[]{:S(2)}) collective-permute-start(bf16[576,768]{1,0:T(8,128)(2,1)} %maximum_select_fusion.1), channel_id=1, source_target_pairs={{0,8},{8,0},{1,9},{9,1},{2,10},{10,2},{3,11},{11,3},{4,12},{12,4},... | collective-permute-start | bytes 2654216 | tf_op jit(solution)/shard_map/ppermute | solution.py:34
  97.3 10.4 %collective-permute-start.10 = (bf16[384,384]{1,0:T(8,128)(2,1)S(1)}, bf16[384,384]{1,0:T(8,128)(2,1)S(1)}, u32[]{:S(2)}, u32[]{:S(2)}) collective-permute-start(bf16[384,384]{1,0:T(8,128)(2,1)S(1)} %slice.559), channel_id=1, source_target_pairs={{0,132},{4,128},{128,4},{132,0},{1,133},{5,129},{129,5},{133,1},{2... | collective-permute-start | bytes 884744 | tf_op jit(solution)/shard_map/ppermute | solution.py:51
  135.7 22.3 %collective-permute-start.12 = (bf16[576,768]{1,0:T(8,128)(2,1)}, bf16[576,768]{1,0:T(8,128)(2,1)S(1)}, u32[]{:S(2)}, u32[]{:S(2)}) collective-permute-start(bf16[576,768]{1,0:T(8,128)(2,1)} %get-tuple-element.28), channel_id=1, source_target_pairs={{0,8},{8,0},{1,9},{9,1},{2,10},{10,2},{3,11},{11,3},{4,12},{12,4},... | collective-permute-start | bytes 2654216 | tf_op jit(solution)/shard_map/ppermute | solution.py:34
  135.8 41.1 %all-to-all-start.3 = ((bf16[4,384,768]{2,1,0:T(8,128)(2,1)}), bf16[4,384,768]{2,1,0:T(8,128)(2,1)}, u32[]{:S(2)}, u32[]{:S(2)}) async-start(bf16[4,384,768]{2,1,0:T(8,128)(2,1)} %bitcast.50), calls=%async_computation.3 | async-start | bytes 4718592 | tf_op jit(solution)/shard_map/all_to_all | solution.py:40
  142.8 9.4 %collective-permute-start.17 = (bf16[384,384]{1,0:T(8,128)(2,1)}, bf16[384,384]{1,0:T(8,128)(2,1)}, u32[]{:S(2)}, u32[]{:S(2)}) collective-permute-start(bf16[384,384]{1,0:T(8,128)(2,1)} %get-tuple-element.119), channel_id=1, source_target_pairs={{0,128},{4,132},{128,0},{132,4},{1,129},{5,133},{129,1},{133,5},{2... | collective-permute-start | bytes 884744 | tf_op jit(solution)/shard_map/ppermute | solution.py:51
  143.0 13.8 %collective-permute-start.15 = (bf16[384,384]{1,0:T(8,128)(2,1)}, bf16[384,384]{1,0:T(8,128)(2,1)}, u32[]{:S(2)}, u32[]{:S(2)}) collective-permute-start(bf16[384,384]{1,0:T(8,128)(2,1)} %get-tuple-element.118), channel_id=1, source_target_pairs={{0,132},{4,128},{128,4},{132,0},{1,133},{5,129},{129,5},{133,1},{2... | collective-permute-start | bytes 884744 | tf_op jit(solution)/shard_map/ppermute | solution.py:51
  154.2 18.3 %collective-permute-start.18 = (bf16[768,384]{1,0:T(8,128)(2,1)}, bf16[768,384]{1,0:T(8,128)(2,1)}, u32[]{:S(2)}, u32[]{:S(2)}) collective-permute-start(bf16[768,384]{1,0:T(8,128)(2,1)} %pad_maximum_fusion.5), channel_id=1, source_target_pairs={{0,132},{4,128},{128,4},{132,0},{1,133},{5,129},{129,5},{133,1},{2... | collective-permute-start | bytes 1769480 | tf_op jit(solution)/shard_map/ppermute | solution.py:51
  157.9 14.6 %collective-permute-start.16 = (bf16[768,384]{1,0:T(8,128)(2,1)S(1)}, bf16[768,384]{1,0:T(8,128)(2,1)}, u32[]{:S(2)}, u32[]{:S(2)}) collective-permute-start(bf16[768,384]{1,0:T(8,128)(2,1)S(1)} %pad_maximum_fusion.4), channel_id=1, source_target_pairs={{0,128},{4,132},{128,0},{132,4},{1,129},{5,133},{129,1},{133,5},{2... | collective-permute-start | bytes 1769480 | tf_op jit(solution)/shard_map/ppermute | solution.py:51
  174.8 13.5 %collective-permute-start.23 = (f32[64,768]{1,0:T(8,128)S(1)}, f32[64,768]{1,0:T(8,128)S(1)}, u32[]{:S(2)}, u32[]{:S(2)}) collective-permute-start(f32[64,768]{1,0:T(8,128)S(1)} %add.312), channel_id=1, source_target_pairs={{0,128},{128,0},{1,129},{129,1},{2,130},{130,2},{3,131},{131,3},{4... | collective-permute-start | bytes 589832 | tf_op jit(solution)/shard_map/ppermute | solution.py:119
  179.2 15.5 %all-to-all-start.4 = ((bf16[4,192,384]{2,1,0:T(8,128)(2,1)}), bf16[4,192,384]{2,1,0:T(8,128)(2,1)S(1)}, u32[]{:S(2)}, u32[]{:S(2)}) async-start(bf16[4,192,384]{2,1,0:T(8,128)(2,1)} %bitcast.11), calls=%async_computation.4 | async-start | bytes 1179648 | tf_op jit(solution)/shard_map/all_to_all | solution.py:40
  184.1 9.8 %collective-permute-start.21 = (bf16[192,384]{1,0:T(8,128)(2,1)S(1)}, bf16[192,384]{1,0:T(8,128)(2,1)S(1)}, u32[]{:S(2)}, u32[]{:S(2)}) collective-permute-start(bf16[192,384]{1,0:T(8,128)(2,1)S(1)} %get-tuple-element.116), channel_id=1, source_target_pairs={{0,132},{4,128},{128,4},{132,0},{1,133},{5,129},{129,5},{133,1},{2... | collective-permute-start | bytes 442376 | tf_op jit(solution)/shard_map/ppermute | solution.py:51
  184.8 9.1 %collective-permute-start.20 = (bf16[192,384]{1,0:T(8,128)(2,1)S(1)}, bf16[192,384]{1,0:T(8,128)(2,1)S(1)}, u32[]{:S(2)}, u32[]{:S(2)}) collective-permute-start(bf16[192,384]{1,0:T(8,128)(2,1)S(1)} %get-tuple-element.117), channel_id=1, source_target_pairs={{0,4},{4,0},{128,132},{132,128},{1,5},{5,1},{129,133},{133,129},{2... | collective-permute-start | bytes 442376 | tf_op jit(solution)/shard_map/ppermute | solution.py:51
  208.0 19.9 %all-to-all-start.6 = ((bf16[8,40,768]{2,1,0:T(8,128)(2,1)}), bf16[8,40,768]{2,1,0:T(8,128)(2,1)S(1)}, u32[]{:S(2)}, u32[]{:S(2)}) async-start(bf16[8,40,768]{2,1,0:T(8,128)(2,1)} %pad_maximum_fusion.6), calls=%async_computation.6 | async-start | bytes 983040 | tf_op jit(solution)/shard_map/all_to_all | solution.py:124
  211.6 11.3 %collective-permute-start.14 = (bf16[2,3,48,768]{3,2,1,0:T(8,128)(2,1)S(1)}, bf16[2,3,48,768]{3,2,1,0:T(8,128)(2,1)S(1)}, u32[]{:S(2)}, u32[]{:S(2)}) collective-permute-start(bf16[2,3,48,768]{3,2,1,0:T(8,128)(2,1)S(1)} %get-tuple-element.106), channel_id=1, source_target_pairs={{1,0},{2,1},{3,2},{4,3},{5,4},{6,5},{7,6},{9,8},{10,9},{11,10},{12... | collective-permute-start | bytes 1327112 | tf_op jit(solution)/shard_map/ppermute | solution.py:29
  214.7 11.0 %collective-permute-start.13 = (bf16[2,3,48,768]{3,2,1,0:T(8,128)(2,1)S(1)}, bf16[2,3,48,768]{3,2,1,0:T(8,128)(2,1)S(1)}, u32[]{:S(2)}, u32[]{:S(2)}) collective-permute-start(bf16[2,3,48,768]{3,2,1,0:T(8,128)(2,1)S(1)} %get-tuple-element.105), channel_id=1, source_target_pairs={{0,1},{1,2},{2,3},{3,4},{4,5},{5,6},{6,7},{8,9},{9,10},{10,11},{11... | collective-permute-start | bytes 1327112 | tf_op jit(solution)/shard_map/ppermute | solution.py:28
  228.9 19.4 %all-to-all-start.7 = ((bf16[8,40,768]{2,1,0:T(8,128)(2,1)}), bf16[8,40,768]{2,1,0:T(8,128)(2,1)S(1)}, u32[]{:S(2)}, u32[]{:S(2)}) async-start(bf16[8,40,768]{2,1,0:T(8,128)(2,1)} %broadcast_in_dim.126), calls=%async_computation.7 | async-start | bytes 983040 | tf_op jit(solution)/shard_map/all_to_all | solution.py:46
  (26 other events, 202.0 us)

commit v2 on v1

--- a/solution.py
+++ b/solution.py
@@ -51,42 +51,13 @@
     return lax.ppermute(cells, Y, [(i, i ^ flip) for i in range(4)])
 
 
-def relative(cells):
-    half = cells.shape[-1] // 2
-    turned = jnp.concatenate([cells[..., half:], cells[..., :half]], axis=-1)
-    return jnp.where(lax.axis_index("y_hi") == 1, turned, cells)
-
-
-def gather_z(w1_t, w2, b1):
-    x, y_hi = lax.axis_index("x"), lax.axis_index("y_hi")
-    mine = [lax.dynamic_slice(w, (x * 24, y_hi * 384), (24, 384)) for w in (w1_t, w2)]
-    bias = jnp.pad(b1[None], ((0, 7), (0, 384 - b1.shape[0])))
-    return gather(jnp.concatenate(mine + [bias], axis=0), "z")
-
-
-def gather_w1(along_z):
-    part = along_z[:, :24].reshape(192, 384)
-    near, far, last = [across(part, m) for m in (1, 2, 3)]
-    whole = jnp.concatenate(
-        [jnp.concatenate([part, far], axis=1), jnp.concatenate([near, last], axis=1)], axis=0
-    )
-    return gather(whole, "x").reshape(-1, 768)
-
-
-def gather_w2(part):
-    half = part.shape[0] // 2
-    near, last = across(part, 1), across(part, 3)
-    far = jnp.concatenate([across(last[:half], 1), across(near[half:], 3)], axis=0)
-    return part, near, far, last
-
-
-def gather_b1(along_z):
-    bias = along_z[:, 48, :96]
-    bias = jnp.stack([bias, across(bias, 1)]).reshape(2, 8, 4, 24).astype(jnp.float32)
-    return bias.transpose(2, 0, 1, 3).reshape(-1)
-
-
-def scatter_terms(d_w1, parts):
+def gather_weights(w1_t, w2, b1):
+    whole = lax.all_gather(jnp.concatenate([w1_t, w2], axis=1), PAIRS, axis=0, tiled=True)
+    bias = gather(b1.astype(jnp.float32), PAIRS).reshape(-1)
+    return whole, bias
+
+
+def scatter_terms(first, parts):
     own, near, far, last = parts
     half = far.shape[0] // 2
     up = across(far[:half], 1).astype(jnp.float32)
@@ -99,13 +70,20 @@
     )
     second = own.astype(jnp.float32)
     second = second + across(near, 1).astype(jnp.float32) + across(last, 3).astype(jnp.float32)
-    first = spread_sum(d_w1, "x").astype(jnp.bfloat16)
+    first = jnp.sum(lax.all_to_all(first, "x", 0, 0).astype(jnp.float32), axis=0)
+    first = first.astype(jnp.bfloat16).reshape(2, 4, 2, 48, 384)
     first, second = lax.optimization_barrier((first, second.astype(jnp.bfloat16)))
     second = spread_sum(second, "x")
-    sent = (first[192:, :384], first[:192, 384:], first[192:, 384:])
-    first = first[:192, :384].astype(jnp.float32)
+    y_lo, y_hi = lax.axis_index("y_lo"), lax.axis_index("y_hi")
+    sent = [
+        lax.dynamic_slice(
+            first, (y_lo ^ (m % 2), 0, y_hi ^ (m // 2), 0, 0), (1, 4, 1, 48, 384)
+        ).reshape(192, 384)
+        for m in range(4)
+    ]
+    first = sent[0].astype(jnp.float32)
     for m in (1, 2, 3):
-        first = first + across(sent[m - 1], m).astype(jnp.float32)
+        first = first + across(sent[m], m).astype(jnp.float32)
     return first, second
 
 
@@ -118,16 +96,18 @@
     small = small + swap(small)
     small = small + lax.ppermute(small, "y_lo", [(0, 1), (1, 0)])
     first, second, small = lax.optimization_barrier((first, second, small))
-    small = two(spread_sum(small, ROWS))
-    terms = jnp.concatenate([first, second], axis=1).astype(jnp.bfloat16).reshape(8, 24, 768)
+    small = spread_sum(small, ROWS)
+    small = two(jnp.concatenate([small[:, :384], small[:, 384:]], axis=0))
+    terms = jnp.concatenate([first, second], axis=0).astype(jnp.bfloat16).reshape(8, 48, 384)
     small = jnp.broadcast_to(small[None], (8,) + small.shape)
     pieces = lax.all_to_all(jnp.concatenate([terms, small], axis=1), "z", 0, 0)
     total = jnp.sum(pieces.astype(jnp.float32), axis=0)
-    small = total[24:32] + total[32:]
-    total = gather(jnp.concatenate([total[:24].astype(jnp.bfloat16), two(small)], axis=0), ROWS)
+    small = two(total[48:64] + total[64:])
+    total = gather(jnp.concatenate([total[:48].astype(jnp.bfloat16), small], axis=0), ROWS)
     total = total.astype(jnp.float32)
-    blocks = total[:, :24].reshape(2, 4, 24, 2, 384).transpose(3, 1, 2, 0, 4).reshape(2, 96, 768)
-    return blocks[0], blocks[1], (total[:, 24:32] + total[:, 32:]).reshape(-1, 768)
+    share = total[:, :48].reshape(2, 4, 48, 384).transpose(0, 2, 1, 3).reshape(96, 1536)
+    small = (total[:, 48:64] + total[:, 64:]).reshape(8, 2, 8, 384).transpose(0, 2, 1, 3)
+    return share, small.reshape(-1, 768)
 
 
 BLOCK = 384
@@ -139,7 +119,7 @@
 
 
 def mlp_kernel(
-    normed, scaled, w1, q0, q1, q2, q3, b1, d_w1, m0, m1, m2, m3, own, peer, d_b1, row, sums
+    place, normed, scaled, w1, w2, b1, first, m0, m1, m2, m3, own, peer, d_b1, row, sums
 ):
     @pl.when(pl.program_id(0) == 0)
     def _():
@@ -147,29 +127,39 @@
         row[...] = jnp.zeros_like(row)
 
     n, s = normed[...], scaled[...]
-    high, wide = q0.shape
-    w2 = jnp.concatenate(
-        [
-            jnp.concatenate([q0[...], q2[...]], axis=1),
-            jnp.concatenate([q1[...], q3[...]], axis=1),
-        ],
-        axis=0,
-    )
+    step = pl.program_id(0)
     preact = lax.dot_general(w1[...], n, NT, preferred_element_type=jnp.float32) + b1[:, :1]
     cdf = 0.5 * (1.0 + lax.erf(preact * INV_ROOT_TWO))
     hidden = (preact * cdf).astype(jnp.bfloat16)
     slope = cdf + preact * jnp.exp(-0.5 * preact * preact) * INV_ROOT_TWO_PI
-    grad_hidden = lax.dot_general(w2, s, NT, preferred_element_type=jnp.float32)
+    grad_hidden = lax.dot_general(w2[...], s, NT, preferred_element_type=jnp.float32)
     grad_preact = (grad_hidden * slope).astype(jnp.bfloat16)
-    d_w1[...] = lax.dot_general(grad_preact, n, NN, preferred_element_type=jnp.float32).astype(
-        jnp.bfloat16
-    )
     moment = lax.dot_general(hidden, s, NN, preferred_element_type=jnp.float32)
-    m0[...] = moment[:high, :wide].astype(jnp.bfloat16)
-    m1[...] = moment[high:, :wide].astype(jnp.bfloat16)
-    m2[...] = moment[:high, wide:].astype(jnp.bfloat16)
-    m3[...] = moment[high:, wide:].astype(jnp.bfloat16)
-    row[...] += jnp.sum(moment * w2.astype(jnp.float32), axis=0, keepdims=True)
+    d_w1 = lax.dot_general(grad_preact, n, NN, preferred_element_type=jnp.float32)
+    quarters = [
+        half[:, at : at + 384].astype(jnp.bfloat16) for half in (d_w1, moment) for at in (0, 384)
+    ]
+
+    for y_lo in range(2):
+
+        @pl.when(step == 2 * y_lo)
+        def _():
+            for x in range(4):
+                first[x, y_lo * BLOCK : (y_lo + 1) * BLOCK] = quarters[x]
+
+    for y_hi in range(2):
+        m = ((step // 2) ^ place[0]) + 2 * (y_hi ^ place[1])
+        for k, part in enumerate((m0, m1, m2, m3)):
+
+            @pl.when((step % 2 == 1) & (m == k))
+            def _():
+                for x in range(4):
+                    for z in range(4):
+                        at = x * 192 + z * 48
+                        rows = quarters[x][z * 96 + y_hi * 48 : z * 96 + y_hi * 48 + 48]
+                        part[at : at + 48] = rows
+
+    row[...] += jnp.sum(moment * w2[...].astype(jnp.float32), axis=0, keepdims=True)
     d_b1[...] = jnp.broadcast_to(
         jnp.sum(grad_preact.astype(jnp.float32), axis=1, keepdims=True), d_b1.shape
     )
@@ -182,20 +172,37 @@
         peer[...] = sums[half:].astype(jnp.bfloat16)
 
 
-def mlp(normed, scaled, w1, parts, b1):
+def mlp(normed, scaled, weights, b1):
     pixels, chans = normed.shape
-    hid = w1.shape[0]
+    hid = weights.shape[0]
+    place = jnp.stack([lax.axis_index("y_lo"), lax.axis_index("y_hi")]).astype(jnp.int32)
     whole = pl.BlockSpec((pixels, chans), lambda i: (0, 0))
     half = pl.BlockSpec((pixels // 2, chans), lambda i: (0, 0))
-    block = pl.BlockSpec((BLOCK, chans), lambda i: (i, 0))
-    part = pl.BlockSpec((BLOCK // 2, chans // 2), lambda i: (i, 0))
+    part = pl.BlockSpec((hid // 2, chans // 2), lambda i: (0, 0))
     lane = pl.BlockSpec((BLOCK, LANES), lambda i: (i, 0))
     return pl.pallas_call(
         mlp_kernel,
         grid=(hid // BLOCK,),
-        in_specs=[whole, whole, block] + [part] * 4 + [lane],
-        out_specs=[block] + [part] * 4 + [half, half, lane, pl.BlockSpec((1, chans), lambda i: (0, 0))],
-        out_shape=[jax.ShapeDtypeStruct((hid, chans), jnp.bfloat16)]
+        in_specs=[
+            pl.BlockSpec(memory_space=pltpu.SMEM),
+            whole,
+            whole,
+            pl.BlockSpec((BLOCK, chans), lambda i: (i, 0)),
+            pl.BlockSpec((BLOCK, chans), lambda i: (i, 1)),
+            lane,
+        ],
+        out_specs=[
+            pl.BlockSpec((4, hid // 2, chans // 2), lambda i: (0, 0, 0)),
+            part,
+            part,
+            part,
+            part,
+            half,
+            half,
+            lane,
+            pl.BlockSpec((1, chans), lambda i: (0, 0)),
+        ],
+        out_shape=[jax.ShapeDtypeStruct((4, hid // 2, chans // 2), jnp.bfloat16)]
         + [jax.ShapeDtypeStruct((hid // 2, chans // 2), jnp.bfloat16)] * 4
         + [
             jax.ShapeDtypeStruct((pixels // 2, chans), jnp.float32),
@@ -208,7 +215,7 @@
         cost_estimate=pl.CostEstimate(
             flops=10 * pixels * hid * chans, bytes_accessed=2**24, transcendentals=2 * pixels * hid
         ),
-    )(normed, scaled, w1, *parts, jnp.broadcast_to(b1[:, None], (hid, LANES)))
+    )(place, normed, scaled, weights, weights, jnp.broadcast_to(b1[:, None], (hid, LANES)))
 
 
 def transposed_kernel(padded, cotangent, kernel, d_input, wide):
@@ -314,15 +321,8 @@
     pixels = images * rows_here * cols
     flat_cot = cotangent.reshape(pixels, chans).astype(jnp.float32)
     scaled = (flat_cot * gamma).astype(jnp.bfloat16)
-    along_z = gather_z(w1.T, w2, b1)
-    maps, along_z = lax.optimization_barrier((block_input, along_z))
-    w2_part = gather(along_z[:, 24:48].reshape(192, 384), "x").reshape(768, 384)
-    w1_h = gather_w1(along_z)
-    b1_h = gather_b1(along_z)
-    padded, w2_part = lax.optimization_barrier((halo(maps), w2_part))
-    padded = pad_columns(padded)
-    w2_parts = gather_w2(w2_part)
-    scaled = relative(scaled)
+    weights, b1_h = gather_weights(w1.T, w2, b1)
+    padded = pad_columns(halo(block_input))
     scaled2 = jnp.concatenate([scaled, swap(scaled)], axis=0)
     conv = depthwise(padded, dw_kernel, rows_here, cols) + dw_bias
     center = conv - jnp.mean(conv, axis=-1, keepdims=True)
@@ -330,13 +330,11 @@
     rstd = lax.rsqrt(spread + EPSILON).reshape(pixels, 1)
     norm = center.reshape(pixels, chans) * rstd
     normed = (norm * ln_gain + ln_bias).astype(jnp.bfloat16)
-    normed = relative(normed)
     normed2 = jnp.concatenate([normed, swap(normed)], axis=0)
 
-    d_w1, *parts, own, peer, sums_b1, moment_row = mlp(normed2, scaled2, w1_h, w2_parts, b1_h)
-    first, second = scatter_terms(d_w1, parts)
-    grad_normed = relative(own + swap(peer).astype(jnp.float32))
-    moment_row = relative(moment_row)
+    first, *parts, own, peer, sums_b1, moment_row = mlp(normed2, scaled2, weights, b1_h)
+    first, second = scatter_terms(first, parts)
+    grad_normed = own + swap(peer).astype(jnp.float32)
 
     weighted = grad_normed * ln_gain
     grad_conv = (
@@ -355,7 +353,7 @@
     cot_sums = jnp.sum(flat_cot, axis=0)
     core = lax.axis_index("core")
     y_lo = lax.axis_index("y_lo")
-    sums_b1 = jnp.roll(sums_b1[:, 0].reshape(4, 2, 8, 24), y_lo, 1).reshape(1, -1)
+    sums_b1 = sums_b1[:, 0][None]
     pair_b1 = jnp.where(core == jnp.arange(2)[:, None], sums_b1, 0.0)
     local_small = jnp.concatenate(
         [
@@ -370,13 +368,14 @@
         ],
         axis=0,
     )
-    d_w1, d_w2, total_small = finish(first, second, local_small)
+    share, total_small = finish(first, second, local_small)
     factor = 1.0 / math.sqrt(pixels * 256)
     param_grads = total_small[:54] * factor
-    sums = total_small[54:58].reshape(2, 4, 2, 8, 24)
-    mine = (core, 0, y_lo, lax.axis_index("z"), 0)
-    d_b1 = lax.dynamic_slice(sums, mine, (1, 4, 1, 1, 24)).reshape(shard) * factor
-    d_w1, d_w2 = (d_w1 * factor).T, d_w2 * factor
+    at = (y_lo * 8 + lax.axis_index("z")) * shard
+    sums = total_small[54:58].reshape(2, -1)
+    d_b1 = lax.dynamic_slice(sums, (core, at), (1, shard)).reshape(shard) * factor
+    share = share * factor
+    d_w1, d_w2 = share[:, :chans].T, share[:, chans:]
     return (d_input.reshape(block_input.shape), d_w1, d_b1, d_w2, param_grads)
 
 

time: 254 us -> 248 us (0.976)
  waiting for transfers between devices: 36.4 us -> 61.9 us
  starting transfers between devices: 81 us -> 64.5 us
  local copies, waits for them, and re-layouts: 32.1 us -> 15.9 us
  between operations: 1.29 us -> 14.6 us
  blocking collectives: 12.3 us -> 0 us
  other arithmetic: 45.5 us -> 41.6 us
  Pallas kernels: 43.7 us -> 46.5 us
    all_gather x0 -> x1, waiting for transfers between devices: none -> 34.2 us  [gather_weights(): lax.all_gather(jnp.concatenate([w1_t, w2], axis=1), PAIRS, axis=0, tiled=...]
    ppermute x15 -> x7, starting transfers between devices: 21.7 us -> 6.39 us  [across(): return lax.ppermute(cells, Y, [(i, i ^ flip) for i in range(4)])]
    all_to_all x4 -> x2, starting transfers between devices: 31.8 us -> 18.4 us  [gather(): lax.all_to_all(jnp.broadcast_to(part[None], (count,) + part.shape), axes,...]
    all_to_all x1 -> x0, blocking collectives: 12.3 us -> none  [spread_sum(): pieces = lax.all_to_all(pieces, axes, 0, 0)]
    all_to_all x0 -> x1, starting transfers between devices: none -> 11.3 us  [scatter_terms(): lax.all_to_all(first, 'x', 0, 0).astype(jnp.float32)]
    all_to_all x4 -> x2, waiting for transfers between devices: 9.7 us -> 0.01 us  [gather(): lax.all_to_all(jnp.broadcast_to(part[None], (count,) + part.shape), axes,...]
    all_to_all x2, waiting for transfers between devices: 0.01 us -> 7.24 us  [spread_sum(): pieces = lax.all_to_all(pieces, axes, 0, 0)]
    ppermute x15 -> x7, waiting for transfers between devices: 18.5 us -> 12.5 us  [across(): return lax.ppermute(cells, Y, [(i, i ^ flip) for i in range(4)])]
  transfers between devices with their start and end apart: 31 -> 23, of which waited for: 10 -> 7; matrix products, arithmetic and copies ran while one was open for 26% -> 20% of each run, Pallas kernels for 8% -> 9%
where the time goes in v2:
time: 248 us; the launch traced here: 245 us
  starting transfers between devices  64.5 us (26%)
  waiting for transfers between devices  61.9 us (25%)
  Pallas kernels  46.5 us (19%)
  other arithmetic  41.6 us (17%)
  local copies, waits for them, and re-layouts  15.9 us (6%)
  between operations  14.6 us (6%)
    all_gather x1, waiting for transfers between devices, gather_weights(): lax.all_gather(jnp.concatenate([w1_t, w2], axis=1), PAIRS, axis=0, tiled=...  34.2 us
    pallas_call x1, Pallas kernels, mlp(): pl.pallas_call(mlp_kernel, grid=(hid // BLOCK,), in_specs=[pl.BlockSpec(m...  25.5 us
    all_to_all x2, starting transfers between devices, gather(): lax.all_to_all(jnp.broadcast_to(part[None], (count,) + part.shape), axes,...  18.4 us
    reduce_sum x1, other arithmetic, shards(): center = conv - jnp.mean(conv, axis=-1, keepdims=True)  13.4 us
    ppermute x7, waiting for transfers between devices, across(): return lax.ppermute(cells, Y, [(i, i ^ flip) for i in range(4)])  12.5 us
    all_to_all x1, starting transfers between devices, scatter_terms(): lax.all_to_all(first, 'x', 0, 0).astype(jnp.float32)  11.3 us
    all_to_all x2, starting transfers between devices, spread_sum(): pieces = lax.all_to_all(pieces, axes, 0, 0)  11.2 us
    pallas_call x1, Pallas kernels, tap_sums(): pl.pallas_call(taps_kernel, grid=(chans // LANES, images), in_specs=[pl.B...  10.7 us
  transfers between devices with their start and end apart: 23, of which 7 were waited for; matrix products, arithmetic and copies ran while one was open for 20% of the time, Pallas kernels for 9%

profile of v2, /device:TPU:2, one launch (start us, length us, event | category | flops | bytes accessed | tf_op | source)
XLA Modules:
  0.0 245.0 jit_solution(47659161701642265)
XLA Ops:
  10.3 4.3 %collective-permute-start.1 = (bf16[2,3,48,768]{3,2,1,0:T(8,128)(2,1)S(1)}, bf16[2,3,48,768]{3,2,1,0:T(8,128)(2,1)S(1)}, u32[]{:S(2)}, u32[]{:S(2)}) collective-permute-start(bf16[2,3,48,768]{3,2,1,0:T(8,128)(2,1)S(1)} %get-tuple-element.99), channel_id=1, source_target_pairs={{1,0},{2,1},{3,2},{4,3},{5,4},{6,5},{7,6},{9,8},{10,9},{11,10},{12... | collective-permute-start | bytes 1327112 | tf_op jit(solution)/shard_map/ppermute | solution.py:29
  18.3 9.4 %all-to-all-start = ((f32[16,1,96]{2,1,0:T(1,128)}), f32[16,1,96]{2,1,0:T(1,128)}, u32[]{:S(2)}, u32[]{:S(2)}) async-start(f32[16,1,96]{2,1,0:T(1,128)} %broadcast_in_dim.84), calls=%async_computation | async-start | bytes 16384 | tf_op jit(solution)/shard_map/all_to_all | solution.py:46
  32.9 13.4 %fusion.12 = (f32[2,6,48]{2,1,0:T(8,128)S(1)}, f32[2,6,48,768]{3,2,1,0:T(8,128)S(1)}) fusion(f32[768]{0:T(1024)S(1)} %copy-done.11, f32[768]{0:T(1024)S(1)} %get-tuple-element.85, bf16[2,12,56,768]{3,2,1,0:T(8,128)(2,1)S(1)} %fusion.5.padded, f32[768]{0:T(1024)S(1)} %get-tuple-element.38, f32[768]{0:T(1024)S(1)} %get-tuple-element.39, ...), kind=kLoop, calls=%fused_computation.122 | loop fusion | flops 65469888 | bytes 45277440 | tf_op jit(solution)/shard_map/reduce_sum | solution.py:328
  51.4 2.8 %pad_maximum_fusion.1.scaled = bf16[1152,768]{1,0:T(8,128)(2,1)} fusion(bf16[576,768]{1,0:T(8,128)(2,1)} %collective-permute-done.3, bf16[576,768]{1,0:T(8,128)(2,1)} %fusion.6), kind=kLoop, calls=%fused_computation.11 | loop fusion | flops 3538944 | bytes 3538944 | tf_op jit(solution)/shard_map/concatenate | solution.py:326
  54.1 2.5 %pad_maximum_fusion.normed = bf16[1152,768]{1,0:T(8,128)(2,1)} fusion(bf16[576,768]{1,0:T(8,128)(2,1)S(1)} %collective-permute-done.2, bf16[576,768]{1,0:T(8,128)(2,1)} %get-tuple-element.88), kind=kLoop, calls=%fused_computation.10 | loop fusion | flops 3538944 | bytes 3538944 | tf_op jit(solution)/shard_map/concatenate | solution.py:333
  56.7 34.2 %all-gather.2.cloned.1.call-done.w1.w2 = bf16[1536,1536]{1,0:T(8,128)(2,1)} async-done(((bf16[96,1536]{1,0:T(8,128)(2,1)}), bf16[1536,1536]{1,0:T(8,128)(2,1)}) %all-gather.2.cloned.1.call-update) | async-done | bytes 4718608 | tf_op jit(solution)/shard_map/all_gather | solution.py:55
  92.1 25.5 %shard_map.146 = (bf16[4,768,384]{2,1,0:T(8,128)(2,1)}, bf16[768,384]{1,0:T(8,128)(2,1)}, bf16[768,384]{1,0:T(8,128)(2,1)}, bf16[768,384]{1,0:T(8,128)(2,1)}, bf...) custom-call(s32[2]{0:T(128)} %pad_add_fusion.place, ...), custom_call_target="tpu_custom_call" | custom-call | flops 13589544960 | bytes 16777216 | tf_op jit(solution)/shard_map/pallas_call | solution.py:183
  117.7 11.3 %all-to-all-start.1 = ((bf16[4,768,384]{2,1,0:T(8,128)(2,1)}), bf16[4,768,384]{2,1,0:T(8,128)(2,1)}, u32[]{:S(2)}, u32[]{:S(2)}) async-start(bf16[4,768,384]{2,1,0:T(8,128)(2,1)} %get-tuple-element.21), calls=%async_computation.1 | async-start | bytes 4718592 | tf_op jit(solution)/shard_map/all_to_all | solution.py:73
  134.3 5.9 %collective-permute-done.9 = bf16[384,384]{1,0:T(8,128)(2,1)} collective-permute-done((bf16[384,384]{1,0:T(8,128)(2,1)}, bf16[384,384]{1,0:T(8,128)(2,1)}, u32[]{:S(2)}, u32[]{:S(2)}) %collective-permute-start.9) | collective-permute-done | bytes 294944 | tf_op jit(solution)/shard_map/ppermute | solution.py:51
  146.7 10.7 %shard_map.148 = f32[49,768]{1,0:T(8,128)} custom-call(bf16[2,12,56,768]{3,2,1,0:T(8,128)(2,1)} %copy-done, bf16[2,6,48,768]{3,2,1,0:T(8,128)(2,1)} %bitcast.36), custom_call_target="tpu_custom_call" | custom-call | flops 10000000000 | bytes 4194304 | tf_op jit(solution)/shard_map/pallas_call | solution.py:285
  158.8 2.3 add_convert_fusion.1
  162.2 2.3 reduce_sum.115
  164.6 4.8 %all-to-all-start.2 = ((bf16[4,192,384]{2,1,0:T(8,128)(2,1)}), bf16[4,192,384]{2,1,0:T(8,128)(2,1)S(1)}, u32[]{:S(2)}, u32[]{:S(2)}) async-start(bf16[4,192,384]{2,1,0:T(8,128)(2,1)} %bitcast.11), calls=%async_computation.2 | async-start | bytes 1179648 | tf_op jit(solution)/shard_map/all_to_all | solution.py:40
  169.4 3.3 %collective-permute-start.13 = (bf16[192,384]{1,0:T(8,128)(2,1)S(1)}, bf16[192,384]{1,0:T(8,128)(2,1)S(1)}, u32[]{:S(2)}, u32[]{:S(2)}) collective-permute-start(bf16[192,384]{1,0:T(8,128)(2,1)S(1)} %bitcast.48), channel_id=1, source_target_pairs={{0,132},{4,128},{128,4},{132,0},{1,133},{5,129},{129,5},{133,1},{2... | collective-permute-start | bytes 442376 | tf_op jit(solution)/shard_map/ppermute | solution.py:51
  174.4 4.4 %collective-permute-done.13 = bf16[192,384]{1,0:T(8,128)(2,1)S(1)} collective-permute-done((bf16[192,384]{1,0:T(8,128)(2,1)S(1)}, bf16[192,384]{1,0:T(8,128)(2,1)S(1)}, u32[]{:S(2)}, u32[]{:S(2)}) %collective-permute-start.13) | collective-permute-done | bytes 147488 | tf_op jit(solution)/shard_map/ppermute | solution.py:51
  181.2 6.4 %all-to-all-start.3 = ((f32[8,8,768]{2,1,0:T(8,128)}), f32[8,8,768]{2,1,0:T(8,128)S(1)}, u32[]{:S(2)}, u32[]{:S(2)}) async-start(f32[8,8,768]{2,1,0:T(8,128)} %bitcast.13), calls=%async_computation.3 | async-start | bytes 393216 | tf_op jit(solution)/shard_map/all_to_all | solution.py:40
  187.6 7.2 %all-to-all-done.3 = f32[8,8,768]{2,1,0:T(8,128)S(1)} async-done(((f32[8,8,768]{2,1,0:T(8,128)}), f32[8,8,768]{2,1,0:T(8,128)S(1)}, u32[]{:S(2)}, u32[]{:S(2)}) %all-to-all-start.3) | async-done | bytes 196640 | tf_op jit(solution)/shard_map/all_to_all | solution.py:40
  195.8 3.5 %all-to-all-start.4 = ((bf16[8,80,384]{2,1,0:T(8,128)(2,1)}), bf16[8,80,384]{2,1,0:T(8,128)(2,1)S(1)}, u32[]{:S(2)}, u32[]{:S(2)}) async-start(bf16[8,80,384]{2,1,0:T(8,128)(2,1)} %pad_maximum_fusion.4), calls=%async_computation.4 | async-start | bytes 983040 | tf_op jit(solution)/shard_map/all_to_all | solution.py:103
  199.3 3.1 %collective-permute-start.6 = (bf16[2,3,48,768]{3,2,1,0:T(8,128)(2,1)S(1)}, bf16[2,3,48,768]{3,2,1,0:T(8,128)(2,1)S(1)}, u32[]{:S(2)}, u32[]{:S(2)}) collective-permute-start(bf16[2,3,48,768]{3,2,1,0:T(8,128)(2,1)S(1)} %get-tuple-element.95), channel_id=1, source_target_pairs={{1,0},{2,1},{3,2},{4,3},{5,4},{6,5},{7,6},{9,8},{10,9},{11,10},{12... | collective-permute-start | bytes 1327112 | tf_op jit(solution)/shard_map/ppermute | solution.py:29
  202.4 2.8 %collective-permute-start.5 = (bf16[2,3,48,768]{3,2,1,0:T(8,128)(2,1)S(1)}, bf16[2,3,48,768]{3,2,1,0:T(8,128)(2,1)S(1)}, u32[]{:S(2)}, u32[]{:S(2)}) collective-permute-start(bf16[2,3,48,768]{3,2,1,0:T(8,128)(2,1)S(1)} %get-tuple-element.94), channel_id=1, source_target_pairs={{0,1},{1,2},{2,3},{3,4},{4,5},{5,6},{6,7},{8,9},{9,10},{10,11},{11... | collective-permute-start | bytes 1327112 | tf_op jit(solution)/shard_map/ppermute | solution.py:28
  205.2 5.0 %collective-permute-done.6 = bf16[2,3,48,768]{3,2,1,0:T(8,128)(2,1)S(1)} collective-permute-done((bf16[2,3,48,768]{3,2,1,0:T(8,128)(2,1)S(1)}, bf16[2,3,48,768]{3,2,1,0:T(8,128)(2,1)S(1)}, u32[]{:S(2)}, u32[]{:S(2)}) %collective-permute-start.6) | collective-permute-done | bytes 442400 | tf_op jit(solution)/shard_map/ppermute | solution.py:29
  210.2 2.9 %collective-permute-done.5 = bf16[2,3,48,768]{3,2,1,0:T(8,128)(2,1)S(1)} collective-permute-done((bf16[2,3,48,768]{3,2,1,0:T(8,128)(2,1)S(1)}, bf16[2,3,48,768]{3,2,1,0:T(8,128)(2,1)S(1)}, u32[]{:S(2)}, u32[]{:S(2)}) %collective-permute-start.5) | collective-permute-done | bytes 442400 | tf_op jit(solution)/shard_map/ppermute | solution.py:28
  216.2 9.0 %all-to-all-start.5 = ((bf16[8,80,384]{2,1,0:T(8,128)(2,1)}), bf16[8,80,384]{2,1,0:T(8,128)(2,1)S(1)}, u32[]{:S(2)}, u32[]{:S(2)}) async-start(bf16[8,80,384]{2,1,0:T(8,128)(2,1)} %broadcast_in_dim.102), calls=%async_computation.5 | async-start | bytes 983040 | tf_op jit(solution)/shard_map/all_to_all | solution.py:46
  225.2 10.3 %shard_map.147 = bf16[2,6,48,768]{3,2,1,0:T(8,128)(2,1)} custom-call(bf16[2,12,56,768]{3,2,1,0:T(8,128)(2,1)} %select_maximum_fusion.padded, bf16[2,6,48,768]{3,2,1,0:T(8,128)(2,1)} %cotangent.1, f32[49,768]{1,0:T(8,128)} %kernel.1), custom_call_target="tpu_custom_call" | custom-call | flops 10000000000 | bytes 4194304 | tf_op jit(solution)/shard_map/pallas_call | solution.py:241
  (140 shorter events, 43.2 us)
Async XLA Ops:
  7.2 83.7 %all-gather.2.cloned.1.call-start = ((), (), s32[]{:S(2)}) async-start(), calls=%async_computation.6 | async-start | bytes 5013504 | tf_op jit(solution)/shard_map/all_gather | solution.py:55
  10.3 21.5 %copy-start.1 = (bf16[2,6,48,768]{3,2,1,0:T(8,128)(2,1)S(1)}, bf16[2,6,48,768]{3,2,1,0:T(8,128)(2,1)}, u32[]{:S(2)}) copy-start(bf16[2,6,48,768]{3,2,1,0:T(8,128)(2,1)} %param.11) | copy-start | bytes 2654212
  10.3 21.6 %collective-permute-start.1 = (bf16[2,3,48,768]{3,2,1,0:T(8,128)(2,1)S(1)}, bf16[2,3,48,768]{3,2,1,0:T(8,128)(2,1)S(1)}, u32[]{:S(2)}, u32[]{:S(2)}) collective-permute-start(bf16[2,3,48,768]{3,2,1,0:T(8,128)(2,1)S(1)} %get-tuple-element.99), channel_id=1, source_target_pairs={{1,0},{2,1},{3,2},{4,3},{5,4},{6,5},{7,6},{9,8},{10,9},{11,10},{12... | collective-permute-start | bytes 1327112 | tf_op jit(solution)/shard_map/ppermute | solution.py:29
  14.6 17.1 %collective-permute-start = (bf16[2,3,48,768]{3,2,1,0:T(8,128)(2,1)S(1)}, bf16[2,3,48,768]{3,2,1,0:T(8,128)(2,1)S(1)}, u32[]{:S(2)}, u32[]{:S(2)}) collective-permute-start(bf16[2,3,48,768]{3,2,1,0:T(8,128)(2,1)S(1)} %get-tuple-element.98), channel_id=1, source_target_pairs={{0,1},{1,2},{2,3},{3,4},{4,5},{5,6},{6,7},{8,9},{9,10},{10,11},{11... | collective-permute-start | bytes 1327112 | tf_op jit(solution)/shard_map/ppermute | solution.py:28
  17.6 33.7 %collective-permute-start.3 = (bf16[576,768]{1,0:T(8,128)(2,1)}, bf16[576,768]{1,0:T(8,128)(2,1)}, u32[]{:S(2)}, u32[]{:S(2)}) collective-permute-start(bf16[576,768]{1,0:T(8,128)(2,1)} %fusion.6), channel_id=1, source_target_pairs={{0,8},{8,0},{1,9},{9,1},{2,10},{10,2},{3,11},{11,3},{4,12},{12,4},... | collective-permute-start | bytes 2654216 | tf_op jit(solution)/shard_map/ppermute | solution.py:34
  18.3 31.1 %all-to-all-start = ((f32[16,1,96]{2,1,0:T(1,128)}), f32[16,1,96]{2,1,0:T(1,128)}, u32[]{:S(2)}, u32[]{:S(2)}) async-start(f32[16,1,96]{2,1,0:T(1,128)} %broadcast_in_dim.84), calls=%async_computation | async-start | bytes 16384 | tf_op jit(solution)/shard_map/all_to_all | solution.py:46
  48.2 5.9 %collective-permute-start.2 = (bf16[576,768]{1,0:T(8,128)(2,1)}, bf16[576,768]{1,0:T(8,128)(2,1)S(1)}, u32[]{:S(2)}, u32[]{:S(2)}) collective-permute-start(bf16[576,768]{1,0:T(8,128)(2,1)} %get-tuple-element.88), channel_id=1, source_target_pairs={{0,8},{8,0},{1,9},{9,1},{2,10},{10,2},{3,11},{11,3},{4,12},{12,4},... | collective-permute-start | bytes 2654216 | tf_op jit(solution)/shard_map/ppermute | solution.py:34
  117.6 26.9 %collective-permute-start.4 = (bf16[576,768]{1,0:T(8,128)(2,1)}, bf16[576,768]{1,0:T(8,128)(2,1)S(1)}, u32[]{:S(2)}, u32[]{:S(2)}) collective-permute-start(bf16[576,768]{1,0:T(8,128)(2,1)} %get-tuple-element.20), channel_id=1, source_target_pairs={{0,8},{8,0},{1,9},{9,1},{2,10},{10,2},{3,11},{11,3},{4,12},{12,4},... | collective-permute-start | bytes 2654216 | tf_op jit(solution)/shard_map/ppermute | solution.py:34
  117.7 44.6 %all-to-all-start.1 = ((bf16[4,768,384]{2,1,0:T(8,128)(2,1)}), bf16[4,768,384]{2,1,0:T(8,128)(2,1)}, u32[]{:S(2)}, u32[]{:S(2)}) async-start(bf16[4,768,384]{2,1,0:T(8,128)(2,1)} %get-tuple-element.21), calls=%async_computation.1 | async-start | bytes 4718592 | tf_op jit(solution)/shard_map/all_to_all | solution.py:73
  130.8 9.4 %collective-permute-start.9 = (bf16[384,384]{1,0:T(8,128)(2,1)}, bf16[384,384]{1,0:T(8,128)(2,1)}, u32[]{:S(2)}, u32[]{:S(2)}) collective-permute-start(bf16[384,384]{1,0:T(8,128)(2,1)} %get-tuple-element.107), channel_id=1, source_target_pairs={{0,128},{4,132},{128,0},{132,4},{1,129},{5,133},{129,1},{133,5},{2... | collective-permute-start | bytes 884744 | tf_op jit(solution)/shard_map/ppermute | solution.py:51
  131.9 10.4 %collective-permute-start.7 = (bf16[384,384]{1,0:T(8,128)(2,1)}, bf16[384,384]{1,0:T(8,128)(2,1)}, u32[]{:S(2)}, u32[]{:S(2)}) collective-permute-start(bf16[384,384]{1,0:T(8,128)(2,1)} %get-tuple-element.106), channel_id=1, source_target_pairs={{0,132},{4,128},{128,4},{132,0},{1,133},{5,129},{129,5},{133,1},{2... | collective-permute-start | bytes 884744 | tf_op jit(solution)/shard_map/ppermute | solution.py:51
  142.3 16.5 %collective-permute-start.10 = (bf16[768,384]{1,0:T(8,128)(2,1)}, bf16[768,384]{1,0:T(8,128)(2,1)}, u32[]{:S(2)}, u32[]{:S(2)}) collective-permute-start(bf16[768,384]{1,0:T(8,128)(2,1)} %pad_maximum_fusion.3), channel_id=1, source_target_pairs={{0,132},{4,128},{128,4},{132,0},{1,133},{5,129},{129,5},{133,1},{2... | collective-permute-start | bytes 1769480 | tf_op jit(solution)/shard_map/ppermute | solution.py:51
  143.4 15.4 %collective-permute-start.8 = (bf16[768,384]{1,0:T(8,128)(2,1)S(1)}, bf16[768,384]{1,0:T(8,128)(2,1)}, u32[]{:S(2)}, u32[]{:S(2)}) collective-permute-start(bf16[768,384]{1,0:T(8,128)(2,1)S(1)} %pad_maximum_fusion.2), channel_id=1, source_target_pairs={{0,128},{4,132},{128,0},{132,4},{1,129},{5,133},{129,1},{133,5},{2... | collective-permute-start | bytes 1769480 | tf_op jit(solution)/shard_map/ppermute | solution.py:51
  158.5 2.6 %collective-permute-start.14 = (f32[64,768]{1,0:T(8,128)S(1)}, f32[64,768]{1,0:T(8,128)S(1)}, u32[]{:S(2)}, u32[]{:S(2)}) collective-permute-start(f32[64,768]{1,0:T(8,128)S(1)} %concatenate.71), channel_id=1, source_target_pairs={{0,8},{8,0},{1,9},{9,1},{2,10},{10,2},{3,11},{11,3},{4,12},{12,4},... | collective-permute-start | bytes 589832 | tf_op jit(solution)/shard_map/ppermute | solution.py:34
  161.1 12.6 %collective-permute-start.15 = (f32[64,768]{1,0:T(8,128)S(1)}, f32[64,768]{1,0:T(8,128)S(1)}, u32[]{:S(2)}, u32[]{:S(2)}) collective-permute-start(f32[64,768]{1,0:T(8,128)S(1)} %add.308), channel_id=1, source_target_pairs={{0,128},{128,0},{1,129},{129,1},{2,130},{130,2},{3,131},{131,3},{4... | collective-permute-start | bytes 589832 | tf_op jit(solution)/shard_map/ppermute | solution.py:97
  164.6 16.5 %all-to-all-start.2 = ((bf16[4,192,384]{2,1,0:T(8,128)(2,1)}), bf16[4,192,384]{2,1,0:T(8,128)(2,1)S(1)}, u32[]{:S(2)}, u32[]{:S(2)}) async-start(bf16[4,192,384]{2,1,0:T(8,128)(2,1)} %bitcast.11), calls=%async_computation.2 | async-start | bytes 1179648 | tf_op jit(solution)/shard_map/all_to_all | solution.py:40
  169.4 9.4 %collective-permute-start.13 = (bf16[192,384]{1,0:T(8,128)(2,1)S(1)}, bf16[192,384]{1,0:T(8,128)(2,1)S(1)}, u32[]{:S(2)}, u32[]{:S(2)}) collective-permute-start(bf16[192,384]{1,0:T(8,128)(2,1)S(1)} %bitcast.48), channel_id=1, source_target_pairs={{0,132},{4,128},{128,4},{132,0},{1,133},{5,129},{129,5},{133,1},{2... | collective-permute-start | bytes 442376 | tf_op jit(solution)/shard_map/ppermute | solution.py:51
  172.8 8.2 %collective-permute-start.12 = (bf16[192,384]{1,0:T(8,128)(2,1)S(1)}, bf16[192,384]{1,0:T(8,128)(2,1)S(1)}, u32[]{:S(2)}, u32[]{:S(2)}) collective-permute-start(bf16[192,384]{1,0:T(8,128)(2,1)S(1)} %bitcast.47), channel_id=1, source_target_pairs={{0,4},{4,0},{128,132},{132,128},{1,5},{5,1},{129,133},{133,129},{2... | collective-permute-start | bytes 442376 | tf_op jit(solution)/shard_map/ppermute | solution.py:51
  172.8 8.2 %collective-permute-start.11 = (bf16[192,384]{1,0:T(8,128)(2,1)S(1)}, bf16[192,384]{1,0:T(8,128)(2,1)S(1)}, u32[]{:S(2)}, u32[]{:S(2)}) collective-permute-start(bf16[192,384]{1,0:T(8,128)(2,1)S(1)} %bitcast.46), channel_id=1, source_target_pairs={{0,128},{4,132},{128,0},{132,4},{1,129},{5,133},{129,1},{133,5},{2... | collective-permute-start | bytes 442376 | tf_op jit(solution)/shard_map/ppermute | solution.py:51
  181.2 13.6 %all-to-all-start.3 = ((f32[8,8,768]{2,1,0:T(8,128)}), f32[8,8,768]{2,1,0:T(8,128)S(1)}, u32[]{:S(2)}, u32[]{:S(2)}) async-start(f32[8,8,768]{2,1,0:T(8,128)} %bitcast.13), calls=%async_computation.3 | async-start | bytes 393216 | tf_op jit(solution)/shard_map/all_to_all | solution.py:40
  195.8 19.5 %all-to-all-start.4 = ((bf16[8,80,384]{2,1,0:T(8,128)(2,1)}), bf16[8,80,384]{2,1,0:T(8,128)(2,1)S(1)}, u32[]{:S(2)}, u32[]{:S(2)}) async-start(bf16[8,80,384]{2,1,0:T(8,128)(2,1)} %pad_maximum_fusion.4), calls=%async_computation.4 | async-start | bytes 983040 | tf_op jit(solution)/shard_map/all_to_all | solution.py:103
  199.3 10.8 %collective-permute-start.6 = (bf16[2,3,48,768]{3,2,1,0:T(8,128)(2,1)S(1)}, bf16[2,3,48,768]{3,2,1,0:T(8,128)(2,1)S(1)}, u32[]{:S(2)}, u32[]{:S(2)}) collective-permute-start(bf16[2,3,48,768]{3,2,1,0:T(8,128)(2,1)S(1)} %get-tuple-element.95), channel_id=1, source_target_pairs={{1,0},{2,1},{3,2},{4,3},{5,4},{6,5},{7,6},{9,8},{10,9},{11,10},{12... | collective-permute-start | bytes 1327112 | tf_op jit(solution)/shard_map/ppermute | solution.py:29
  202.4 10.6 %collective-permute-start.5 = (bf16[2,3,48,768]{3,2,1,0:T(8,128)(2,1)S(1)}, bf16[2,3,48,768]{3,2,1,0:T(8,128)(2,1)S(1)}, u32[]{:S(2)}, u32[]{:S(2)}) collective-permute-start(bf16[2,3,48,768]{3,2,1,0:T(8,128)(2,1)S(1)} %get-tuple-element.94), channel_id=1, source_target_pairs={{0,1},{1,2},{2,3},{3,4},{4,5},{5,6},{6,7},{8,9},{9,10},{10,11},{11... | collective-permute-start | bytes 1327112 | tf_op jit(solution)/shard_map/ppermute | solution.py:28
  216.2 19.3 %all-to-all-start.5 = ((bf16[8,80,384]{2,1,0:T(8,128)(2,1)}), bf16[8,80,384]{2,1,0:T(8,128)(2,1)S(1)}, u32[]{:S(2)}, u32[]{:S(2)}) async-start(bf16[8,80,384]{2,1,0:T(8,128)(2,1)} %broadcast_in_dim.102), calls=%async_computation.5 | async-start | bytes 983040 | tf_op jit(solution)/shard_map/all_to_all | solution.py:46
  (15 other events, 109.2 us)
Sparse Core Ops, SparseCore 0:
  10.4 80.4 all-gather.1

commit v3 on v2

--- a/solution.py
+++ b/solution.py
@@ -58,18 +58,9 @@
 
 
 def scatter_terms(first, parts):
-    own, near, far, last = parts
-    half = far.shape[0] // 2
-    up = across(far[:half], 1).astype(jnp.float32)
-    down = across(far[half:], 3).astype(jnp.float32)
-    last = jnp.concatenate(
-        [(last[:half].astype(jnp.float32) + up).astype(jnp.bfloat16), last[half:]], axis=0
-    )
-    near = jnp.concatenate(
-        [near[:half], (near[half:].astype(jnp.float32) + down).astype(jnp.bfloat16)], axis=0
-    )
-    second = own.astype(jnp.float32)
-    second = second + across(near, 1).astype(jnp.float32) + across(last, 3).astype(jnp.float32)
+    second = parts[0].astype(jnp.float32)
+    for m in (1, 2, 3):
+        second = second + across(parts[m], m).astype(jnp.float32)
     first = jnp.sum(lax.all_to_all(first, "x", 0, 0).astype(jnp.float32), axis=0)
     first = first.astype(jnp.bfloat16).reshape(2, 4, 2, 48, 384)
     first, second = lax.optimization_barrier((first, second.astype(jnp.bfloat16)))
@@ -92,22 +83,35 @@
     return jnp.concatenate([high, cells - high], axis=0).astype(jnp.bfloat16)
 
 
-def finish(first, second, small):
+def spread_small(small):
+    x, y_hi = lax.axis_index("x"), lax.axis_index("y_hi")
     small = small + swap(small)
-    small = small + lax.ppermute(small, "y_lo", [(0, 1), (1, 0)])
-    first, second, small = lax.optimization_barrier((first, second, small))
-    small = spread_sum(small, ROWS)
+    small = small + across(small, 1)
+    mine = lax.dynamic_slice(small, (y_hi * 32, 0), (32, 768))
+    small = mine + across(lax.dynamic_slice(small, ((1 - y_hi) * 32, 0), (32, 768)), 2)
+    total = lax.dynamic_slice(small, (x * 8, 0), (8, 768))
+    for k in (1, 2, 3):
+        sent = lax.dynamic_slice(small, ((x + k) % 4 * 8, 0), (8, 768))
+        total = total + lax.ppermute(sent, "x", [(i, (i + k) % 4) for i in range(4)])
+    return total
+
+
+def finish(first, second, small, beside):
+    small = spread_small(small)
+    work, cells = beside
+    cells, first, second, small = lax.optimization_barrier((cells, first, second, small))
     small = two(jnp.concatenate([small[:, :384], small[:, 384:]], axis=0))
     terms = jnp.concatenate([first, second], axis=0).astype(jnp.bfloat16).reshape(8, 48, 384)
     small = jnp.broadcast_to(small[None], (8,) + small.shape)
     pieces = lax.all_to_all(jnp.concatenate([terms, small], axis=1), "z", 0, 0)
+    pieces, done = lax.optimization_barrier((pieces, work(cells)))
     total = jnp.sum(pieces.astype(jnp.float32), axis=0)
     small = two(total[48:64] + total[64:])
     total = gather(jnp.concatenate([total[:48].astype(jnp.bfloat16), small], axis=0), ROWS)
     total = total.astype(jnp.float32)
     share = total[:, :48].reshape(2, 4, 48, 384).transpose(0, 2, 1, 3).reshape(96, 1536)
     small = (total[:, 48:64] + total[:, 64:]).reshape(8, 2, 8, 384).transpose(0, 2, 1, 3)
-    return share, small.reshape(-1, 768)
+    return share, small.reshape(-1, 768), done
 
 
 BLOCK = 384
@@ -347,7 +351,6 @@
     ).astype(jnp.bfloat16)
     grad_maps = grad_conv.reshape(block_input.shape)
     grad_padded = pad_columns(halo(grad_maps))
-    d_input = transposed(grad_padded, cotangent, dw_kernel)
 
     grad_wide = grad_maps.astype(jnp.float32)
     cot_sums = jnp.sum(flat_cot, axis=0)
@@ -368,7 +371,9 @@
         ],
         axis=0,
     )
-    share, total_small = finish(first, second, local_small)
+    share, total_small, d_input = finish(
+        first, second, local_small, (lambda g: transposed(g, cotangent, dw_kernel), grad_padded)
+    )
     factor = 1.0 / math.sqrt(pixels * 256)
     param_grads = total_small[:54] * factor
     at = (y_lo * 8 + lax.axis_index("z")) * shard

time: 248 us -> 251 us (1.012)
  starting transfers between devices: 64.5 us -> 70.4 us
  other arithmetic: 41.6 us -> 44.4 us
  local copies, waits for them, and re-layouts: 15.9 us -> 13.2 us
    all_to_all x2, waiting for transfers between devices: 0.01 us -> 15.3 us  [gather(): lax.all_to_all(jnp.broadcast_to(part[None], (count,) + part.shape), axes,...]
    all_gather x1, waiting for transfers between devices: 34.2 us -> 22.8 us  [gather_weights(): lax.all_gather(jnp.concatenate([w1_t, w2], axis=1), PAIRS, axis=0, tiled=...]
    ppermute x1 -> x3, starting transfers between devices: 1.1 us -> 11 us  [spread_small(): lax.ppermute(sent, 'x', [(i, (i + k) % 4) for i in range(4)])]
    ppermute x2, waiting for transfers between devices: 2.87 us -> 8.91 us  [halo(): above = lax.ppermute(cells[:, -MARGIN:], ROWS, down)]
    ppermute x7 -> x8, starting transfers between devices: 6.39 us -> 12 us  [across(): return lax.ppermute(cells, Y, [(i, i ^ flip) for i in range(4)])]
    all_to_all x2 -> x1, waiting for transfers between devices: 7.24 us -> 1.73 us  [spread_sum(): pieces = lax.all_to_all(pieces, axes, 0, 0)]
    all_to_all x2 -> x1, starting transfers between devices: 11.2 us -> 5.86 us  [spread_sum(): pieces = lax.all_to_all(pieces, axes, 0, 0)]
    ppermute x2, waiting for transfers between devices: 4.95 us -> 0.01 us  [halo(): below = lax.ppermute(cells[:, :MARGIN], ROWS, up)]
  transfers between devices with their start and end apart: 23 -> 25, of which waited for: 7 -> 10; matrix products, arithmetic and copies ran while one was open for 20% -> 20% of each run, Pallas kernels for 9% -> 8%
where the time goes in v3:
time: 251 us; the launch traced here: 250 us
  starting transfers between devices  70.4 us (28%)
  waiting for transfers between devices  60.7 us (24%)
  Pallas kernels  46.5 us (19%)
  other arithmetic  44.4 us (18%)
  between operations  14.7 us (6%)
  local copies, waits for them, and re-layouts  13.2 us (5%)
    pallas_call x1, Pallas kernels, mlp(): pl.pallas_call(mlp_kernel, grid=(hid // BLOCK,), in_specs=[pl.BlockSpec(m...  25.5 us
    all_gather x1, waiting for transfers between devices, gather_weights(): lax.all_gather(jnp.concatenate([w1_t, w2], axis=1), PAIRS, axis=0, tiled=...  22.8 us
    all_to_all x2, waiting for transfers between devices, gather(): lax.all_to_all(jnp.broadcast_to(part[None], (count,) + part.shape), axes,...  15.3 us
    all_to_all x2, starting transfers between devices, gather(): lax.all_to_all(jnp.broadcast_to(part[None], (count,) + part.shape), axes,...  14.7 us
    reduce_sum x1, other arithmetic, shards(): center = conv - jnp.mean(conv, axis=-1, keepdims=True)  13.3 us
    ppermute x8, starting transfers between devices, across(): return lax.ppermute(cells, Y, [(i, i ^ flip) for i in range(4)])  12 us
    all_to_all x1, starting transfers between devices, scatter_terms(): lax.all_to_all(first, 'x', 0, 0).astype(jnp.float32)  11.1 us
    ppermute x3, starting transfers between devices, spread_small(): lax.ppermute(sent, 'x', [(i, (i + k) % 4) for i in range(4)])  11 us
  transfers between devices with their start and end apart: 25, of which 10 were waited for; matrix products, arithmetic and copies ran while one was open for 20% of the time, Pallas kernels for 8%

profile of v3, /device:TPU:2, one launch (start us, length us, event | category | flops | bytes accessed | tf_op | source)
XLA Modules:
  0.0 249.9 jit_solution(8149117316875374830)
XLA Ops:
  10.3 4.3 %collective-permute-start.1 = (bf16[2,3,48,768]{3,2,1,0:T(8,128)(2,1)S(1)}, bf16[2,3,48,768]{3,2,1,0:T(8,128)(2,1)S(1)}, u32[]{:S(2)}, u32[]{:S(2)}) collective-permute-start(bf16[2,3,48,768]{3,2,1,0:T(8,128)(2,1)S(1)} %get-tuple-element.105), channel_id=1, source_target_pairs={{1,0},{2,1},{3,2},{4,3},{5,4},{6,5},{7,6},{9,8},{10,9},{11,10},{12... | collective-permute-start | bytes 1327112 | tf_op jit(solution)/shard_map/ppermute | solution.py:29
  18.1 8.1 %collective-permute-done = bf16[2,3,48,768]{3,2,1,0:T(8,128)(2,1)S(1)} collective-permute-done((bf16[2,3,48,768]{3,2,1,0:T(8,128)(2,1)S(1)}, bf16[2,3,48,768]{3,2,1,0:T(8,128)(2,1)S(1)}, u32[]{:S(2)}, u32[]{:S(2)}) %collective-permute-start) | collective-permute-done | bytes 442400 | tf_op jit(solution)/shard_map/ppermute | solution.py:28
  27.4 13.3 %fusion.12 = (f32[2,6,48]{2,1,0:T(8,128)S(1)}, f32[2,6,48,768]{3,2,1,0:T(8,128)S(1)}) fusion(f32[768]{0:T(1024)S(1)} %copy-done.14, f32[768]{0:T(1024)S(1)} %get-tuple-element.91, bf16[2,12,56,768]{3,2,1,0:T(8,128)(2,1)S(1)} %fusion.5.padded, f32[768]{0:T(1024)S(1)} %get-tuple-element.44, f32[768]{0:T(1024)S(1)} %get-tuple-element.45, ...), kind=kLoop, calls=%fused_computation.124 | loop fusion | flops 65469888 | bytes 45277440 | tf_op jit(solution)/shard_map/reduce_sum | solution.py:332
  43.3 9.8 %all-to-all-start = ((f32[16,1,96]{2,1,0:T(1,128)}), f32[16,1,96]{2,1,0:T(1,128)S(1)}, u32[]{:S(2)}, u32[]{:S(2)}) async-start(f32[16,1,96]{2,1,0:T(1,128)} %broadcast_in_dim.84), calls=%async_computation | async-start | bytes 16384 | tf_op jit(solution)/shard_map/all_to_all | solution.py:46
  55.1 6.4 %all-to-all-done = f32[16,1,96]{2,1,0:T(1,128)S(1)} async-done(((f32[16,1,96]{2,1,0:T(1,128)}), f32[16,1,96]{2,1,0:T(1,128)S(1)}, u32[]{:S(2)}, u32[]{:S(2)}) %all-to-all-start) | async-done | bytes 6176 | tf_op jit(solution)/shard_map/all_to_all | solution.py:46
  62.8 2.8 %pad_maximum_fusion.1.scaled = bf16[1152,768]{1,0:T(8,128)(2,1)} fusion(bf16[576,768]{1,0:T(8,128)(2,1)} %collective-permute-done.3, bf16[576,768]{1,0:T(8,128)(2,1)} %fusion.6), kind=kLoop, calls=%fused_computation.11 | loop fusion | flops 3538944 | bytes 3538944 | tf_op jit(solution)/shard_map/concatenate | solution.py:330
  65.5 2.5 %pad_maximum_fusion.normed = bf16[1152,768]{1,0:T(8,128)(2,1)} fusion(bf16[576,768]{1,0:T(8,128)(2,1)S(1)} %collective-permute-done.2, bf16[576,768]{1,0:T(8,128)(2,1)} %get-tuple-element.94), kind=kLoop, calls=%fused_computation.10 | loop fusion | flops 3538944 | bytes 3538944 | tf_op jit(solution)/shard_map/concatenate | solution.py:337
  68.1 22.8 %all-gather.2.cloned.1.call-done.w1.w2 = bf16[1536,1536]{1,0:T(8,128)(2,1)} async-done(((bf16[96,1536]{1,0:T(8,128)(2,1)}), bf16[1536,1536]{1,0:T(8,128)(2,1)}) %all-gather.2.cloned.1.call-update) | async-done | bytes 4718608 | tf_op jit(solution)/shard_map/all_gather | solution.py:55
  92.0 25.5 %shard_map.146 = (bf16[4,768,384]{2,1,0:T(8,128)(2,1)}, bf16[768,384]{1,0:T(8,128)(2,1)}, bf16[768,384]{1,0:T(8,128)(2,1)}, bf16[768,384]{1,0:T(8,128)(2,1)}, bf...) custom-call(s32[2]{0:T(128)} %pad_add_fusion.place, ...), custom_call_target="tpu_custom_call" | custom-call | flops 13589544960 | bytes 16777216 | tf_op jit(solution)/shard_map/pallas_call | solution.py:187
  119.5 11.1 %all-to-all-start.1 = ((bf16[4,768,384]{2,1,0:T(8,128)(2,1)}), bf16[4,768,384]{2,1,0:T(8,128)(2,1)}, u32[]{:S(2)}, u32[]{:S(2)}) async-start(bf16[4,768,384]{2,1,0:T(8,128)(2,1)} %get-tuple-element.24), calls=%async_computation.1 | async-start | bytes 4718592 | tf_op jit(solution)/shard_map/all_to_all | solution.py:64
  130.6 3.5 %collective-permute-start.8 = (bf16[768,384]{1,0:T(8,128)(2,1)}, bf16[768,384]{1,0:T(8,128)(2,1)}, u32[]{:S(2)}, u32[]{:S(2)}) collective-permute-start(bf16[768,384]{1,0:T(8,128)(2,1)} %get-tuple-element.27), channel_id=1, source_target_pairs={{0,4},{4,0},{128,132},{132,128},{1,5},{5,1},{129,133},{133,129},{2... | collective-permute-start | bytes 1769480 | tf_op jit(solution)/shard_map/ppermute | solution.py:51
  142.0 2.6 %convert_reduce_fusion = (f32[768]{0:T(1024)S(1)}, bf16[576,768]{1,0:T(8,128)(2,1)}) fusion(f32[576,768]{1,0:T(8,128)S(1)} %get-tuple-element.95, f32[576]{0:T(1024)S(1)} %get-tuple-element.123, f32[576]{0:T(1024)S(1)} %get-tuple-element.124, f32[768]{0:T(1024)S(1)} %copy-done.8, f32[576,768]{1,0:T(8,128)S(1)} %copy-done.3, ...), kind=kLoop, calls=%fused_computation.16 | loop fusion | flops 4422912 | bytes 5321472 | tf_op jit(solution)/shard_map/reduce_sum | solution.py:364
  144.7 10.7 %shard_map.147 = f32[49,768]{1,0:T(8,128)} custom-call(bf16[2,12,56,768]{3,2,1,0:T(8,128)(2,1)} %copy-done, bf16[2,6,48,768]{3,2,1,0:T(8,128)(2,1)} %bitcast.35), custom_call_target="tpu_custom_call" | custom-call | flops 10000000000 | bytes 4194304 | tf_op jit(solution)/shard_map/pallas_call | solution.py:289
  159.5 3.8 %collective-permute-start.5 = (bf16[2,3,48,768]{3,2,1,0:T(8,128)(2,1)S(1)}, bf16[2,3,48,768]{3,2,1,0:T(8,128)(2,1)S(1)}, u32[]{:S(2)}, u32[]{:S(2)}) collective-permute-start(bf16[2,3,48,768]{3,2,1,0:T(8,128)(2,1)S(1)} %get-tuple-element.100), channel_id=1, source_target_pairs={{0,1},{1,2},{2,3},{3,4},{4,5},{5,6},{6,7},{8,9},{9,10},{10,11},{11... | collective-permute-start | bytes 1327112 | tf_op jit(solution)/shard_map/ppermute | solution.py:28
  166.0 2.5 %add_convert_fusion.1 = bf16[768,384]{1,0:T(8,128)(2,1)} fusion(bf16[768,384]{1,0:T(8,128)(2,1)} %collective-permute-done.9, bf16[768,384]{1,0:T(8,128)(2,1)} %collective-permute-done.8, bf16[768,384]{1,0:T(8,128)(2,1)} %collective-permute-done.7, bf16[768,384]{1,0:T(8,128)(2,1)S(1)} %copy-done.5), kind=kLoop, calls=%fused_computation.25 | loop fusion | flops 2359296 | bytes 2949120 | tf_op jit(solution)/shard_map/convert_element_type | solution.py:66
  168.6 2.8 %collective-permute-done.14 = f32[64,768]{1,0:T(8,128)S(1)} collective-permute-done((f32[64,768]{1,0:T(8,128)S(1)}, f32[64,768]{1,0:T(8,128)S(1)}, u32[]{:S(2)}, u32[]{:S(2)}) %collective-permute-start.14) | collective-permute-done | bytes 196640 | tf_op jit(solution)/shard_map/ppermute | solution.py:51
  177.6 9.4 %collective-permute-start.18 = (f32[8,768]{1,0:T(8,128)S(1)}, f32[8,768]{1,0:T(8,128)S(1)}, u32[]{:S(2)}, u32[]{:S(2)}) collective-permute-start(f32[8,768]{1,0:T(8,128)S(1)} %get-tuple-element.115), channel_id=1, source_target_pairs={{0,3},{1,0},{2,1},{3,2},{4,7},{5,4},{6,5},{7,6},{8,11},{9,8},{10,9... | collective-permute-start | bytes 73736 | tf_op jit(solution)/shard_map/ppermute | solution.py:95
  195.6 5.9 %all-to-all-start.2 = ((bf16[4,192,384]{2,1,0:T(8,128)(2,1)}), bf16[4,192,384]{2,1,0:T(8,128)(2,1)S(1)}, u32[]{:S(2)}, u32[]{:S(2)}) async-start(bf16[4,192,384]{2,1,0:T(8,128)(2,1)} %bitcast.11), calls=%async_computation.2 | async-start | bytes 1179648 | tf_op jit(solution)/shard_map/all_to_all | solution.py:40
  201.6 5.1 %collective-permute-done.10 = bf16[192,384]{1,0:T(8,128)(2,1)S(1)} collective-permute-done((bf16[192,384]{1,0:T(8,128)(2,1)S(1)}, bf16[192,384]{1,0:T(8,128)(2,1)S(1)}, u32[]{:S(2)}, u32[]{:S(2)}) %collective-permute-start.10) | collective-permute-done | bytes 147488 | tf_op jit(solution)/shard_map/ppermute | solution.py:51
  209.5 3.5 %all-to-all-start.3 = ((bf16[8,80,384]{2,1,0:T(8,128)(2,1)}), bf16[8,80,384]{2,1,0:T(8,128)(2,1)S(1)}, u32[]{:S(2)}, u32[]{:S(2)}) async-start(bf16[8,80,384]{2,1,0:T(8,128)(2,1)} %pad_maximum_fusion.2), calls=%async_computation.3 | async-start | bytes 983040 | tf_op jit(solution)/shard_map/all_to_all | solution.py:106
  213.0 10.4 %shard_map.148 = bf16[2,6,48,768]{3,2,1,0:T(8,128)(2,1)} custom-call(bf16[2,12,56,768]{3,2,1,0:T(8,128)(2,1)} %select_maximum_fusion.padded, bf16[2,6,48,768]{3,2,1,0:T(8,128)(2,1)} %cotangent.1, f32[49,768]{1,0:T(8,128)} %kernel.1), custom_call_target="tpu_custom_call" | custom-call | flops 10000000000 | bytes 4194304 | tf_op jit(solution)/shard_map/pallas_call | solution.py:245
  223.3 2.5 all-to-all-done.3
  226.8 4.8 %all-to-all-start.4 = ((bf16[8,80,384]{2,1,0:T(8,128)(2,1)}), bf16[8,80,384]{2,1,0:T(8,128)(2,1)S(1)}, u32[]{:S(2)}, u32[]{:S(2)}) async-start(bf16[8,80,384]{2,1,0:T(8,128)(2,1)} %broadcast_in_dim.102), calls=%async_computation.4 | async-start | bytes 983040 | tf_op jit(solution)/shard_map/all_to_all | solution.py:46
  231.6 8.9 %all-to-all-done.4 = bf16[8,80,384]{2,1,0:T(8,128)(2,1)S(1)} async-done(((bf16[8,80,384]{2,1,0:T(8,128)(2,1)}), bf16[8,80,384]{2,1,0:T(8,128)(2,1)S(1)}, u32[]{:S(2)}, u32[]{:S(2)}) %all-to-all-start.4) | async-done | bytes 491552 | tf_op jit(solution)/shard_map/all_to_all | solution.py:46
  (144 shorter events, 52.4 us)
Async XLA Ops:
  7.2 83.7 %all-gather.2.cloned.1.call-start = ((), (), s32[]{:S(2)}) async-start(), calls=%async_computation.5 | async-start | bytes 5013504 | tf_op jit(solution)/shard_map/all_gather | solution.py:55
  10.3 16.0 %collective-permute-start.1 = (bf16[2,3,48,768]{3,2,1,0:T(8,128)(2,1)S(1)}, bf16[2,3,48,768]{3,2,1,0:T(8,128)(2,1)S(1)}, u32[]{:S(2)}, u32[]{:S(2)}) collective-permute-start(bf16[2,3,48,768]{3,2,1,0:T(8,128)(2,1)S(1)} %get-tuple-element.105), channel_id=1, source_target_pairs={{1,0},{2,1},{3,2},{4,3},{5,4},{6,5},{7,6},{9,8},{10,9},{11,10},{12... | collective-permute-start | bytes 1327112 | tf_op jit(solution)/shard_map/ppermute | solution.py:29
  14.6 11.5 %collective-permute-start = (bf16[2,3,48,768]{3,2,1,0:T(8,128)(2,1)S(1)}, bf16[2,3,48,768]{3,2,1,0:T(8,128)(2,1)S(1)}, u32[]{:S(2)}, u32[]{:S(2)}) collective-permute-start(bf16[2,3,48,768]{3,2,1,0:T(8,128)(2,1)S(1)} %get-tuple-element.104), channel_id=1, source_target_pairs={{0,1},{1,2},{2,3},{3,4},{4,5},{5,6},{6,7},{8,9},{9,10},{10,11},{11... | collective-permute-start | bytes 1327112 | tf_op jit(solution)/shard_map/ppermute | solution.py:28
  17.7 45.1 %collective-permute-start.3 = (bf16[576,768]{1,0:T(8,128)(2,1)}, bf16[576,768]{1,0:T(8,128)(2,1)}, u32[]{:S(2)}, u32[]{:S(2)}) collective-permute-start(bf16[576,768]{1,0:T(8,128)(2,1)} %fusion.6), channel_id=1, source_target_pairs={{0,8},{8,0},{1,9},{9,1},{2,10},{10,2},{3,11},{11,3},{4,12},{12,4},... | collective-permute-start | bytes 2654216 | tf_op jit(solution)/shard_map/ppermute | solution.py:34
  42.7 22.9 %collective-permute-start.2 = (bf16[576,768]{1,0:T(8,128)(2,1)}, bf16[576,768]{1,0:T(8,128)(2,1)S(1)}, u32[]{:S(2)}, u32[]{:S(2)}) collective-permute-start(bf16[576,768]{1,0:T(8,128)(2,1)} %get-tuple-element.94), channel_id=1, source_target_pairs={{0,8},{8,0},{1,9},{9,1},{2,10},{10,2},{3,11},{11,3},{4,12},{12,4},... | collective-permute-start | bytes 2654216 | tf_op jit(solution)/shard_map/ppermute | solution.py:34
  43.3 18.2 %all-to-all-start = ((f32[16,1,96]{2,1,0:T(1,128)}), f32[16,1,96]{2,1,0:T(1,128)S(1)}, u32[]{:S(2)}, u32[]{:S(2)}) async-start(f32[16,1,96]{2,1,0:T(1,128)} %broadcast_in_dim.84), calls=%async_computation | async-start | bytes 16384 | tf_op jit(solution)/shard_map/all_to_all | solution.py:46
  117.5 22.6 %collective-permute-start.4 = (bf16[576,768]{1,0:T(8,128)(2,1)}, bf16[576,768]{1,0:T(8,128)(2,1)}, u32[]{:S(2)}, u32[]{:S(2)}) collective-permute-start(bf16[576,768]{1,0:T(8,128)(2,1)} %get-tuple-element.23), channel_id=1, source_target_pairs={{0,8},{8,0},{1,9},{9,1},{2,10},{10,2},{3,11},{11,3},{4,12},{12,4},... | collective-permute-start | bytes 2654216 | tf_op jit(solution)/shard_map/ppermute | solution.py:34
  119.5 69.1 %all-to-all-start.1 = ((bf16[4,768,384]{2,1,0:T(8,128)(2,1)}), bf16[4,768,384]{2,1,0:T(8,128)(2,1)}, u32[]{:S(2)}, u32[]{:S(2)}) async-start(bf16[4,768,384]{2,1,0:T(8,128)(2,1)} %get-tuple-element.24), calls=%async_computation.1 | async-start | bytes 4718592 | tf_op jit(solution)/shard_map/all_to_all | solution.py:64
  130.6 33.6 %collective-permute-start.9 = (bf16[768,384]{1,0:T(8,128)(2,1)}, bf16[768,384]{1,0:T(8,128)(2,1)}, u32[]{:S(2)}, u32[]{:S(2)}) collective-permute-start(bf16[768,384]{1,0:T(8,128)(2,1)} %get-tuple-element.28), channel_id=1, source_target_pairs={{0,132},{4,128},{128,4},{132,0},{1,133},{5,129},{129,5},{133,1},{2... | collective-permute-start | bytes 1769480 | tf_op jit(solution)/shard_map/ppermute | solution.py:51
  130.6 35.4 %collective-permute-start.8 = (bf16[768,384]{1,0:T(8,128)(2,1)}, bf16[768,384]{1,0:T(8,128)(2,1)}, u32[]{:S(2)}, u32[]{:S(2)}) collective-permute-start(bf16[768,384]{1,0:T(8,128)(2,1)} %get-tuple-element.27), channel_id=1, source_target_pairs={{0,4},{4,0},{128,132},{132,128},{1,5},{5,1},{129,133},{133,129},{2... | collective-permute-start | bytes 1769480 | tf_op jit(solution)/shard_map/ppermute | solution.py:51
  134.1 31.9 %collective-permute-start.7 = (bf16[768,384]{1,0:T(8,128)(2,1)}, bf16[768,384]{1,0:T(8,128)(2,1)}, u32[]{:S(2)}, u32[]{:S(2)}) collective-permute-start(bf16[768,384]{1,0:T(8,128)(2,1)} %get-tuple-element.26), channel_id=1, source_target_pairs={{0,128},{4,132},{128,0},{132,4},{1,129},{5,133},{129,1},{133,5},{2... | collective-permute-start | bytes 1769480 | tf_op jit(solution)/shard_map/ppermute | solution.py:51
  156.7 16.2 %collective-permute-start.6 = (bf16[2,3,48,768]{3,2,1,0:T(8,128)(2,1)S(1)}, bf16[2,3,48,768]{3,2,1,0:T(8,128)(2,1)S(1)}, u32[]{:S(2)}, u32[]{:S(2)}) collective-permute-start(bf16[2,3,48,768]{3,2,1,0:T(8,128)(2,1)S(1)} %get-tuple-element.101), channel_id=1, source_target_pairs={{1,0},{2,1},{3,2},{4,3},{5,4},{6,5},{7,6},{9,8},{10,9},{11,10},{12... | collective-permute-start | bytes 1327112 | tf_op jit(solution)/shard_map/ppermute | solution.py:29
  159.5 14.3 %collective-permute-start.5 = (bf16[2,3,48,768]{3,2,1,0:T(8,128)(2,1)S(1)}, bf16[2,3,48,768]{3,2,1,0:T(8,128)(2,1)S(1)}, u32[]{:S(2)}, u32[]{:S(2)}) collective-permute-start(bf16[2,3,48,768]{3,2,1,0:T(8,128)(2,1)S(1)} %get-tuple-element.100), channel_id=1, source_target_pairs={{0,1},{1,2},{2,3},{3,4},{4,5},{5,6},{6,7},{8,9},{9,10},{10,11},{11... | collective-permute-start | bytes 1327112 | tf_op jit(solution)/shard_map/ppermute | solution.py:28
  164.3 7.0 %collective-permute-start.14 = (f32[64,768]{1,0:T(8,128)S(1)}, f32[64,768]{1,0:T(8,128)S(1)}, u32[]{:S(2)}, u32[]{:S(2)}) collective-permute-start(f32[64,768]{1,0:T(8,128)S(1)} %add.353), channel_id=1, source_target_pairs={{0,128},{4,132},{128,0},{132,4},{1,129},{5,133},{129,1},{133,5},{2... | collective-permute-start | bytes 589832 | tf_op jit(solution)/shard_map/ppermute | solution.py:51
  171.4 6.2 %collective-permute-start.15 = (f32[32,768]{1,0:T(8,128)S(1)}, f32[32,768]{1,0:T(8,128)S(1)}, u32[]{:S(2)}, u32[]{:S(2)}) collective-permute-start(f32[32,768]{1,0:T(8,128)S(1)} %constant_dynamic-slice_fusion.3), channel_id=1, source_target_pairs={{0,4},{4,0},{128,132},{132,128},{1,5},{5,1},{129,133},{133,129},{2... | collective-permute-start | bytes 294920 | tf_op jit(solution)/shard_map/ppermute | solution.py:51
  177.6 23.9 %collective-permute-start.18 = (f32[8,768]{1,0:T(8,128)S(1)}, f32[8,768]{1,0:T(8,128)S(1)}, u32[]{:S(2)}, u32[]{:S(2)}) collective-permute-start(f32[8,768]{1,0:T(8,128)S(1)} %get-tuple-element.115), channel_id=1, source_target_pairs={{0,3},{1,0},{2,1},{3,2},{4,7},{5,4},{6,5},{7,6},{8,11},{9,8},{10,9... | collective-permute-start | bytes 73736 | tf_op jit(solution)/shard_map/ppermute | solution.py:95
  187.0 14.5 %collective-permute-start.17 = (f32[8,768]{1,0:T(8,128)S(1)}, f32[8,768]{1,0:T(8,128)S(1)}, u32[]{:S(2)}, u32[]{:S(2)}) collective-permute-start(f32[8,768]{1,0:T(8,128)S(1)} %get-tuple-element.116), channel_id=1, source_target_pairs={{0,2},{1,3},{2,0},{3,1},{4,6},{5,7},{6,4},{7,5},{8,10},{9,11},{10,... | collective-permute-start | bytes 73736 | tf_op jit(solution)/shard_map/ppermute | solution.py:95
  187.0 14.5 %collective-permute-start.16 = (f32[8,768]{1,0:T(8,128)S(1)}, f32[8,768]{1,0:T(8,128)S(1)}, u32[]{:S(2)}, u32[]{:S(2)}) collective-permute-start(f32[8,768]{1,0:T(8,128)S(1)} %get-tuple-element.114), channel_id=1, source_target_pairs={{0,1},{1,2},{2,3},{3,0},{4,5},{5,6},{6,7},{7,4},{8,9},{9,10},{10,1... | collective-permute-start | bytes 73736 | tf_op jit(solution)/shard_map/ppermute | solution.py:95
  191.0 10.6 %collective-permute-start.12 = (bf16[192,384]{1,0:T(8,128)(2,1)S(1)}, bf16[192,384]{1,0:T(8,128)(2,1)S(1)}, u32[]{:S(2)}, u32[]{:S(2)}) collective-permute-start(bf16[192,384]{1,0:T(8,128)(2,1)S(1)} %bitcast.47), channel_id=1, source_target_pairs={{0,132},{4,128},{128,4},{132,0},{1,133},{5,129},{129,5},{133,1},{2... | collective-permute-start | bytes 442376 | tf_op jit(solution)/shard_map/ppermute | solution.py:51
  193.3 8.3 %collective-permute-start.11 = (bf16[192,384]{1,0:T(8,128)(2,1)S(1)}, bf16[192,384]{1,0:T(8,128)(2,1)S(1)}, u32[]{:S(2)}, u32[]{:S(2)}) collective-permute-start(bf16[192,384]{1,0:T(8,128)(2,1)S(1)} %bitcast.46), channel_id=1, source_target_pairs={{0,4},{4,0},{128,132},{132,128},{1,5},{5,1},{129,133},{133,129},{2... | collective-permute-start | bytes 442376 | tf_op jit(solution)/shard_map/ppermute | solution.py:51
  195.6 12.8 %all-to-all-start.2 = ((bf16[4,192,384]{2,1,0:T(8,128)(2,1)}), bf16[4,192,384]{2,1,0:T(8,128)(2,1)S(1)}, u32[]{:S(2)}, u32[]{:S(2)}) async-start(bf16[4,192,384]{2,1,0:T(8,128)(2,1)} %bitcast.11), calls=%async_computation.2 | async-start | bytes 1179648 | tf_op jit(solution)/shard_map/all_to_all | solution.py:40
  201.5 5.1 %collective-permute-start.10 = (bf16[192,384]{1,0:T(8,128)(2,1)S(1)}, bf16[192,384]{1,0:T(8,128)(2,1)S(1)}, u32[]{:S(2)}, u32[]{:S(2)}) collective-permute-start(bf16[192,384]{1,0:T(8,128)(2,1)S(1)} %bitcast.45), channel_id=1, source_target_pairs={{0,128},{4,132},{128,0},{132,4},{1,129},{5,133},{129,1},{133,5},{2... | collective-permute-start | bytes 442376 | tf_op jit(solution)/shard_map/ppermute | solution.py:51
  209.5 16.3 %all-to-all-start.3 = ((bf16[8,80,384]{2,1,0:T(8,128)(2,1)}), bf16[8,80,384]{2,1,0:T(8,128)(2,1)S(1)}, u32[]{:S(2)}, u32[]{:S(2)}) async-start(bf16[8,80,384]{2,1,0:T(8,128)(2,1)} %pad_maximum_fusion.2), calls=%async_computation.3 | async-start | bytes 983040 | tf_op jit(solution)/shard_map/all_to_all | solution.py:106
  226.8 13.7 %all-to-all-start.4 = ((bf16[8,80,384]{2,1,0:T(8,128)(2,1)}), bf16[8,80,384]{2,1,0:T(8,128)(2,1)S(1)}, u32[]{:S(2)}, u32[]{:S(2)}) async-start(bf16[8,80,384]{2,1,0:T(8,128)(2,1)} %broadcast_in_dim.102), calls=%async_computation.4 | async-start | bytes 983040 | tf_op jit(solution)/shard_map/all_to_all | solution.py:46
  (19 other events, 156.9 us)
Sparse Core Ops, SparseCore 0:
  10.4 80.4 all-gather.1

commit v4 on v3

--- a/solution.py
+++ b/solution.py
@@ -57,13 +57,14 @@
     return whole, bias
 
 
-def scatter_terms(first, parts):
+def scatter_terms(first, parts, small):
     second = parts[0].astype(jnp.float32)
     for m in (1, 2, 3):
         second = second + across(parts[m], m).astype(jnp.float32)
     first = jnp.sum(lax.all_to_all(first, "x", 0, 0).astype(jnp.float32), axis=0)
     first = first.astype(jnp.bfloat16).reshape(2, 4, 2, 48, 384)
-    first, second = lax.optimization_barrier((first, second.astype(jnp.bfloat16)))
+    small = small + swap(small)
+    first, second, small = lax.optimization_barrier((first, second.astype(jnp.bfloat16), small))
     second = spread_sum(second, "x")
     y_lo, y_hi = lax.axis_index("y_lo"), lax.axis_index("y_hi")
     sent = [
@@ -75,7 +76,7 @@
     first = sent[0].astype(jnp.float32)
     for m in (1, 2, 3):
         first = first + across(sent[m], m).astype(jnp.float32)
-    return first, second
+    return first, second, small
 
 
 def two(cells):
@@ -85,10 +86,9 @@
 
 def spread_small(small):
     x, y_hi = lax.axis_index("x"), lax.axis_index("y_hi")
-    small = small + swap(small)
-    small = small + across(small, 1)
     mine = lax.dynamic_slice(small, (y_hi * 32, 0), (32, 768))
-    small = mine + across(lax.dynamic_slice(small, ((1 - y_hi) * 32, 0), (32, 768)), 2)
+    other = lax.dynamic_slice(small, ((1 - y_hi) * 32, 0), (32, 768))
+    small = mine + across(mine, 1) + across(other, 2) + across(other, 3)
     total = lax.dynamic_slice(small, (x * 8, 0), (8, 768))
     for k in (1, 2, 3):
         sent = lax.dynamic_slice(small, ((x + k) % 4 * 8, 0), (8, 768))
@@ -337,7 +337,6 @@
     normed2 = jnp.concatenate([normed, swap(normed)], axis=0)
 
     first, *parts, own, peer, sums_b1, moment_row = mlp(normed2, scaled2, weights, b1_h)
-    first, second = scatter_terms(first, parts)
     grad_normed = own + swap(peer).astype(jnp.float32)
 
     weighted = grad_normed * ln_gain
@@ -371,6 +370,7 @@
         ],
         axis=0,
     )
+    first, second, local_small = scatter_terms(first, parts, local_small)
     share, total_small, d_input = finish(
         first, second, local_small, (lambda g: transposed(g, cotangent, dw_kernel), grad_padded)
     )

time: 251 us -> 247 us (0.984)
  waiting for transfers between devices: 60.7 us -> 57.5 us
    ppermute x8 -> x9, waiting for transfers between devices: 9.48 us -> 6.11 us  [across(): return lax.ppermute(cells, Y, [(i, i ^ flip) for i in range(4)])]
    ppermute x8 -> x9, starting transfers between devices: 12 us -> 12.5 us  [across(): return lax.ppermute(cells, Y, [(i, i ^ flip) for i in range(4)])]
  transfers between devices with their start and end apart: 25 -> 26, of which waited for: 10 -> 11; matrix products, arithmetic and copies ran while one was open for 20% -> 19% of each run, Pallas kernels for 8% -> 9%
where the time goes in v4:
time: 247 us; the launch traced here: 245 us
  starting transfers between devices  71 us (29%)
  waiting for transfers between devices  57.5 us (23%)
  Pallas kernels  46.5 us (19%)
  other arithmetic  42.9 us (17%)
  between operations  14.7 us (6%)
  local copies, waits for them, and re-layouts  12.5 us (5%)
    pallas_call x1, Pallas kernels, mlp(): pl.pallas_call(mlp_kernel, grid=(hid // BLOCK,), in_specs=[pl.BlockSpec(m...  25.5 us
    all_gather x1, waiting for transfers between devices, gather_weights(): lax.all_gather(jnp.concatenate([w1_t, w2], axis=1), PAIRS, axis=0, tiled=...  22.8 us
    all_to_all x2, starting transfers between devices, gather(): lax.all_to_all(jnp.broadcast_to(part[None], (count,) + part.shape), axes,...  15.3 us
    all_to_all x2, waiting for transfers between devices, gather(): lax.all_to_all(jnp.broadcast_to(part[None], (count,) + part.shape), axes,...  15.2 us
    reduce_sum x1, other arithmetic, shards(): center = conv - jnp.mean(conv, axis=-1, keepdims=True)  13.3 us
    ppermute x9, starting transfers between devices, across(): return lax.ppermute(cells, Y, [(i, i ^ flip) for i in range(4)])  12.5 us
    ppermute x3, starting transfers between devices, spread_small(): lax.ppermute(sent, 'x', [(i, (i + k) % 4) for i in range(4)])  12.4 us
    all_to_all x1, starting transfers between devices, scatter_terms(): lax.all_to_all(first, 'x', 0, 0).astype(jnp.float32)  11.1 us
  transfers between devices with their start and end apart: 26, of which 11 were waited for; matrix products, arithmetic and copies ran while one was open for 19% of the time, Pallas kernels for 9%

profile of v4, /device:TPU:2, one launch (start us, length us, event | category | flops | bytes accessed | tf_op | source)
XLA Modules:
  0.0 245.0 jit_solution(7687089445398010474)
XLA Ops:
  10.3 4.3 %collective-permute-start.1 = (bf16[2,3,48,768]{3,2,1,0:T(8,128)(2,1)S(1)}, bf16[2,3,48,768]{3,2,1,0:T(8,128)(2,1)S(1)}, u32[]{:S(2)}, u32[]{:S(2)}) collective-permute-start(bf16[2,3,48,768]{3,2,1,0:T(8,128)(2,1)S(1)} %get-tuple-element.107), channel_id=1, source_target_pairs={{1,0},{2,1},{3,2},{4,3},{5,4},{6,5},{7,6},{9,8},{10,9},{11,10},{12... | collective-permute-start | bytes 1327112 | tf_op jit(solution)/shard_map/ppermute | solution.py:29
  18.1 8.1 %collective-permute-done = bf16[2,3,48,768]{3,2,1,0:T(8,128)(2,1)S(1)} collective-permute-done((bf16[2,3,48,768]{3,2,1,0:T(8,128)(2,1)S(1)}, bf16[2,3,48,768]{3,2,1,0:T(8,128)(2,1)S(1)}, u32[]{:S(2)}, u32[]{:S(2)}) %collective-permute-start) | collective-permute-done | bytes 442400 | tf_op jit(solution)/shard_map/ppermute | solution.py:28
  27.4 13.3 %fusion.12 = (f32[2,6,48]{2,1,0:T(8,128)S(1)}, f32[2,6,48,768]{3,2,1,0:T(8,128)S(1)}) fusion(f32[768]{0:T(1024)S(1)} %copy-done.15, f32[768]{0:T(1024)S(1)} %get-tuple-element.93, bf16[2,12,56,768]{3,2,1,0:T(8,128)(2,1)S(1)} %fusion.5.padded, f32[768]{0:T(1024)S(1)} %get-tuple-element.46, f32[768]{0:T(1024)S(1)} %get-tuple-element.47, ...), kind=kLoop, calls=%fused_computation.125 | loop fusion | flops 65469888 | bytes 45277440 | tf_op jit(solution)/shard_map/reduce_sum | solution.py:332
  43.3 9.8 %all-to-all-start = ((f32[16,1,96]{2,1,0:T(1,128)}), f32[16,1,96]{2,1,0:T(1,128)S(1)}, u32[]{:S(2)}, u32[]{:S(2)}) async-start(f32[16,1,96]{2,1,0:T(1,128)} %broadcast_in_dim.84), calls=%async_computation | async-start | bytes 16384 | tf_op jit(solution)/shard_map/all_to_all | solution.py:46
  55.1 6.4 %all-to-all-done = f32[16,1,96]{2,1,0:T(1,128)S(1)} async-done(((f32[16,1,96]{2,1,0:T(1,128)}), f32[16,1,96]{2,1,0:T(1,128)S(1)}, u32[]{:S(2)}, u32[]{:S(2)}) %all-to-all-start) | async-done | bytes 6176 | tf_op jit(solution)/shard_map/all_to_all | solution.py:46
  62.8 2.8 %pad_maximum_fusion.1.scaled = bf16[1152,768]{1,0:T(8,128)(2,1)} fusion(bf16[576,768]{1,0:T(8,128)(2,1)} %collective-permute-done.3, bf16[576,768]{1,0:T(8,128)(2,1)} %fusion.6), kind=kLoop, calls=%fused_computation.11 | loop fusion | flops 3538944 | bytes 3538944 | tf_op jit(solution)/shard_map/concatenate | solution.py:330
  65.5 2.5 %pad_maximum_fusion.normed = bf16[1152,768]{1,0:T(8,128)(2,1)} fusion(bf16[576,768]{1,0:T(8,128)(2,1)S(1)} %collective-permute-done.2, bf16[576,768]{1,0:T(8,128)(2,1)} %get-tuple-element.96), kind=kLoop, calls=%fused_computation.10 | loop fusion | flops 3538944 | bytes 3538944 | tf_op jit(solution)/shard_map/concatenate | solution.py:337
  68.1 22.8 %all-gather.2.cloned.1.call-done.w1.w2 = bf16[1536,1536]{1,0:T(8,128)(2,1)} async-done(((bf16[96,1536]{1,0:T(8,128)(2,1)}), bf16[1536,1536]{1,0:T(8,128)(2,1)}) %all-gather.2.cloned.1.call-update) | async-done | bytes 4718608 | tf_op jit(solution)/shard_map/all_gather | solution.py:55
  92.0 25.5 %shard_map.146 = (bf16[4,768,384]{2,1,0:T(8,128)(2,1)}, bf16[768,384]{1,0:T(8,128)(2,1)}, bf16[768,384]{1,0:T(8,128)(2,1)}, bf16[768,384]{1,0:T(8,128)(2,1)}, bf...) custom-call(s32[2]{0:T(128)} %pad_add_fusion.place, ...), custom_call_target="tpu_custom_call" | custom-call | flops 13589544960 | bytes 16777216 | tf_op jit(solution)/shard_map/pallas_call | solution.py:187
  119.5 11.1 %all-to-all-start.1 = ((bf16[4,768,384]{2,1,0:T(8,128)(2,1)}), bf16[4,768,384]{2,1,0:T(8,128)(2,1)}, u32[]{:S(2)}, u32[]{:S(2)}) async-start(bf16[4,768,384]{2,1,0:T(8,128)(2,1)} %get-tuple-element.25), calls=%async_computation.1 | async-start | bytes 4718592 | tf_op jit(solution)/shard_map/all_to_all | solution.py:64
  130.6 3.5 %collective-permute-start.8 = (bf16[768,384]{1,0:T(8,128)(2,1)}, bf16[768,384]{1,0:T(8,128)(2,1)}, u32[]{:S(2)}, u32[]{:S(2)}) collective-permute-start(bf16[768,384]{1,0:T(8,128)(2,1)} %get-tuple-element.28), channel_id=1, source_target_pairs={{0,4},{4,0},{128,132},{132,128},{1,5},{5,1},{129,133},{133,129},{2... | collective-permute-start | bytes 1769480 | tf_op jit(solution)/shard_map/ppermute | solution.py:51
  146.1 3.9 %collective-permute-start.5 = (bf16[2,3,48,768]{3,2,1,0:T(8,128)(2,1)S(1)}, bf16[2,3,48,768]{3,2,1,0:T(8,128)(2,1)S(1)}, u32[]{:S(2)}, u32[]{:S(2)}) collective-permute-start(bf16[2,3,48,768]{3,2,1,0:T(8,128)(2,1)S(1)} %get-tuple-element.102), channel_id=1, source_target_pairs={{0,1},{1,2},{2,3},{3,4},{4,5},{5,6},{6,7},{8,9},{9,10},{10,11},{11... | collective-permute-start | bytes 1327112 | tf_op jit(solution)/shard_map/ppermute | solution.py:28
  150.0 10.6 %shard_map.147 = f32[49,768]{1,0:T(8,128)} custom-call(bf16[2,12,56,768]{3,2,1,0:T(8,128)(2,1)} %copy-done, bf16[2,6,48,768]{3,2,1,0:T(8,128)(2,1)} %bitcast.36), custom_call_target="tpu_custom_call" | custom-call | flops 10000000000 | bytes 4194304 | tf_op jit(solution)/shard_map/pallas_call | solution.py:289
  162.2 2.5 %add_convert_fusion.1 = bf16[768,384]{1,0:T(8,128)(2,1)} fusion(bf16[768,384]{1,0:T(8,128)(2,1)} %collective-permute-done.9, bf16[768,384]{1,0:T(8,128)(2,1)} %collective-permute-done.8, bf16[768,384]{1,0:T(8,128)(2,1)} %collective-permute-done.7, bf16[768,384]{1,0:T(8,128)(2,1)S(1)} %copy-done.7), kind=kLoop, calls=%fused_computation.25 | loop fusion | flops 2359296 | bytes 2949120 | tf_op jit(solution)/shard_map/convert_element_type | solution.py:67
  164.8 2.4 reduce_sum.106
  167.3 3.5 %collective-permute-start.15 = (f32[32,768]{1,0:T(8,128)S(1)}, f32[32,768]{1,0:T(8,128)S(1)}, u32[]{:S(2)}, u32[]{:S(2)}) collective-permute-start(f32[32,768]{1,0:T(8,128)S(1)} %get-tuple-element.115), channel_id=1, source_target_pairs={{0,4},{4,0},{128,132},{132,128},{1,5},{5,1},{129,133},{133,129},{2... | collective-permute-start | bytes 294920 | tf_op jit(solution)/shard_map/ppermute | solution.py:51
  176.4 7.7 %collective-permute-start.19 = (f32[8,768]{1,0:T(8,128)S(1)}, f32[8,768]{1,0:T(8,128)S(1)}, u32[]{:S(2)}, u32[]{:S(2)}) collective-permute-start(f32[8,768]{1,0:T(8,128)S(1)} %get-tuple-element.119), channel_id=1, source_target_pairs={{0,3},{1,0},{2,1},{3,2},{4,7},{5,4},{6,5},{7,6},{8,11},{9,8},{10,9... | collective-permute-start | bytes 73736 | tf_op jit(solution)/shard_map/ppermute | solution.py:95
  186.3 2.5 %collective-permute-start.17 = (f32[8,768]{1,0:T(8,128)S(1)}, f32[8,768]{1,0:T(8,128)S(1)}, u32[]{:S(2)}, u32[]{:S(2)}) collective-permute-start(f32[8,768]{1,0:T(8,128)S(1)} %get-tuple-element.118), channel_id=1, source_target_pairs={{0,1},{1,2},{2,3},{3,0},{4,5},{5,6},{6,7},{7,4},{8,9},{9,10},{10,1... | collective-permute-start | bytes 73736 | tf_op jit(solution)/shard_map/ppermute | solution.py:95
  191.3 3.6 %all-to-all-start.2 = ((bf16[4,192,384]{2,1,0:T(8,128)(2,1)}), bf16[4,192,384]{2,1,0:T(8,128)(2,1)S(1)}, u32[]{:S(2)}, u32[]{:S(2)}) async-start(bf16[4,192,384]{2,1,0:T(8,128)(2,1)} %bitcast.11), calls=%async_computation.2 | async-start | bytes 1179648 | tf_op jit(solution)/shard_map/all_to_all | solution.py:40
  202.8 3.5 %all-to-all-start.3 = ((bf16[8,80,384]{2,1,0:T(8,128)(2,1)}), bf16[8,80,384]{2,1,0:T(8,128)(2,1)S(1)}, u32[]{:S(2)}, u32[]{:S(2)}) async-start(bf16[8,80,384]{2,1,0:T(8,128)(2,1)} %pad_maximum_fusion.2), calls=%async_computation.3 | async-start | bytes 983040 | tf_op jit(solution)/shard_map/all_to_all | solution.py:106
  206.3 10.4 %shard_map.148 = bf16[2,6,48,768]{3,2,1,0:T(8,128)(2,1)} custom-call(bf16[2,12,56,768]{3,2,1,0:T(8,128)(2,1)} %select_maximum_fusion.padded, bf16[2,6,48,768]{3,2,1,0:T(8,128)(2,1)} %cotangent.1, f32[49,768]{1,0:T(8,128)} %kernel.1), custom_call_target="tpu_custom_call" | custom-call | flops 10000000000 | bytes 4194304 | tf_op jit(solution)/shard_map/pallas_call | solution.py:245
  216.7 3.5 %all-to-all-done.3 = bf16[8,80,384]{2,1,0:T(8,128)(2,1)S(1)} async-done(((bf16[8,80,384]{2,1,0:T(8,128)(2,1)}), bf16[8,80,384]{2,1,0:T(8,128)(2,1)S(1)}, u32[]{:S(2)}, u32[]{:S(2)}) %all-to-all-start.3) | async-done | bytes 491552 | tf_op jit(solution)/shard_map/all_to_all | solution.py:106
  221.1 5.5 %all-to-all-start.4 = ((bf16[8,80,384]{2,1,0:T(8,128)(2,1)}), bf16[8,80,384]{2,1,0:T(8,128)(2,1)S(1)}, u32[]{:S(2)}, u32[]{:S(2)}) async-start(bf16[8,80,384]{2,1,0:T(8,128)(2,1)} %broadcast_in_dim.102), calls=%async_computation.4 | async-start | bytes 983040 | tf_op jit(solution)/shard_map/all_to_all | solution.py:46
  226.7 8.9 %all-to-all-done.4 = bf16[8,80,384]{2,1,0:T(8,128)(2,1)S(1)} async-done(((bf16[8,80,384]{2,1,0:T(8,128)(2,1)}), bf16[8,80,384]{2,1,0:T(8,128)(2,1)S(1)}, u32[]{:S(2)}, u32[]{:S(2)}) %all-to-all-start.4) | async-done | bytes 491552 | tf_op jit(solution)/shard_map/all_to_all | solution.py:46
  (147 shorter events, 51.7 us)
Async XLA Ops:
  7.2 83.7 %all-gather.2.cloned.1.call-start = ((), (), s32[]{:S(2)}) async-start(), calls=%async_computation.5 | async-start | bytes 5013504 | tf_op jit(solution)/shard_map/all_gather | solution.py:55
  10.3 16.0 %collective-permute-start.1 = (bf16[2,3,48,768]{3,2,1,0:T(8,128)(2,1)S(1)}, bf16[2,3,48,768]{3,2,1,0:T(8,128)(2,1)S(1)}, u32[]{:S(2)}, u32[]{:S(2)}) collective-permute-start(bf16[2,3,48,768]{3,2,1,0:T(8,128)(2,1)S(1)} %get-tuple-element.107), channel_id=1, source_target_pairs={{1,0},{2,1},{3,2},{4,3},{5,4},{6,5},{7,6},{9,8},{10,9},{11,10},{12... | collective-permute-start | bytes 1327112 | tf_op jit(solution)/shard_map/ppermute | solution.py:29
  14.6 11.5 %collective-permute-start = (bf16[2,3,48,768]{3,2,1,0:T(8,128)(2,1)S(1)}, bf16[2,3,48,768]{3,2,1,0:T(8,128)(2,1)S(1)}, u32[]{:S(2)}, u32[]{:S(2)}) collective-permute-start(bf16[2,3,48,768]{3,2,1,0:T(8,128)(2,1)S(1)} %get-tuple-element.106), channel_id=1, source_target_pairs={{0,1},{1,2},{2,3},{3,4},{4,5},{5,6},{6,7},{8,9},{9,10},{10,11},{11... | collective-permute-start | bytes 1327112 | tf_op jit(solution)/shard_map/ppermute | solution.py:28
  17.7 45.1 %collective-permute-start.3 = (bf16[576,768]{1,0:T(8,128)(2,1)}, bf16[576,768]{1,0:T(8,128)(2,1)}, u32[]{:S(2)}, u32[]{:S(2)}) collective-permute-start(bf16[576,768]{1,0:T(8,128)(2,1)} %fusion.6), channel_id=1, source_target_pairs={{0,8},{8,0},{1,9},{9,1},{2,10},{10,2},{3,11},{11,3},{4,12},{12,4},... | collective-permute-start | bytes 2654216 | tf_op jit(solution)/shard_map/ppermute | solution.py:34
  42.7 22.9 %collective-permute-start.2 = (bf16[576,768]{1,0:T(8,128)(2,1)}, bf16[576,768]{1,0:T(8,128)(2,1)S(1)}, u32[]{:S(2)}, u32[]{:S(2)}) collective-permute-start(bf16[576,768]{1,0:T(8,128)(2,1)} %get-tuple-element.96), channel_id=1, source_target_pairs={{0,8},{8,0},{1,9},{9,1},{2,10},{10,2},{3,11},{11,3},{4,12},{12,4},... | collective-permute-start | bytes 2654216 | tf_op jit(solution)/shard_map/ppermute | solution.py:34
  43.3 18.2 %all-to-all-start = ((f32[16,1,96]{2,1,0:T(1,128)}), f32[16,1,96]{2,1,0:T(1,128)S(1)}, u32[]{:S(2)}, u32[]{:S(2)}) async-start(f32[16,1,96]{2,1,0:T(1,128)} %broadcast_in_dim.84), calls=%async_computation | async-start | bytes 16384 | tf_op jit(solution)/shard_map/all_to_all | solution.py:46
  117.5 22.6 %collective-permute-start.4 = (bf16[576,768]{1,0:T(8,128)(2,1)}, bf16[576,768]{1,0:T(8,128)(2,1)}, u32[]{:S(2)}, u32[]{:S(2)}) collective-permute-start(bf16[576,768]{1,0:T(8,128)(2,1)} %get-tuple-element.24), channel_id=1, source_target_pairs={{0,8},{8,0},{1,9},{9,1},{2,10},{10,2},{3,11},{11,3},{4,12},{12,4},... | collective-permute-start | bytes 2654216 | tf_op jit(solution)/shard_map/ppermute | solution.py:34
  119.5 45.2 %all-to-all-start.1 = ((bf16[4,768,384]{2,1,0:T(8,128)(2,1)}), bf16[4,768,384]{2,1,0:T(8,128)(2,1)}, u32[]{:S(2)}, u32[]{:S(2)}) async-start(bf16[4,768,384]{2,1,0:T(8,128)(2,1)} %get-tuple-element.25), calls=%async_computation.1 | async-start | bytes 4718592 | tf_op jit(solution)/shard_map/all_to_all | solution.py:64
  130.6 31.2 %collective-permute-start.9 = (bf16[768,384]{1,0:T(8,128)(2,1)}, bf16[768,384]{1,0:T(8,128)(2,1)}, u32[]{:S(2)}, u32[]{:S(2)}) collective-permute-start(bf16[768,384]{1,0:T(8,128)(2,1)} %get-tuple-element.29), channel_id=1, source_target_pairs={{0,132},{4,128},{128,4},{132,0},{1,133},{5,129},{129,5},{133,1},{2... | collective-permute-start | bytes 1769480 | tf_op jit(solution)/shard_map/ppermute | solution.py:51
  130.6 31.5 %collective-permute-start.8 = (bf16[768,384]{1,0:T(8,128)(2,1)}, bf16[768,384]{1,0:T(8,128)(2,1)}, u32[]{:S(2)}, u32[]{:S(2)}) collective-permute-start(bf16[768,384]{1,0:T(8,128)(2,1)} %get-tuple-element.28), channel_id=1, source_target_pairs={{0,4},{4,0},{128,132},{132,128},{1,5},{5,1},{129,133},{133,129},{2... | collective-permute-start | bytes 1769480 | tf_op jit(solution)/shard_map/ppermute | solution.py:51
  134.1 28.0 %collective-permute-start.7 = (bf16[768,384]{1,0:T(8,128)(2,1)}, bf16[768,384]{1,0:T(8,128)(2,1)}, u32[]{:S(2)}, u32[]{:S(2)}) collective-permute-start(bf16[768,384]{1,0:T(8,128)(2,1)} %get-tuple-element.27), channel_id=1, source_target_pairs={{0,128},{4,132},{128,0},{132,4},{1,129},{5,133},{129,1},{133,5},{2... | collective-permute-start | bytes 1769480 | tf_op jit(solution)/shard_map/ppermute | solution.py:51
  144.0 27.4 %collective-permute-start.6 = (bf16[2,3,48,768]{3,2,1,0:T(8,128)(2,1)S(1)}, bf16[2,3,48,768]{3,2,1,0:T(8,128)(2,1)S(1)}, u32[]{:S(2)}, u32[]{:S(2)}) collective-permute-start(bf16[2,3,48,768]{3,2,1,0:T(8,128)(2,1)S(1)} %get-tuple-element.103), channel_id=1, source_target_pairs={{1,0},{2,1},{3,2},{4,3},{5,4},{6,5},{7,6},{9,8},{10,9},{11,10},{12... | collective-permute-start | bytes 1327112 | tf_op jit(solution)/shard_map/ppermute | solution.py:29
  146.1 25.3 %collective-permute-start.5 = (bf16[2,3,48,768]{3,2,1,0:T(8,128)(2,1)S(1)}, bf16[2,3,48,768]{3,2,1,0:T(8,128)(2,1)S(1)}, u32[]{:S(2)}, u32[]{:S(2)}) collective-permute-start(bf16[2,3,48,768]{3,2,1,0:T(8,128)(2,1)S(1)} %get-tuple-element.102), channel_id=1, source_target_pairs={{0,1},{1,2},{2,3},{3,4},{4,5},{5,6},{6,7},{8,9},{9,10},{10,11},{11... | collective-permute-start | bytes 1327112 | tf_op jit(solution)/shard_map/ppermute | solution.py:28
  167.2 8.6 %collective-permute-start.16 = (f32[32,768]{1,0:T(8,128)S(1)}, f32[32,768]{1,0:T(8,128)S(1)}, u32[]{:S(2)}, u32[]{:S(2)}) collective-permute-start(f32[32,768]{1,0:T(8,128)S(1)} %get-tuple-element.115), channel_id=1, source_target_pairs={{0,132},{4,128},{128,4},{132,0},{1,133},{5,129},{129,5},{133,1},{2... | collective-permute-start | bytes 294920 | tf_op jit(solution)/shard_map/ppermute | solution.py:51
  167.3 8.5 %collective-permute-start.15 = (f32[32,768]{1,0:T(8,128)S(1)}, f32[32,768]{1,0:T(8,128)S(1)}, u32[]{:S(2)}, u32[]{:S(2)}) collective-permute-start(f32[32,768]{1,0:T(8,128)S(1)} %get-tuple-element.115), channel_id=1, source_target_pairs={{0,4},{4,0},{128,132},{132,128},{1,5},{5,1},{129,133},{133,129},{2... | collective-permute-start | bytes 294920 | tf_op jit(solution)/shard_map/ppermute | solution.py:51
  170.8 5.6 %collective-permute-start.14 = (f32[32,768]{1,0:T(8,128)S(1)}, f32[32,768]{1,0:T(8,128)S(1)}, u32[]{:S(2)}, u32[]{:S(2)}) collective-permute-start(f32[32,768]{1,0:T(8,128)S(1)} %get-tuple-element.114), channel_id=1, source_target_pairs={{0,128},{4,132},{128,0},{132,4},{1,129},{5,133},{129,1},{133,5},{2... | collective-permute-start | bytes 294920 | tf_op jit(solution)/shard_map/ppermute | solution.py:51
  176.4 18.4 %collective-permute-start.19 = (f32[8,768]{1,0:T(8,128)S(1)}, f32[8,768]{1,0:T(8,128)S(1)}, u32[]{:S(2)}, u32[]{:S(2)}) collective-permute-start(f32[8,768]{1,0:T(8,128)S(1)} %get-tuple-element.119), channel_id=1, source_target_pairs={{0,3},{1,0},{2,1},{3,2},{4,7},{5,4},{6,5},{7,6},{8,11},{9,8},{10,9... | collective-permute-start | bytes 73736 | tf_op jit(solution)/shard_map/ppermute | solution.py:95
  184.1 12.5 %collective-permute-start.18 = (f32[8,768]{1,0:T(8,128)S(1)}, f32[8,768]{1,0:T(8,128)S(1)}, u32[]{:S(2)}, u32[]{:S(2)}) collective-permute-start(f32[8,768]{1,0:T(8,128)S(1)} %get-tuple-element.120), channel_id=1, source_target_pairs={{0,2},{1,3},{2,0},{3,1},{4,6},{5,7},{6,4},{7,5},{8,10},{9,11},{10,... | collective-permute-start | bytes 73736 | tf_op jit(solution)/shard_map/ppermute | solution.py:95
  186.3 10.4 %collective-permute-start.17 = (f32[8,768]{1,0:T(8,128)S(1)}, f32[8,768]{1,0:T(8,128)S(1)}, u32[]{:S(2)}, u32[]{:S(2)}) collective-permute-start(f32[8,768]{1,0:T(8,128)S(1)} %get-tuple-element.118), channel_id=1, source_target_pairs={{0,1},{1,2},{2,3},{3,0},{4,5},{5,6},{6,7},{7,4},{8,9},{9,10},{10,1... | collective-permute-start | bytes 73736 | tf_op jit(solution)/shard_map/ppermute | solution.py:95
  188.9 8.7 %collective-permute-start.13 = (bf16[192,384]{1,0:T(8,128)(2,1)S(1)}, bf16[192,384]{1,0:T(8,128)(2,1)S(1)}, u32[]{:S(2)}, u32[]{:S(2)}) collective-permute-start(bf16[192,384]{1,0:T(8,128)(2,1)S(1)} %bitcast.47), channel_id=1, source_target_pairs={{0,132},{4,128},{128,4},{132,0},{1,133},{5,129},{129,5},{133,1},{2... | collective-permute-start | bytes 442376 | tf_op jit(solution)/shard_map/ppermute | solution.py:51
  190.2 7.5 %collective-permute-start.12 = (bf16[192,384]{1,0:T(8,128)(2,1)S(1)}, bf16[192,384]{1,0:T(8,128)(2,1)S(1)}, u32[]{:S(2)}, u32[]{:S(2)}) collective-permute-start(bf16[192,384]{1,0:T(8,128)(2,1)S(1)} %bitcast.46), channel_id=1, source_target_pairs={{0,4},{4,0},{128,132},{132,128},{1,5},{5,1},{129,133},{133,129},{2... | collective-permute-start | bytes 442376 | tf_op jit(solution)/shard_map/ppermute | solution.py:51
  191.3 10.5 %all-to-all-start.2 = ((bf16[4,192,384]{2,1,0:T(8,128)(2,1)}), bf16[4,192,384]{2,1,0:T(8,128)(2,1)S(1)}, u32[]{:S(2)}, u32[]{:S(2)}) async-start(bf16[4,192,384]{2,1,0:T(8,128)(2,1)} %bitcast.11), calls=%async_computation.2 | async-start | bytes 1179648 | tf_op jit(solution)/shard_map/all_to_all | solution.py:40
  202.8 17.4 %all-to-all-start.3 = ((bf16[8,80,384]{2,1,0:T(8,128)(2,1)}), bf16[8,80,384]{2,1,0:T(8,128)(2,1)S(1)}, u32[]{:S(2)}, u32[]{:S(2)}) async-start(bf16[8,80,384]{2,1,0:T(8,128)(2,1)} %pad_maximum_fusion.2), calls=%async_computation.3 | async-start | bytes 983040 | tf_op jit(solution)/shard_map/all_to_all | solution.py:106
  221.1 14.4 %all-to-all-start.4 = ((bf16[8,80,384]{2,1,0:T(8,128)(2,1)}), bf16[8,80,384]{2,1,0:T(8,128)(2,1)S(1)}, u32[]{:S(2)}, u32[]{:S(2)}) async-start(bf16[8,80,384]{2,1,0:T(8,128)(2,1)} %broadcast_in_dim.102), calls=%async_computation.4 | async-start | bytes 983040 | tf_op jit(solution)/shard_map/all_to_all | solution.py:46
  (21 other events, 178.2 us)
Sparse Core Ops, SparseCore 0:
  10.4 80.4 all-gather.1

commit v5 on v4

--- a/solution.py
+++ b/solution.py
@@ -52,24 +52,30 @@
 
 
 def gather_weights(w1_t, w2, b1):
-    whole = lax.all_gather(jnp.concatenate([w1_t, w2], axis=1), PAIRS, axis=0, tiled=True)
-    bias = gather(b1.astype(jnp.float32), PAIRS).reshape(-1)
+    pair = jnp.concatenate([w1_t, w2], axis=1)
+    pair = jnp.concatenate([pair, across(pair, 1)], axis=0)
+    whole = lax.all_gather(pair, "z", axis=0, tiled=True)
+    bias = gather(b1.astype(jnp.float32), PAIRS).reshape(2, 8, -1)
+    bias = jnp.roll(bias, lax.axis_index("y_lo"), 0).transpose(1, 0, 2).reshape(-1)
     return whole, bias
 
 
 def scatter_terms(first, parts, small):
-    second = parts[0].astype(jnp.float32)
-    for m in (1, 2, 3):
-        second = second + across(parts[m], m).astype(jnp.float32)
+    own, near, far, last = parts
+    half = far.shape[0] // 2
+    far = [across(across(far[:half], 1), 3), across(across(far[half:], 3), 1)]
+    second = own.astype(jnp.float32) + across(near, 1).astype(jnp.float32)
+    second = second + across(last, 3).astype(jnp.float32)
+    second = second + jnp.concatenate(far, axis=0).astype(jnp.float32)
     first = jnp.sum(lax.all_to_all(first, "x", 0, 0).astype(jnp.float32), axis=0)
-    first = first.astype(jnp.bfloat16).reshape(2, 4, 2, 48, 384)
+    first = first.astype(jnp.bfloat16).reshape(4, 2, 2, 48, 384)
     small = small + swap(small)
     first, second, small = lax.optimization_barrier((first, second.astype(jnp.bfloat16), small))
     second = spread_sum(second, "x")
-    y_lo, y_hi = lax.axis_index("y_lo"), lax.axis_index("y_hi")
+    y_hi = lax.axis_index("y_hi")
     sent = [
         lax.dynamic_slice(
-            first, (y_lo ^ (m % 2), 0, y_hi ^ (m // 2), 0, 0), (1, 4, 1, 48, 384)
+            first, (0, m % 2, y_hi ^ (m // 2), 0, 0), (4, 1, 1, 48, 384)
         ).reshape(192, 384)
         for m in range(4)
     ]
@@ -144,24 +150,27 @@
         half[:, at : at + 384].astype(jnp.bfloat16) for half in (d_w1, moment) for at in (0, 384)
     ]
 
-    for y_lo in range(2):
-
-        @pl.when(step == 2 * y_lo)
+    for two_z in range(2):
+
+        @pl.when(step == two_z)
         def _():
             for x in range(4):
-                first[x, y_lo * BLOCK : (y_lo + 1) * BLOCK] = quarters[x]
-
-    for y_hi in range(2):
-        m = ((step // 2) ^ place[0]) + 2 * (y_hi ^ place[1])
-        for k, part in enumerate((m0, m1, m2, m3)):
-
-            @pl.when((step % 2 == 1) & (m == k))
-            def _():
-                for x in range(4):
-                    for z in range(4):
-                        at = x * 192 + z * 48
-                        rows = quarters[x][z * 96 + y_hi * 48 : z * 96 + y_hi * 48 + 48]
-                        part[at : at + 48] = rows
+                first[x, two_z * BLOCK : (two_z + 1) * BLOCK] = quarters[x]
+
+        for p in range(2):
+            for y_hi in range(2):
+                m = p + 2 * (y_hi ^ place[0])
+                for k, part in enumerate((m0, m1, m2, m3)):
+                    if k % 2 != p:
+                        continue
+
+                    @pl.when((step == 2 + two_z) & (m == k))
+                    def _():
+                        for x in range(4):
+                            for z in range(2):
+                                at = x * 192 + (two_z * 2 + z) * 48
+                                source = z * 192 + p * 96 + y_hi * 48
+                                part[at : at + 48] = quarters[x][source : source + 48]
 
     row[...] += jnp.sum(moment * w2[...].astype(jnp.float32), axis=0, keepdims=True)
     d_b1[...] = jnp.broadcast_to(
@@ -179,7 +188,7 @@
 def mlp(normed, scaled, weights, b1):
     pixels, chans = normed.shape
     hid = weights.shape[0]
-    place = jnp.stack([lax.axis_index("y_lo"), lax.axis_index("y_hi")]).astype(jnp.int32)
+    place = lax.axis_index("y_hi").astype(jnp.int32).reshape(1)
     whole = pl.BlockSpec((pixels, chans), lambda i: (0, 0))
     half = pl.BlockSpec((pixels // 2, chans), lambda i: (0, 0))
     part = pl.BlockSpec((hid // 2, chans // 2), lambda i: (0, 0))
@@ -355,7 +364,8 @@
     cot_sums = jnp.sum(flat_cot, axis=0)
     core = lax.axis_index("core")
     y_lo = lax.axis_index("y_lo")
-    sums_b1 = sums_b1[:, 0][None]
+    sums_b1 = jnp.roll(sums_b1[:, 0].reshape(8, 2, shard), y_lo, 1)
+    sums_b1 = sums_b1.transpose(1, 0, 2).reshape(1, -1)
     pair_b1 = jnp.where(core == jnp.arange(2)[:, None], sums_b1, 0.0)
     local_small = jnp.concatenate(
         [

time: 247 us -> 244 us (0.988)
  starting transfers between devices: 71 us -> 64.6 us
  local copies, waits for them, and re-layouts: 12.5 us -> 18.4 us
    ppermute x9 -> x13, waiting for transfers between devices: 6.11 us -> 24.7 us  [across(): return lax.ppermute(cells, Y, [(i, i ^ flip) for i in range(4)])]
    ppermute x2, waiting for transfers between devices: 8.07 us -> 0.01 us  [halo(): above = lax.ppermute(cells[:, -MARGIN:], ROWS, down)]
    all_to_all x2, waiting for transfers between devices: 15.2 us -> 8.89 us  [gather(): lax.all_to_all(jnp.broadcast_to(part[None], (count,) + part.shape), axes,...]
    all_to_all x1, starting transfers between devices: 11.1 us -> 5.01 us  [scatter_terms(): lax.all_to_all(first, 'x', 0, 0).astype(jnp.float32)]
    all_gather x1, waiting for transfers between devices: 22.8 us -> 17.2 us  [gather_weights(): whole = lax.all_gather(pair, 'z', axis=0, tiled=True)]
    ppermute x3, starting transfers between devices: 12.4 us -> 8.15 us  [spread_small(): lax.ppermute(sent, 'x', [(i, (i + k) % 4) for i in range(4)])]
    ppermute x9 -> x13, starting transfers between devices: 12.5 us -> 16.7 us  [across(): return lax.ppermute(cells, Y, [(i, i ^ flip) for i in range(4)])]
    slice x3, local copies, waits for them, and re-layouts: 0.42 us -> 4.14 us  [depthwise(): kernel[row_tap * KERNEL + col_tap]]
  transfers between devices with their start and end apart: 26 -> 30, of which waited for: 11 -> 11; matrix products, arithmetic and copies ran while one was open for 19% -> 21% of each run, Pallas kernels for 9% -> 9%
where the time goes in v5:
time: 244 us; the launch traced here: 242 us
  starting transfers between devices  64.6 us (26%)
  waiting for transfers between devices  55.9 us (23%)
  Pallas kernels  46.6 us (19%)
  other arithmetic  41.7 us (17%)
  local copies, waits for them, and re-layouts  18.4 us (8%)
  between operations  14.8 us (6%)
    pallas_call x1, Pallas kernels, mlp(): pl.pallas_call(mlp_kernel, grid=(hid // BLOCK,), in_specs=[pl.BlockSpec(m...  25.6 us
    ppermute x13, waiting for transfers between devices, across(): return lax.ppermute(cells, Y, [(i, i ^ flip) for i in range(4)])  24.7 us
    all_gather x1, waiting for transfers between devices, gather_weights(): whole = lax.all_gather(pair, 'z', axis=0, tiled=True)  17.2 us
    ppermute x13, starting transfers between devices, across(): return lax.ppermute(cells, Y, [(i, i ^ flip) for i in range(4)])  16.7 us
    all_to_all x2, starting transfers between devices, gather(): lax.all_to_all(jnp.broadcast_to(part[None], (count,) + part.shape), axes,...  14.5 us
    reduce_sum x1, other arithmetic, shards(): center = conv - jnp.mean(conv, axis=-1, keepdims=True)  13.4 us
    pallas_call x1, Pallas kernels, tap_sums(): pl.pallas_call(taps_kernel, grid=(chans // LANES, images), in_specs=[pl.B...  10.6 us
    pallas_call x1, Pallas kernels, transposed(): pl.pallas_call(transposed_kernel, grid=(chans // LANES, images), in_specs...  10.4 us
  transfers between devices with their start and end apart: 30, of which 11 were waited for; matrix products, arithmetic and copies ran while one was open for 21% of the time, Pallas kernels for 9%

profile of v5, /device:TPU:2, one launch (start us, length us, event | category | flops | bytes accessed | tf_op | source)
XLA Modules:
  0.0 241.9 jit_solution(9741661664860028679)
XLA Ops:
  10.0 7.2 %collective-permute-done.4 = bf16[96,1536]{1,0:T(8,128)(2,1)S(1)} collective-permute-done((bf16[96,1536]{1,0:T(8,128)(2,1)S(1)}, bf16[96,1536]{1,0:T(8,128)(2,1)S(1)}, u32[]{:S(2)}, u32[]{:S(2)}) %collective-permute-start.4) | collective-permute-done | bytes 294944 | tf_op jit(solution)/shard_map/ppermute | solution.py:51
  21.4 3.6 %collective-permute-start = (bf16[2,3,48,768]{3,2,1,0:T(8,128)(2,1)S(1)}, bf16[2,3,48,768]{3,2,1,0:T(8,128)(2,1)S(1)}, u32[]{:S(2)}, u32[]{:S(2)}) collective-permute-start(bf16[2,3,48,768]{3,2,1,0:T(8,128)(2,1)S(1)} %get-tuple-element.106), channel_id=1, source_target_pairs={{0,1},{1,2},{2,3},{3,4},{4,5},{5,6},{6,7},{8,9},{9,10},{10,11},{11... | collective-permute-start | bytes 1327112 | tf_op jit(solution)/shard_map/ppermute | solution.py:28
  26.7 9.6 %all-to-all-start = ((f32[16,1,96]{2,1,0:T(1,128)}), f32[16,1,96]{2,1,0:T(1,128)}, u32[]{:S(2)}, u32[]{:S(2)}) async-start(f32[16,1,96]{2,1,0:T(1,128)} %broadcast_in_dim.84), calls=%async_computation | async-start | bytes 16384 | tf_op jit(solution)/shard_map/all_to_all | solution.py:46
  41.7 13.4 %fusion.16 = (f32[2,6,48]{2,1,0:T(8,128)S(1)}, f32[2,6,48,768]{3,2,1,0:T(8,128)S(1)}) fusion(f32[768]{0:T(1024)S(1)} %copy-done.16, f32[768]{0:T(1024)S(1)} %get-tuple-element.93, bf16[2,12,56,768]{3,2,1,0:T(8,128)(2,1)S(1)} %fusion.5.padded, f32[768]{0:T(1024)S(1)} %get-tuple-element.46, f32[768]{0:T(1024)S(1)} %get-tuple-element.47, ...), kind=kLoop, calls=%fused_computation.133 | loop fusion | flops 65469888 | bytes 45277440 | tf_op jit(solution)/shard_map/reduce_sum | solution.py:341
  59.5 2.8 %pad_maximum_fusion.1.scaled = bf16[1152,768]{1,0:T(8,128)(2,1)} fusion(bf16[576,768]{1,0:T(8,128)(2,1)} %collective-permute-done.3, bf16[576,768]{1,0:T(8,128)(2,1)} %fusion.6), kind=kLoop, calls=%fused_computation.11 | loop fusion | flops 3538944 | bytes 3538944 | tf_op jit(solution)/shard_map/concatenate | solution.py:339
  62.3 2.5 %pad_maximum_fusion.normed = bf16[1152,768]{1,0:T(8,128)(2,1)} fusion(bf16[576,768]{1,0:T(8,128)(2,1)S(1)} %collective-permute-done.2, bf16[576,768]{1,0:T(8,128)(2,1)} %get-tuple-element.96), kind=kLoop, calls=%fused_computation.10 | loop fusion | flops 3538944 | bytes 3538944 | tf_op jit(solution)/shard_map/concatenate | solution.py:346
  64.8 17.2 %all-gather.2.cloned.1.call-done.w1.w2 = bf16[1536,1536]{1,0:T(8,128)(2,1)} async-done(((bf16[192,1536]{1,0:T(8,128)(2,1)}), bf16[1536,1536]{1,0:T(8,128)(2,1)}) %all-gather.2.cloned.1.call-update) | async-done | bytes 4718608 | tf_op jit(solution)/shard_map/all_gather | solution.py:57
  83.2 25.6 %shard_map.146 = (bf16[4,768,384]{2,1,0:T(8,128)(2,1)}, bf16[768,384]{1,0:T(8,128)(2,1)}, bf16[768,384]{1,0:T(8,128)(2,1)}, bf16[768,384]{1,0:T(8,128)(2,1)}, bf...) custom-call(s32[1]{0:T(128)} %bitcast.place, ...), custom_call_target="tpu_custom_call" | custom-call | flops 13589544960 | bytes 16777216 | tf_op jit(solution)/shard_map/pallas_call | solution.py:196
  109.0 5.0 %all-to-all-start.1 = ((bf16[4,768,384]{2,1,0:T(8,128)(2,1)}), bf16[4,768,384]{2,1,0:T(8,128)(2,1)}, u32[]{:S(2)}, u32[]{:S(2)}) async-start(bf16[4,768,384]{2,1,0:T(8,128)(2,1)} %get-tuple-element.25), calls=%async_computation.1 | async-start | bytes 4718592 | tf_op jit(solution)/shard_map/all_to_all | solution.py:70
  114.0 2.8 %collective-permute-start.9 = (bf16[768,384]{1,0:T(8,128)(2,1)}, bf16[768,384]{1,0:T(8,128)(2,1)}, u32[]{:S(2)}, u32[]{:S(2)}) collective-permute-start(bf16[768,384]{1,0:T(8,128)(2,1)} %get-tuple-element.28), channel_id=1, source_target_pairs={{0,132},{4,128},{128,4},{132,0},{1,133},{5,129},{129,5},{133,1},{2... | collective-permute-start | bytes 1769480 | tf_op jit(solution)/shard_map/ppermute | solution.py:51
  128.3 9.0 %collective-permute-done.12 = bf16[384,384]{1,0:T(8,128)(2,1)} collective-permute-done((bf16[384,384]{1,0:T(8,128)(2,1)}, bf16[384,384]{1,0:T(8,128)(2,1)}, u32[]{:S(2)}, u32[]{:S(2)}) %collective-permute-start.12) | collective-permute-done | bytes 294944 | tf_op jit(solution)/shard_map/ppermute | solution.py:51
  146.2 3.9 %collective-permute-start.6 = (bf16[2,3,48,768]{3,2,1,0:T(8,128)(2,1)S(1)}, bf16[2,3,48,768]{3,2,1,0:T(8,128)(2,1)S(1)}, u32[]{:S(2)}, u32[]{:S(2)}) collective-permute-start(bf16[2,3,48,768]{3,2,1,0:T(8,128)(2,1)S(1)} %get-tuple-element.102), channel_id=1, source_target_pairs={{0,1},{1,2},{2,3},{3,4},{4,5},{5,6},{6,7},{8,9},{9,10},{10,11},{11... | collective-permute-start | bytes 1327112 | tf_op jit(solution)/shard_map/ppermute | solution.py:28
  150.1 10.6 %shard_map.147 = f32[49,768]{1,0:T(8,128)} custom-call(bf16[2,12,56,768]{3,2,1,0:T(8,128)(2,1)} %copy-done, bf16[2,6,48,768]{3,2,1,0:T(8,128)(2,1)} %bitcast.40), custom_call_target="tpu_custom_call" | custom-call | flops 10000000000 | bytes 4194304 | tf_op jit(solution)/shard_map/pallas_call | solution.py:298
  162.0 2.5 %add_convert_fusion.1 = bf16[768,384]{1,0:T(8,128)(2,1)} fusion(bf16[768,384]{1,0:T(8,128)(2,1)} %collective-permute-done.9, bf16[768,384]{1,0:T(8,128)(2,1)} %collective-permute-done.8, bf16[768,384]{1,0:T(8,128)(2,1)S(1)} %copy-done.8, bf16[384,384]{1,0:T(8,128)(2,1)} %copy-done.9, bf16[384,384]{1,0:T(8,128)(2,1)} %collective-permute-done.11), kind=kLoop, calls=%fused_computation.25 | loop fusion | flops 3244032 | bytes 2949120 | tf_op jit(solution)/shard_map/convert_element_type | solution.py:73
  176.5 2.7 %collective-permute-start.23 = (f32[8,768]{1,0:T(8,128)S(1)}, f32[8,768]{1,0:T(8,128)S(1)}, u32[]{:S(2)}, u32[]{:S(2)}) collective-permute-start(f32[8,768]{1,0:T(8,128)S(1)} %get-tuple-element.121), channel_id=1, source_target_pairs={{0,3},{1,0},{2,1},{3,2},{4,7},{5,4},{6,5},{7,6},{8,11},{9,8},{10,9... | collective-permute-start | bytes 73736 | tf_op jit(solution)/shard_map/ppermute | solution.py:101
  179.1 3.0 %collective-permute-start.22 = (f32[8,768]{1,0:T(8,128)S(1)}, f32[8,768]{1,0:T(8,128)S(1)}, u32[]{:S(2)}, u32[]{:S(2)}) collective-permute-start(f32[8,768]{1,0:T(8,128)S(1)} %get-tuple-element.122), channel_id=1, source_target_pairs={{0,2},{1,3},{2,0},{3,1},{4,6},{5,7},{6,4},{7,5},{8,10},{9,11},{10,... | collective-permute-start | bytes 73736 | tf_op jit(solution)/shard_map/ppermute | solution.py:101
  182.1 2.5 %collective-permute-start.21 = (f32[8,768]{1,0:T(8,128)S(1)}, f32[8,768]{1,0:T(8,128)S(1)}, u32[]{:S(2)}, u32[]{:S(2)}) collective-permute-start(f32[8,768]{1,0:T(8,128)S(1)} %get-tuple-element.120), channel_id=1, source_target_pairs={{0,1},{1,2},{2,3},{3,0},{4,5},{5,6},{6,7},{7,4},{8,9},{9,10},{10,1... | collective-permute-start | bytes 73736 | tf_op jit(solution)/shard_map/ppermute | solution.py:101
  188.3 3.5 %all-to-all-start.2 = ((bf16[4,192,384]{2,1,0:T(8,128)(2,1)}), bf16[4,192,384]{2,1,0:T(8,128)(2,1)S(1)}, u32[]{:S(2)}, u32[]{:S(2)}) async-start(bf16[4,192,384]{2,1,0:T(8,128)(2,1)} %bitcast.13), calls=%async_computation.2 | async-start | bytes 1179648 | tf_op jit(solution)/shard_map/all_to_all | solution.py:40
  193.5 3.5 %collective-permute-done.15 = bf16[192,384]{1,0:T(8,128)(2,1)S(1)} collective-permute-done((bf16[192,384]{1,0:T(8,128)(2,1)S(1)}, bf16[192,384]{1,0:T(8,128)(2,1)S(1)}, u32[]{:S(2)}, u32[]{:S(2)}) %collective-permute-start.15) | collective-permute-done | bytes 147488 | tf_op jit(solution)/shard_map/ppermute | solution.py:51
  199.8 4.3 %all-to-all-start.3 = ((bf16[8,80,384]{2,1,0:T(8,128)(2,1)}), bf16[8,80,384]{2,1,0:T(8,128)(2,1)S(1)}, u32[]{:S(2)}, u32[]{:S(2)}) async-start(bf16[8,80,384]{2,1,0:T(8,128)(2,1)} %pad_maximum_fusion.3), calls=%async_computation.3 | async-start | bytes 983040 | tf_op jit(solution)/shard_map/all_to_all | solution.py:112
  204.1 10.4 %shard_map.148 = bf16[2,6,48,768]{3,2,1,0:T(8,128)(2,1)} custom-call(bf16[2,12,56,768]{3,2,1,0:T(8,128)(2,1)} %select_maximum_fusion.padded, bf16[2,6,48,768]{3,2,1,0:T(8,128)(2,1)} %cotangent.1, f32[49,768]{1,0:T(8,128)} %kernel.1), custom_call_target="tpu_custom_call" | custom-call | flops 10000000000 | bytes 4194304 | tf_op jit(solution)/shard_map/pallas_call | solution.py:254
  214.5 3.4 %all-to-all-done.3 = bf16[8,80,384]{2,1,0:T(8,128)(2,1)S(1)} async-done(((bf16[8,80,384]{2,1,0:T(8,128)(2,1)}), bf16[8,80,384]{2,1,0:T(8,128)(2,1)S(1)}, u32[]{:S(2)}, u32[]{:S(2)}) %all-to-all-start.3) | async-done | bytes 491552 | tf_op jit(solution)/shard_map/all_to_all | solution.py:112
  218.7 4.8 %all-to-all-start.4 = ((bf16[8,80,384]{2,1,0:T(8,128)(2,1)}), bf16[8,80,384]{2,1,0:T(8,128)(2,1)S(1)}, u32[]{:S(2)}, u32[]{:S(2)}) async-start(bf16[8,80,384]{2,1,0:T(8,128)(2,1)} %broadcast_in_dim.102), calls=%async_computation.4 | async-start | bytes 983040 | tf_op jit(solution)/shard_map/all_to_all | solution.py:46
  223.6 8.9 %all-to-all-done.4 = bf16[8,80,384]{2,1,0:T(8,128)(2,1)S(1)} async-done(((bf16[8,80,384]{2,1,0:T(8,128)(2,1)}), bf16[8,80,384]{2,1,0:T(8,128)(2,1)S(1)}, u32[]{:S(2)}, u32[]{:S(2)}) %all-to-all-start.4) | async-done | bytes 491552 | tf_op jit(solution)/shard_map/all_to_all | solution.py:46
  (163 shorter events, 64.6 us)
Async XLA Ops:
  7.2 74.9 %all-gather.2.cloned.1.call-start = ((), (), s32[]{:S(2)}) async-start(), calls=%async_computation.5 | async-start | bytes 5308416 | tf_op jit(solution)/shard_map/all_gather | solution.py:57
  8.3 8.8 %collective-permute-start.4 = (bf16[96,1536]{1,0:T(8,128)(2,1)S(1)}, bf16[96,1536]{1,0:T(8,128)(2,1)S(1)}, u32[]{:S(2)}, u32[]{:S(2)}) collective-permute-start(bf16[96,1536]{1,0:T(8,128)(2,1)S(1)} %pad_maximum_fusion.4), channel_id=1, source_target_pairs={{0,128},{4,132},{128,0},{132,4},{1,129},{5,133},{129,1},{133,5},{2... | collective-permute-start | bytes 884744 | tf_op jit(solution)/shard_map/ppermute | solution.py:51
  19.1 21.6 %collective-permute-start.1 = (bf16[2,3,48,768]{3,2,1,0:T(8,128)(2,1)S(1)}, bf16[2,3,48,768]{3,2,1,0:T(8,128)(2,1)S(1)}, u32[]{:S(2)}, u32[]{:S(2)}) collective-permute-start(bf16[2,3,48,768]{3,2,1,0:T(8,128)(2,1)S(1)} %get-tuple-element.107), channel_id=1, source_target_pairs={{1,0},{2,1},{3,2},{4,3},{5,4},{6,5},{7,6},{9,8},{10,9},{11,10},{12... | collective-permute-start | bytes 1327112 | tf_op jit(solution)/shard_map/ppermute | solution.py:29
  21.4 19.1 %collective-permute-start = (bf16[2,3,48,768]{3,2,1,0:T(8,128)(2,1)S(1)}, bf16[2,3,48,768]{3,2,1,0:T(8,128)(2,1)S(1)}, u32[]{:S(2)}, u32[]{:S(2)}) collective-permute-start(bf16[2,3,48,768]{3,2,1,0:T(8,128)(2,1)S(1)} %get-tuple-element.106), channel_id=1, source_target_pairs={{0,1},{1,2},{2,3},{3,4},{4,5},{5,6},{6,7},{8,9},{9,10},{10,11},{11... | collective-permute-start | bytes 1327112 | tf_op jit(solution)/shard_map/ppermute | solution.py:28
  26.1 33.4 %collective-permute-start.3 = (bf16[576,768]{1,0:T(8,128)(2,1)}, bf16[576,768]{1,0:T(8,128)(2,1)}, u32[]{:S(2)}, u32[]{:S(2)}) collective-permute-start(bf16[576,768]{1,0:T(8,128)(2,1)} %fusion.6), channel_id=1, source_target_pairs={{0,8},{8,0},{1,9},{9,1},{2,10},{10,2},{3,11},{11,3},{4,12},{12,4},... | collective-permute-start | bytes 2654216 | tf_op jit(solution)/shard_map/ppermute | solution.py:34
  26.7 32.0 %all-to-all-start = ((f32[16,1,96]{2,1,0:T(1,128)}), f32[16,1,96]{2,1,0:T(1,128)}, u32[]{:S(2)}, u32[]{:S(2)}) async-start(f32[16,1,96]{2,1,0:T(1,128)} %broadcast_in_dim.84), calls=%async_computation | async-start | bytes 16384 | tf_op jit(solution)/shard_map/all_to_all | solution.py:46
  108.9 31.2 %collective-permute-start.5 = (bf16[576,768]{1,0:T(8,128)(2,1)}, bf16[576,768]{1,0:T(8,128)(2,1)}, u32[]{:S(2)}, u32[]{:S(2)}) collective-permute-start(bf16[576,768]{1,0:T(8,128)(2,1)} %get-tuple-element.24), channel_id=1, source_target_pairs={{0,8},{8,0},{1,9},{9,1},{2,10},{10,2},{3,11},{11,3},{4,12},{12,4},... | collective-permute-start | bytes 2654216 | tf_op jit(solution)/shard_map/ppermute | solution.py:34
  109.0 55.6 %all-to-all-start.1 = ((bf16[4,768,384]{2,1,0:T(8,128)(2,1)}), bf16[4,768,384]{2,1,0:T(8,128)(2,1)}, u32[]{:S(2)}, u32[]{:S(2)}) async-start(bf16[4,768,384]{2,1,0:T(8,128)(2,1)} %get-tuple-element.25), calls=%async_computation.1 | async-start | bytes 4718592 | tf_op jit(solution)/shard_map/all_to_all | solution.py:70
  114.0 48.0 %collective-permute-start.9 = (bf16[768,384]{1,0:T(8,128)(2,1)}, bf16[768,384]{1,0:T(8,128)(2,1)}, u32[]{:S(2)}, u32[]{:S(2)}) collective-permute-start(bf16[768,384]{1,0:T(8,128)(2,1)} %get-tuple-element.28), channel_id=1, source_target_pairs={{0,132},{4,128},{128,4},{132,0},{1,133},{5,129},{129,5},{133,1},{2... | collective-permute-start | bytes 1769480 | tf_op jit(solution)/shard_map/ppermute | solution.py:51
  116.7 45.3 %collective-permute-start.8 = (bf16[768,384]{1,0:T(8,128)(2,1)}, bf16[768,384]{1,0:T(8,128)(2,1)}, u32[]{:S(2)}, u32[]{:S(2)}) collective-permute-start(bf16[768,384]{1,0:T(8,128)(2,1)} %get-tuple-element.27), channel_id=1, source_target_pairs={{0,128},{4,132},{128,0},{132,4},{1,129},{5,133},{129,1},{133,5},{2... | collective-permute-start | bytes 1769480 | tf_op jit(solution)/shard_map/ppermute | solution.py:51
  118.9 18.4 %collective-permute-start.12 = (bf16[384,384]{1,0:T(8,128)(2,1)}, bf16[384,384]{1,0:T(8,128)(2,1)}, u32[]{:S(2)}, u32[]{:S(2)}) collective-permute-start(bf16[384,384]{1,0:T(8,128)(2,1)} %get-tuple-element.115), channel_id=1, source_target_pairs={{0,132},{4,128},{128,4},{132,0},{1,133},{5,129},{129,5},{133,1},{2... | collective-permute-start | bytes 884744 | tf_op jit(solution)/shard_map/ppermute | solution.py:51
  120.0 18.5 %collective-permute-start.10 = (bf16[384,384]{1,0:T(8,128)(2,1)}, bf16[384,384]{1,0:T(8,128)(2,1)}, u32[]{:S(2)}, u32[]{:S(2)}) collective-permute-start(bf16[384,384]{1,0:T(8,128)(2,1)} %get-tuple-element.114), channel_id=1, source_target_pairs={{0,128},{4,132},{128,0},{132,4},{1,129},{5,133},{129,1},{133,5},{2... | collective-permute-start | bytes 884744 | tf_op jit(solution)/shard_map/ppermute | solution.py:51
  137.3 8.9 %collective-permute-start.13 = (bf16[384,384]{1,0:T(8,128)(2,1)}, bf16[384,384]{1,0:T(8,128)(2,1)S(1)}, u32[]{:S(2)}, u32[]{:S(2)}) collective-permute-start(bf16[384,384]{1,0:T(8,128)(2,1)} %collective-permute-done.12), channel_id=1, source_target_pairs={{0,128},{4,132},{128,0},{132,4},{1,129},{5,133},{129,1},{133,5},{2... | collective-permute-start | bytes 884744 | tf_op jit(solution)/shard_map/ppermute | solution.py:51
  138.5 23.3 %collective-permute-start.11 = (bf16[384,384]{1,0:T(8,128)(2,1)}, bf16[384,384]{1,0:T(8,128)(2,1)}, u32[]{:S(2)}, u32[]{:S(2)}) collective-permute-start(bf16[384,384]{1,0:T(8,128)(2,1)} %collective-permute-done.10), channel_id=1, source_target_pairs={{0,132},{4,128},{128,4},{132,0},{1,133},{5,129},{129,5},{133,1},{2... | collective-permute-start | bytes 884744 | tf_op jit(solution)/shard_map/ppermute | solution.py:51
  143.8 27.4 %collective-permute-start.7 = (bf16[2,3,48,768]{3,2,1,0:T(8,128)(2,1)S(1)}, bf16[2,3,48,768]{3,2,1,0:T(8,128)(2,1)S(1)}, u32[]{:S(2)}, u32[]{:S(2)}) collective-permute-start(bf16[2,3,48,768]{3,2,1,0:T(8,128)(2,1)S(1)} %get-tuple-element.103), channel_id=1, source_target_pairs={{1,0},{2,1},{3,2},{4,3},{5,4},{6,5},{7,6},{9,8},{10,9},{11,10},{12... | collective-permute-start | bytes 1327112 | tf_op jit(solution)/shard_map/ppermute | solution.py:29
  146.2 25.0 %collective-permute-start.6 = (bf16[2,3,48,768]{3,2,1,0:T(8,128)(2,1)S(1)}, bf16[2,3,48,768]{3,2,1,0:T(8,128)(2,1)S(1)}, u32[]{:S(2)}, u32[]{:S(2)}) collective-permute-start(bf16[2,3,48,768]{3,2,1,0:T(8,128)(2,1)S(1)} %get-tuple-element.102), channel_id=1, source_target_pairs={{0,1},{1,2},{2,3},{3,4},{4,5},{5,6},{6,7},{8,9},{9,10},{10,11},{11... | collective-permute-start | bytes 1327112 | tf_op jit(solution)/shard_map/ppermute | solution.py:28
  176.5 15.3 %collective-permute-start.23 = (f32[8,768]{1,0:T(8,128)S(1)}, f32[8,768]{1,0:T(8,128)S(1)}, u32[]{:S(2)}, u32[]{:S(2)}) collective-permute-start(f32[8,768]{1,0:T(8,128)S(1)} %get-tuple-element.121), channel_id=1, source_target_pairs={{0,3},{1,0},{2,1},{3,2},{4,7},{5,4},{6,5},{7,6},{8,11},{9,8},{10,9... | collective-permute-start | bytes 73736 | tf_op jit(solution)/shard_map/ppermute | solution.py:101
  179.1 13.3 %collective-permute-start.22 = (f32[8,768]{1,0:T(8,128)S(1)}, f32[8,768]{1,0:T(8,128)S(1)}, u32[]{:S(2)}, u32[]{:S(2)}) collective-permute-start(f32[8,768]{1,0:T(8,128)S(1)} %get-tuple-element.122), channel_id=1, source_target_pairs={{0,2},{1,3},{2,0},{3,1},{4,6},{5,7},{6,4},{7,5},{8,10},{9,11},{10,... | collective-permute-start | bytes 73736 | tf_op jit(solution)/shard_map/ppermute | solution.py:101
  182.1 10.4 %collective-permute-start.21 = (f32[8,768]{1,0:T(8,128)S(1)}, f32[8,768]{1,0:T(8,128)S(1)}, u32[]{:S(2)}, u32[]{:S(2)}) collective-permute-start(f32[8,768]{1,0:T(8,128)S(1)} %get-tuple-element.120), channel_id=1, source_target_pairs={{0,1},{1,2},{2,3},{3,0},{4,5},{5,6},{6,7},{7,4},{8,9},{9,10},{10,1... | collective-permute-start | bytes 73736 | tf_op jit(solution)/shard_map/ppermute | solution.py:101
  184.7 8.7 %collective-permute-start.17 = (bf16[192,384]{1,0:T(8,128)(2,1)S(1)}, bf16[192,384]{1,0:T(8,128)(2,1)S(1)}, u32[]{:S(2)}, u32[]{:S(2)}) collective-permute-start(bf16[192,384]{1,0:T(8,128)(2,1)S(1)} %bitcast.53), channel_id=1, source_target_pairs={{0,132},{4,128},{128,4},{132,0},{1,133},{5,129},{129,5},{133,1},{2... | collective-permute-start | bytes 442376 | tf_op jit(solution)/shard_map/ppermute | solution.py:51
  186.1 7.4 %collective-permute-start.16 = (bf16[192,384]{1,0:T(8,128)(2,1)S(1)}, bf16[192,384]{1,0:T(8,128)(2,1)S(1)}, u32[]{:S(2)}, u32[]{:S(2)}) collective-permute-start(bf16[192,384]{1,0:T(8,128)(2,1)S(1)} %bitcast.52), channel_id=1, source_target_pairs={{0,4},{4,0},{128,132},{132,128},{1,5},{5,1},{129,133},{133,129},{2... | collective-permute-start | bytes 442376 | tf_op jit(solution)/shard_map/ppermute | solution.py:51
  188.3 10.5 %all-to-all-start.2 = ((bf16[4,192,384]{2,1,0:T(8,128)(2,1)}), bf16[4,192,384]{2,1,0:T(8,128)(2,1)S(1)}, u32[]{:S(2)}, u32[]{:S(2)}) async-start(bf16[4,192,384]{2,1,0:T(8,128)(2,1)} %bitcast.13), calls=%async_computation.2 | async-start | bytes 1179648 | tf_op jit(solution)/shard_map/all_to_all | solution.py:40
  199.8 18.0 %all-to-all-start.3 = ((bf16[8,80,384]{2,1,0:T(8,128)(2,1)}), bf16[8,80,384]{2,1,0:T(8,128)(2,1)S(1)}, u32[]{:S(2)}, u32[]{:S(2)}) async-start(bf16[8,80,384]{2,1,0:T(8,128)(2,1)} %pad_maximum_fusion.3), calls=%async_computation.3 | async-start | bytes 983040 | tf_op jit(solution)/shard_map/all_to_all | solution.py:112
  218.7 13.7 %all-to-all-start.4 = ((bf16[8,80,384]{2,1,0:T(8,128)(2,1)}), bf16[8,80,384]{2,1,0:T(8,128)(2,1)S(1)}, u32[]{:S(2)}, u32[]{:S(2)}) async-start(bf16[8,80,384]{2,1,0:T(8,128)(2,1)} %broadcast_in_dim.102), calls=%async_computation.4 | async-start | bytes 983040 | tf_op jit(solution)/shard_map/all_to_all | solution.py:46
  (27 other events, 218.4 us)
Sparse Core Ops, SparseCore 0:
  19.2 62.8 all-gather.1
